TPU v7x, 512 devices: a whole 4x8x8 slice. The times are simulated.
512 devices in a mesh: pipe: 64 (over y, x, z_lo), head: 8 (over z_hi, core).
Axes of the slice: x: 4, y: 8, z: 8 (z_hi: 4, z_lo: 2; z = z_hi * 2 + z_lo), core: 2. Of those that a mesh axis runs over, the one named last changes fastest.
Arguments:
- stream: bfloat16 [64, 2048, 128], P('pipe', 'head'), may hold values from -6 to 6
- fresh: bfloat16 [2, 2048, 128], P(None, 'head'), may hold values from -6 to 6
- gain: float32 [64, 2048], P('pipe'), may hold values from 0.25 to 1.75
- final_gain: float32 [2048], replicated, may hold values from 0.25 to 1.75
- w_query: bfloat16 [64, 2048, 2048], P('pipe', None, 'head'), may hold values from -0.125 to 0.125
- w_kv: bfloat16 [64, 2, 2048, 2048], P('pipe', None, None, 'head'), may hold values from -0.125 to 0.125
- w_out: bfloat16 [64, 2048, 2048], P('pipe', 'head'), may hold values from -0.125 to 0.125
- cache_kv: bfloat16 [64, 2, 128, 4096], P('pipe', None, None, 'head'), may hold values from -6 to 6
- cache_grad: bfloat16 [64, 128, 4096], P('pipe', None, 'head'), may hold values from -6 to 6
Outputs:
- stream_out: bfloat16 [64, 2048, 128], P('pipe', 'head')
- new_kv: bfloat16 [64, 2, 128, 4096], P('pipe', None, None, 'head')
- memory_grad: float32 [2048, 128], P(('pipe', 'head'))
All inputs are finite; a program needn't handle non-finite values.
Results may differ from a plain program's by a relative error of at most 0.017.
Values may be sent and summed in bfloat16 or wider, within the bound.
No kernel may reach another device: no remote copies, remote signals or barrier semaphores. Data moves between devices by JAX's collectives and lax.ppermute only.
A program may use at most 64 MiB of HBM per device.

v0:
```python
import jax
import jax.numpy as jnp
from jax import lax
from jax.sharding import PartitionSpec as P

TICKS = 2


EPS = 1e-06


def broadcast(block, axis, source):
    block = jnp.where(lax.axis_index(axis) == source, block, jnp.zeros_like(block))
    return lax.psum(block, axis)


def shifted(value, axis, by):
    size = lax.axis_size(axis)
    pairs = [(i, i + by) for i in range(size) if 0 <= i + by < size]
    return lax.ppermute(value, axis, pairs)


def norm_columns(values, scale_row):
    wide = values.astype(jnp.float32)
    factor = lax.rsqrt(jnp.mean(wide * wide, axis=0, keepdims=True) + EPS)
    return (wide * factor * scale_row[:, None]).astype(jnp.bfloat16)


def attend(query, keys, values):
    scores = lax.dot_general(
        query, keys, (((1,), (1,)), ((), ())), preferred_element_type=jnp.float32
    )
    scores = scores * query.shape[1] ** (-0.5)
    probs = jax.nn.softmax(scores, axis=-1).astype(jnp.bfloat16)
    return jnp.dot(probs, values, preferred_element_type=jnp.float32).astype(jnp.bfloat16)


def body(stream, fresh, gain, final_gain, w_query, w_kv, w_out, cache_kv, cache_grad):
    pipe_count = lax.axis_size("pipe")
    half = pipe_count // 2
    section = lax.axis_index("pipe")
    is_enc = section < half
    is_dec = jnp.logical_not(is_enc)
    current = stream[0]
    scale_row = gain[0]
    wq = w_query[0]
    wkv = w_kv[0]
    wo = w_out[0]
    width = wq.shape[1]
    tokens = current.shape[1]

    def pair_cols(normed):
        both = jnp.einsum("ds,cdh->sch", normed, wkv, preferred_element_type=jnp.float32)
        return both.reshape(normed.shape[1], 2 * width).astype(jnp.bfloat16)

    def empty_pair():
        return jnp.zeros((tokens, 2 * width), jnp.bfloat16)

    produced = []
    latest_kv = None
    for tick in range(TICKS):
        whole = lax.all_gather(current, "head", axis=0, tiled=True)
        normed = norm_columns(whole, scale_row)
        query = lax.dot_general(
            normed, wq, (((0,), (0,)), ((), ())), preferred_element_type=jnp.float32
        ).astype(jnp.bfloat16)
        own_pair = lax.cond(is_enc, lambda: pair_cols(normed), empty_pair)
        cross = cache_kv[0, tick]
        if tick > 0:
            cross = jnp.where(section == half, latest_kv, cross)
        paired = jnp.where(is_enc, own_pair, cross)
        attn = attend(query, paired[:, :width], paired[:, width:])
        summed = lax.psum_scatter(
            lax.dot_general(
                wo, attn, (((0,), (1,)), ((), ())), preferred_element_type=jnp.float32
            ).astype(jnp.bfloat16),
            "head",
            scatter_dimension=0,
            tiled=True,
        ).astype(jnp.float32)
        output = (current.astype(jnp.float32) + summed).astype(jnp.bfloat16)
        output_full = lax.all_gather(output, "head", axis=0, tiled=True)
        output_full = broadcast(output_full, "pipe", half - 1)
        memory = norm_columns(output_full, final_gain)
        latest_kv = lax.cond(is_dec, lambda: pair_cols(memory), empty_pair)
        produced.append(latest_kv)
        passed = shifted(output, "pipe", 1)
        if tick + 1 < TICKS:
            passed = jnp.where(section == 0, fresh[0], passed)
            passed = jnp.where(section == half, fresh[1], passed)
        else:
            passed = jnp.where(section == half, jnp.zeros_like(passed), passed)
        current = passed
    grads = cache_grad[0]
    out_rows = wkv.shape[1] // (pipe_count * lax.axis_size("head"))

    def compute():
        key_rows = wkv[0]
        value_rows = wkv[1]
        term = lax.dot_general(
            key_rows, grads[:, :width], (((1,), (1,)), ((), ())), preferred_element_type=jnp.float32
        )
        return term + lax.dot_general(
            value_rows,
            grads[:, width:],
            (((1,), (1,)), ((), ())),
            preferred_element_type=jnp.float32,
        )

    memory_grad = lax.psum_scatter(
        lax.cond(
            is_dec,
            compute,
            lambda: jnp.zeros(
                (lax.axis_size(("pipe", "head")) * out_rows, grads.shape[0]), jnp.float32
            ),
        ),
        ("pipe", "head"),
        scatter_dimension=0,
        tiled=True,
    )
    return (current[None], jnp.stack(produced, axis=0)[None], memory_grad)


def solution(mesh):
    return jax.shard_map(
        body,
        mesh=mesh,
        in_specs=(
            P("pipe", "head", None),
            P(None, "head", None),
            P("pipe", None),
            P(),
            P("pipe", None, "head"),
            P("pipe", None, None, "head"),
            P("pipe", "head", None),
            P("pipe", None, None, "head"),
            P("pipe", None, "head"),
        ),
        out_specs=(
            P("pipe", "head", None),
            P("pipe", None, None, "head"),
            P(("pipe", "head"), None),
        ),
        check_vma=False,
    )
```

profile of v0, /device:TPU:30, one launch (start us, length us, event | category | flops | bytes accessed | tf_op | source)
XLA Modules:
  0.0 1611.0 jit_solution(11383313471393974794)
XLA Ops:
  8.0 0.0 copy-start
  8.0 0.0 reduce-scatter.3.cloned.1.call-start
  8.1 1.1 copy.37
  9.2 20.8 %all-gather = bf16[1,2048,128]{1,2,0:T(8,128)(2,1)S(1)} all-gather(bf16[1,256,128]{1,2,0:T(8,128)(2,1)S(1)} %copy.37), channel_id=2, replica_groups=mesh['pipe'=64,'head'=8] {'head'}, dimensions={1}, use_global_device_ids=true | all-gather | bytes 589824 | tf_op jit(solution)/shard_map/all_gather | solution.py:62
  29.9 0.8 copy-done.2
  30.7 0.2 fusion.26
  30.9 1.6 fusion.54
  32.6 0.1 copy.48
  32.7 2.0 fusion.28
  34.7 3.2 conditional.5
  34.7 2.1 convolution_convert_fusion
  36.9 1.0 copy.31
  37.9 0.0 copy-start.3
  37.9 0.6 copy-done.3
  38.5 0.9 bitcast_select_fusion.1
  39.5 1.9 fusion.56
  41.4 1.3 fusion.11
  42.7 0.0 reduce-scatter.3.cloned.1.call-update
  42.7 0.0 all-reduce.5.cloned.1.call-start
  42.8 0.9 fusion.55
  43.7 0.1 copy.46
  43.8 0.0 copy-start.8
  43.8 0.7 copy.47
  44.6 0.8 copy.49
  45.3 35.7 %reduce-scatter.3.cloned.1.call-done = bf16[256,128]{0,1:T(8,128)(2,1)} async-done(((bf16[2048,128]{0,1:T(8,128)(2,1)}), bf16[256,128]{0,1:T(8,128)(2,1)}) %reduce-scatter.3.cloned.1.call-update) | async-done | bytes 65552 | tf_op jit(solution)/shard_map/reduce_scatter | solution.py:73
  81.0 0.9 fusion.35
  81.9 15.3 all_gather.14
  97.2 2.4 collective-permute-start
  99.5 0.8 broadcast_select_fusion.1
  100.4 0.0 all-reduce.5.cloned.1.call-update
  100.4 0.0 reduce-scatter.5.cloned.1.call-start
  100.5 3.8 collective-permute-done
  104.3 15.3 all_gather.13
  119.6 0.2 fusion.17
  119.8 1.0 fusion.19
  120.8 1.6 conditional.6
  120.8 1.5 convolution_convert_fusion.1
  122.3 0.1 copy.32
  122.4 584.5 %all-reduce.5.cloned.1.call-done = bf16[2048,128]{0,1:T(8,128)(2,1)} async-done(((bf16[2048,128]{0,1:T(8,128)(2,1)}), bf16[2048,128]{0,1:T(8,128)(2,1)}) %all-reduce.5.cloned.1.call-update) | async-done | bytes 524304 | tf_op jit(solution)/shard_map/psum | solution.py:14
  706.9 1.2 fusion.20
  708.2 2.0 fusion.22
  710.3 1.0 fusion.36
  711.3 1.9 fusion.59
  713.2 1.3 fusion.12
  714.5 0.0 reduce-scatter.5.cloned.1.call-update
  714.5 0.0 all-reduce.9.cloned.1.call-start
  714.5 1.1 conditional.9
  714.6 1.1 broadcast.72
  715.6 0.0 all-reduce.9.cloned.1.call-update
  715.7 0.0 all-reduce.7.cloned.1.call-start
  715.7 39.1 %reduce-scatter.5.cloned.1.call-done = bf16[256,128]{0,1:T(8,128)(2,1)} async-done(((bf16[2048,128]{0,1:T(8,128)(2,1)}), bf16[256,128]{0,1:T(8,128)(2,1)}) %reduce-scatter.5.cloned.1.call-update) | async-done | bytes 65552 | tf_op jit(solution)/shard_map/reduce_scatter | solution.py:73
  754.8 0.9 add_convert_fusion
  755.7 15.4 all_gather.15
  771.1 0.8 broadcast_select_fusion
  772.0 0.0 all-reduce.7.cloned.1.call-update
  772.0 2.4 collective-permute-start.1
  774.4 220.2 %all-reduce.9.cloned.1.call-done = f32[2048,128]{1,0:T(8,128)} async-done(((f32[2048,128]{1,0:T(8,128)}), f32[2048,128]{1,0:T(8,128)}) %all-reduce.9.cloned.1.call-update) | async-done | bytes 1048592
  994.7 1.3 constant_dynamic-slice_fusion
  995.9 0.1 copy.41
  996.1 0.7 copy.43
  996.8 603.8 %all-reduce.7.cloned.1.call-done = bf16[2048,128]{0,1:T(8,128)(2,1)} async-done(((bf16[2048,128]{0,1:T(8,128)(2,1)}), bf16[2048,128]{0,1:T(8,128)(2,1)}) %all-reduce.7.cloned.1.call-update) | async-done | bytes 524304 | tf_op jit(solution)/shard_map/psum | solution.py:14
  1600.6 1.2 fusion.23
  1601.9 1.2 fusion.25
  1603.1 0.7 maximum_bitcast_fusion
  (26 shorter events, 0.3 us)
Async XLA Ops:
  8.0 33.4 %copy-start = (bf16[1,256,2048]{2,1,0:T(8,128)(2,1)S(1)}, bf16[1,256,2048]{2,1,0:T(8,128)(2,1)}, u32[]{:S(2)}) copy-start(bf16[1,256,2048]{2,1,0:T(8,128)(2,1)} %param.25) | copy-start | bytes 3145732
  8.0 26.7 %copy-start.1 = (bf16[1,2,2048,256]{3,2,1,0:T(8,128)(2,1)S(1)}, bf16[1,2,2048,256]{3,2,1,0:T(8,128)(2,1)}, u32[]{:S(2)}) copy-start(bf16[1,2,2048,256]{3,2,1,0:T(8,128)(2,1)} %param.24) | copy-start | bytes 6291460
  8.0 73.0 %reduce-scatter.3.cloned.1.call-start = ((), (), s32[]{:S(2)}) async-start(), calls=%async_computation.2 | async-start | bytes 589824 | tf_op jit(solution)/shard_map/reduce_scatter | solution.py:73
  29.9 0.8 copy-start.2
  37.9 0.7 copy-start.3
  39.5 5.1 copy-start.4
  42.7 664.2 %all-reduce.5.cloned.1.call-start = ((), (), s32[]{:S(2)}) async-start(), calls=%async_computation.3 | async-start | bytes 1048576 | tf_op jit(solution)/shard_map/psum | solution.py:14
  43.8 76.0 %copy-start.8 = (f32[1,2048]{1,0:T(1,128)S(1)}, f32[1,2048]{1,0:T(1,128)}, u32[]{:S(2)}) copy-start(f32[1,2048]{1,0:T(1,128)} %param.21) | copy-start | bytes 24580
  45.3 59.0 %copy-start.6 = (bf16[1,256,128]{1,2,0:T(8,128)(2,1)S(1)}, bf16[1,256,128]{1,2,0:T(8,128)(2,1)}, u32[]{:S(2)}) copy-start(bf16[1,256,128]{1,2,0:T(8,128)(2,1)} %copy.47) | copy-start | bytes 196612
  97.2 7.1 collective-permute-start
  100.4 654.4 %reduce-scatter.5.cloned.1.call-start = ((), (), s32[]{:S(2)}) async-start(), calls=%async_computation.4 | async-start | bytes 589824 | tf_op jit(solution)/shard_map/reduce_scatter | solution.py:73
  120.8 587.4 %copy-start.9 = (f32[2048]{0:T(1024)S(1)}, f32[2048]{0:T(1024)}, u32[]{:S(2)}) copy-start(f32[2048]{0:T(1024)} %param.22) | copy-start | bytes 24580
  122.4 587.8 %copy-start.5 = (bf16[128,512]{0,1:T(8,128)(2,1)}, bf16[128,512]{0,1:T(8,128)(2,1)S(1)}, u32[]{:S(2)}) copy-start(bf16[128,512]{0,1:T(8,128)(2,1)S(1)} %get-tuple-element.73) | copy-start | bytes 393220
  714.5 280.2 %all-reduce.9.cloned.1.call-start = ((), (), s32[]{:S(2)}) async-start(), calls=%async_computation.6 | async-start | bytes 2097152
  715.7 884.9 %all-reduce.7.cloned.1.call-start = ((), (), s32[]{:S(2)}) async-start(), calls=%async_computation.5 | async-start | bytes 1048576 | tf_op jit(solution)/shard_map/psum | solution.py:14
  772.0 224.1 %collective-permute-start.1 = (bf16[256,128]{0,1:T(8,128)(2,1)S(1)}, bf16[256,128]{0,1:T(8,128)(2,1)S(1)}, u32[]{:S(2)}, u32[]{:S(2)}) collective-permute-start(bf16[256,128]{0,1:T(8,128)(2,1)S(1)} %add_convert_fusion), channel_id=1, source_target_pairs={{0,8},{8,16},{16,24},{24,32},{32,40},{40,48},{48,56},{56,64},{64,7... | collective-permute-start | bytes 196616 | tf_op jit(solution)/shard_map/ppermute | solution.py:20
Sparse Core Ops, SparseCore 0:
  42.9 38.0 reduce-scatter.2
  100.5 606.3 all-reduce.4
  714.6 40.1 reduce-scatter.4
Sparse Core Ops, SparseCore 1:
  720.8 273.8 all-reduce.8
  997.4 603.1 all-reduce.6
where the time goes:
time: 1610 us
  waiting for transfers between devices  1490 us (93%)
  blocking collectives  66.8 us (4%)
    psum x2, waiting for transfers between devices, broadcast(): return lax.psum(block, axis)  1190 us
    unnamed x6, waiting for transfers between devices  220 us
    reduce_scatter x2, waiting for transfers between devices, body(): lax.psum_scatter(lax.dot_general(wo, attn, (((0,), (1,)), ((), ())), pref...  74.8 us
    all_gather x2, blocking collectives, body(): whole = lax.all_gather(current, 'head', axis=0, tiled=True)  36.1 us
  transfers between devices with their start and end apart: 7, of which 6 were waited for; matrix products, arithmetic and copies ran while one was open for 1% of the time, Pallas kernels for 0%

commit v1 on v0

v1 whole, which is shorter than its diff:
```python
import jax
import jax.numpy as jnp
from jax import lax
from jax.experimental import pallas as pl
from jax.experimental.pallas import tpu as pltpu
from jax.sharding import Mesh, PartitionSpec as P

TICKS = 2
EPS = 1e-06
PIPE = ("y", "x", "zl")
HEAD = ("zh", "c")
Y, X, ZL, ZH, C = 8, 4, 2, 4, 2
BF, F32 = jnp.bfloat16, jnp.float32


def place(y, x, zl):
    return (y * X + x) * ZL + zl


def norm_into(out, source, scale):
    heads, tokens, width = source.shape
    total = jnp.zeros((tokens, width), F32)
    for h in range(heads):
        wide = source[h].astype(F32)
        total = total + wide * wide
    mean = jnp.sum(total, axis=1, keepdims=True) / (heads * width)
    factor = lax.rsqrt(mean + EPS)
    for h in range(heads):
        wide = source[h].astype(F32)
        out[h] = (wide * factor * scale[h]).astype(BF)


def project(rows, weight):
    heads, tokens, width = rows.shape
    total = jnp.zeros((tokens, weight.shape[1]), F32)
    for h in range(heads):
        total = total + jnp.dot(
            rows[h], weight[h * width : (h + 1) * width, :], preferred_element_type=F32
        )
    return total.astype(BF)


def attend_and_project(query, pair, wo, out):
    width = query.shape[1]
    scores = lax.dot_general(
        query, pair[:, :width], (((1,), (1,)), ((), ())), preferred_element_type=F32
    )
    scores = scores * width ** (-0.5)
    scores = jnp.exp(scores - jnp.max(scores, axis=-1, keepdims=True))
    probs = (scores / jnp.sum(scores, axis=-1, keepdims=True)).astype(BF)
    attn = jnp.dot(probs, pair[:, width:], preferred_element_type=F32).astype(BF)
    for h in range(out.shape[0]):
        out[h] = jnp.dot(
            attn, wo[:, h * width : (h + 1) * width], preferred_element_type=F32
        ).astype(BF)


def first_kernel(section, half, x, gain, wq, wkv, wo, cross, out, normed, pair):
    width = wq.shape[1]
    norm_into(normed, x, gain)
    query = project(normed, wq)

    @pl.when(section[0] < half)
    def _():
        pair[:, :width] = project(normed, wkv.at[0])
        pair[:, width:] = project(normed, wkv.at[1])

    @pl.when(section[0] >= half)
    def _():
        pair[...] = cross[...]

    attend_and_project(query, pair, wo, out)


def second_kernel(
    section, half, x, fresh, gain, final_gain, wq, wkv, wo, cross, out, normed, kv_rows, pair
):
    width = wq.shape[1]

    @pl.when(section[0] == half)
    def _():
        norm_into(normed, fresh, gain)
        norm_into(kv_rows, x, final_gain)
        pair[:, :width] = project(kv_rows, wkv.at[0])
        pair[:, width:] = project(kv_rows, wkv.at[1])

    @pl.when(section[0] != half)
    def _():
        norm_into(normed, x, gain)

    @pl.when(section[0] < half)
    def _():
        pair[:, :width] = project(normed, wkv.at[0])
        pair[:, width:] = project(normed, wkv.at[1])

    @pl.when(section[0] > half)
    def _():
        pair[...] = cross[...]

    attend_and_project(project(normed, wq), pair, wo, out)


def memory_kernel(section, half, first, second, final_gain, wkv, out, rows):
    width = wkv.shape[2]

    @pl.when(section[0] >= half)
    def _():
        for t, source in enumerate((first, second)):
            norm_into(rows, source, final_gain)
            out[t, :, :width] = project(rows, wkv.at[0])
            out[t, :, width:] = project(rows, wkv.at[1])

    @pl.when(section[0] < half)
    def _():
        out[...] = jnp.zeros_like(out)


def call(kernel, section, half, operands, out_shape, scratch, cost):
    def with_half(section_ref, *refs):
        kernel(section_ref, half, *refs)

    return pl.pallas_call(
        with_half,
        out_shape=jax.ShapeDtypeStruct(out_shape, BF),
        in_specs=[pl.BlockSpec(memory_space=pltpu.SMEM)]
        + [pl.BlockSpec(memory_space=pltpu.VMEM)] * len(operands),
        out_specs=pl.BlockSpec(memory_space=pltpu.VMEM),
        scratch_shapes=[pltpu.VMEM(shape, BF) for shape in scratch],
        compiler_params=pltpu.CompilerParams(vmem_limit_bytes=24 * 1024 * 1024),
        cost_estimate=pl.CostEstimate(flops=cost, bytes_accessed=5_000_000, transcendentals=0),
    )(section, *operands)


def spread(block, source):
    y, x, zl = lax.axis_index("y"), lax.axis_index("x"), lax.axis_index("zl")
    sy, sx, sz = source // (X * ZL), source // ZL % X, source % ZL
    held = block
    for to in range(sy + 1, Y):
        sent = lax.ppermute(block, PIPE, [(source, place(to, sx, sz))])
        held = jnp.where(y == to, sent, held)
    column = held
    for to in range(X):
        if to != sx:
            pairs = [(place(k, sx, sz), place(k, to, sz)) for k in range(sy + 1, Y)]
            held = jnp.where(x == to, lax.ppermute(column, PIPE, pairs), held)
    pairs = [
        (place(k, to, sz), place(k, to, 1 - sz)) for k in range(sy + 1, Y) for to in range(X)
    ]
    return jnp.where(zl == sz, held, lax.ppermute(held, PIPE, pairs))


def body(stream, fresh, gain, final_gain, w_query, w_kv, w_out, cache_kv, cache_grad):
    pipe_count, heads = Y * X * ZL, ZH * C
    half = pipe_count // 2
    place_here = lax.axis_index(PIPE)
    section = place_here.astype(jnp.int32)[None]
    wq, wkv, wo = w_query[0], w_kv[0], w_out[0]
    depth, width = wq.shape
    tokens = stream.shape[2]
    scale = gain[0].reshape(heads, 1, width)
    final_scale = final_gain.reshape(heads, 1, width)

    grads = jnp.where(place_here >= half, cache_grad[0], jnp.zeros_like(cache_grad[0]))
    rows_by = (((1,), (1,)), ((), ()))
    share = lax.dot_general(wkv[0], grads[:, :width], rows_by, preferred_element_type=F32)
    share = share + lax.dot_general(wkv[1], grads[:, width:], rows_by, preferred_element_type=F32)
    share = lax.psum_scatter(share, "y", scatter_dimension=0, tiled=True)
    share = lax.psum_scatter(share, "x", scatter_dimension=0, tiled=True)
    share = share.reshape(ZL * heads, 1, depth // (pipe_count * heads), tokens)
    share = jnp.concatenate([share, share, share, share], axis=1)
    share = lax.psum_scatter(share, ("zl",) + HEAD, scatter_dimension=0, tiled=False)
    memory_grad = share[0]

    def whole(block):
        return lax.all_gather(block, HEAD, axis=0)

    def summed(parts, current):
        parts = lax.all_to_all(parts, HEAD, 0, 0, tiled=True)
        return (current.astype(F32) + jnp.sum(parts.astype(F32), axis=0)).astype(BF)

    shift = [(i, i + 1) for i in range(pipe_count - 1)]
    fresh_rows = jnp.swapaxes(fresh, 1, 2)
    fresh_whole = lax.all_gather(fresh_rows, HEAD, axis=0)[:, 1]

    rows8 = (heads, tokens, width)
    pair_shape = (tokens, 2 * width)
    flops = 2 * tokens * depth * width * 4

    current = stream[0].T
    parts = call(
        first_kernel, section, half,
        (whole(current), scale, wq, wkv, wo, cache_kv[0, 0]),
        rows8, (rows8, pair_shape), flops,
    )
    output = summed(parts, current)
    passed = lax.ppermute(output, PIPE, shift)
    first_memory = spread(output, half - 1)

    current = jnp.where(place_here == 0, fresh_rows[0], passed)
    parts = call(
        second_kernel, section, half,
        (whole(current), fresh_whole, scale, final_scale, wq, wkv, wo, cache_kv[0, 1]),
        rows8, (rows8, rows8, pair_shape), flops,
    )
    current = jnp.where(place_here == half, fresh_rows[1], current)
    output = summed(parts, current)
    passed = lax.ppermute(output, PIPE, shift)
    last = jnp.where(place_here == half, jnp.zeros_like(passed), passed)

    second_memory = spread(output, half - 1)
    new_kv = call(
        memory_kernel, section, half,
        (whole(first_memory), whole(second_memory), final_scale, wkv),
        (TICKS, tokens, 2 * width), (rows8,), flops,
    )
    return (last.T[None], new_kv[None], memory_grad)


def solution(mesh):
    split = Mesh(mesh.devices.reshape(Y, X, ZL, ZH, C), PIPE + HEAD)
    return jax.shard_map(
        body,
        mesh=split,
        in_specs=(
            P(PIPE, HEAD, None),
            P(None, HEAD, None),
            P(PIPE, None),
            P(),
            P(PIPE, None, HEAD),
            P(PIPE, None, None, HEAD),
            P(PIPE, HEAD, None),
            P(PIPE, None, None, HEAD),
            P(PIPE, None, HEAD),
        ),
        out_specs=(
            P(PIPE, HEAD, None),
            P(PIPE, None, None, HEAD),
            P(PIPE + HEAD, None),
        ),
        check_vma=False,
    )
```

time: 1610 us -> 302 us (0.19)
  the two profiles are of different devices: /device:TPU:30 before, /device:TPU:33 now
where the time goes in v1:
time: 302 us; the launch traced here: 301 us
  waiting for transfers between devices  151 us (50%)
  blocking collectives  79.2 us (26%)
  starting transfers between devices  27.1 us (9%)
  local copies, waits for them, and re-layouts  19.1 us (6%)
  between operations  16.2 us (5%)
  Pallas kernels  4.66 us (2%)
    unnamed x5, waiting for transfers between devices  115 us
    all_gather x4, blocking collectives, whole(): return lax.all_gather(block, HEAD, axis=0)  79.2 us
    unnamed x31, local copies, waits for them, and re-layouts  13.7 us
    all_to_all x2, waiting for transfers between devices, summed(): parts = lax.all_to_all(parts, HEAD, 0, 0, tiled=True)  12.4 us
    ppermute x2, waiting for transfers between devices, spread(): return jnp.where(zl == sz, held, lax.ppermute(held, PIPE, pairs))  11.3 us
    ppermute x2, waiting for transfers between devices, body(): passed = lax.ppermute(output, PIPE, shift)  10.8 us
    all_to_all x2, starting transfers between devices, summed(): parts = lax.all_to_all(parts, HEAD, 0, 0, tiled=True)  8.66 us
    ppermute x2, starting transfers between devices, body(): passed = lax.ppermute(output, PIPE, shift)  6.51 us
  transfers between devices with their start and end apart: 24, of which 6 were waited for; matrix products, arithmetic and copies ran while one was open for 5% of the time, Pallas kernels for 1%

profile of v1, /device:TPU:33, one launch (start us, length us, event | category | flops | bytes accessed | tf_op | source)
XLA Modules:
  0.0 301.3 jit_solution(1184838733477185150)
XLA Ops:
  8.0 0.0 all-gather.7.cloned.1.call-start
  8.1 1.7 copy.22
  9.8 0.0 all-gather.7.cloned.1.call-update
  9.8 0.9 copy.23
  10.8 21.3 %all-gather = bf16[1024,256]{1,0:T(8,128)(2,1)S(1)} all-gather(bf16[128,256]{1,0:T(8,128)(2,1)S(1)} %bitcast.72), channel_id=2, replica_groups=mesh['y'=8,'x'=4,'zl'=2,'zh'=4,'c'=2] {'zh','c'}, dimensions={0}, use_global_device_ids=true | all-gather | bytes 589824 | tf_op jit(solution)/shard_map/all_gather | solution.py:175
  32.1 1.0 slice_bitcast_fusion.1
  33.1 0.0 copy-start
  33.1 1.6 copy-done
  34.7 1.2 copy-done.3
  35.9 0.7 copy-done.8
  36.6 1.2 shard_map.112
  37.8 0.8 copy-done.7
  38.6 4.9 %all-to-all-start = ((bf16[8,128,256]{2,1,0:T(8,128)(2,1)}), bf16[8,128,256]{2,1,0:T(8,128)(2,1)}, u32[]{:S(2)}, u32[]{:S(2)}) async-start(bf16[8,128,256]{2,1,0:T(8,128)(2,1)} %copy-done.7), calls=%async_computation | async-start | bytes 1048576 | tf_op jit(solution)/shard_map/all_to_all | solution.py:178
  43.5 0.5 fusion.2
  43.9 0.0 copy-start.11
  43.9 1.5 fusion
  45.4 0.0 reduce-scatter.5.cloned.1.call-update
  45.4 12.4 %all-to-all-done = bf16[8,128,256]{2,1,0:T(8,128)(2,1)} async-done(((bf16[8,128,256]{2,1,0:T(8,128)(2,1)}), bf16[8,128,256]{2,1,0:T(8,128)(2,1)}, u32[]{:S(2)}, u32[]{:S(2)}) %all-to-all-start) | async-done | bytes 524320 | tf_op jit(solution)/shard_map/all_to_all | solution.py:178
  57.9 1.1 convert_reduce_fusion.1
  59.0 4.6 %collective-permute-start = (bf16[128,256]{1,0:T(8,128)(2,1)S(1)}, bf16[128,256]{1,0:T(8,128)(2,1)}, u32[]{:S(2)}, u32[]{:S(2)}) collective-permute-start(bf16[128,256]{1,0:T(8,128)(2,1)S(1)} %add_convert_fusion.1), channel_id=1, source_target_pairs={{0,8},{8,16},{16,24},{24,32},{32,40},{40,48},{48,56},{56,64},{64,7... | collective-permute-start | bytes 196616 | tf_op jit(solution)/shard_map/ppermute | solution.py:196
  63.6 4.7 %collective-permute-done = bf16[128,256]{1,0:T(8,128)(2,1)} collective-permute-done((bf16[128,256]{1,0:T(8,128)(2,1)S(1)}, bf16[128,256]{1,0:T(8,128)(2,1)}, u32[]{:S(2)}, u32[]{:S(2)}) %collective-permute-start) | collective-permute-done | bytes 65568 | tf_op jit(solution)/shard_map/ppermute | solution.py:196
  68.3 0.9 fusion.8
  69.2 20.1 %all-gather.1 = bf16[1024,256]{1,0:T(8,128)(2,1)} all-gather(bf16[128,256]{1,0:T(8,128)(2,1)S(1)} %fusion.8), channel_id=3, replica_groups=mesh['y'=8,'x'=4,'zl'=2,'zh'=4,'c'=2] {'zh','c'}, dimensions={0}, use_global_device_ids=true | all-gather | bytes 589824 | tf_op jit(solution)/shard_map/all_gather | solution.py:175
  89.3 1.1 slice_bitcast_fusion.refs_1_
  90.4 0.0 copy-start.4
  90.4 1.2 copy-done.4
  91.6 1.0 copy-done.6
  92.6 1.8 shard_map.113
  94.5 0.8 copy-done.5
  95.3 3.8 %all-to-all-start.1 = ((bf16[8,128,256]{2,1,0:T(8,128)(2,1)}), bf16[8,128,256]{2,1,0:T(8,128)(2,1)S(1)}, u32[]{:S(2)}, u32[]{:S(2)}) async-start(bf16[8,128,256]{2,1,0:T(8,128)(2,1)} %copy-done.5), calls=%async_computation.1 | async-start | bytes 1048576 | tf_op jit(solution)/shard_map/all_to_all | solution.py:178
  99.1 0.7 collective-permute-start.2
  99.7 0.7 collective-permute-start.3
  100.4 0.7 collective-permute-start.4
  101.1 0.7 collective-permute-start.5
  101.8 0.7 collective-permute-start.6
  102.5 0.7 collective-permute-start.7
  103.2 0.7 collective-permute-start.8
  103.9 1.3 collective-permute-start.9
  105.2 1.3 dynamic-slice
  106.5 11.3 %collective-permute-done.9 = bf16[128,256]{1,0:T(8,128)(2,1)S(1)} collective-permute-done((bf16[128,256]{1,0:T(8,128)(2,1)S(1)}, bf16[128,256]{1,0:T(8,128)(2,1)S(1)}, u32[]{:S(2)}, u32[]{:S(2)}) %collective-permute-start.9) | collective-permute-done | bytes 65568 | tf_op jit(solution)/shard_map/ppermute | solution.py:149
  117.8 0.0 reduce-scatter.5.cloned.1.call-done
  117.9 1.7 copy.27
  119.5 0.0 reduce-scatter.7.cloned.1.call-update
  119.5 0.0 all-reduce.3.cloned.1.call-start
  119.6 0.1 convert_reduce_fusion
  119.7 0.7 collective-permute-start.10
  120.4 0.7 collective-permute-start.11
  121.1 0.7 collective-permute-start.12
  121.7 0.7 collective-permute-start.13
  122.4 19.5 %all-gather.3 = bf16[1024,256]{1,0:T(8,128)(2,1)S(1)} all-gather(bf16[128,256]{1,0:T(8,128)(2,1)S(1)} %broadcast_select_fusion.1), channel_id=5, replica_groups=mesh['y'=8,'x'=4,'zl'=2,'zh'=4,'c'=2] {'zh','c'}, dimensions={0}, use_global_device_ids=true | all-gather | bytes 589824 | tf_op jit(solution)/shard_map/all_gather | solution.py:175
  141.9 1.6 reduce-scatter.7.cloned.1.call-done
  143.5 1.4 concatenate.3
  144.9 0.0 all-reduce.3.cloned.1.call-update
  145.0 0.7 collective-permute-start.14
  145.7 0.7 collective-permute-start.15
  146.4 0.7 collective-permute-start.16
  147.0 114.7 %all-reduce.3.cloned.1.call-done = f32[16,4,4,128]{3,2,1,0:T(4,128)} async-done(((f32[16,4,4,128]{3,2,1,0:T(4,128)}), f32[16,4,4,128]{3,2,1,0:T(4,128)}) %all-reduce.3.cloned.1.call-update) | async-done | bytes 131088
  261.7 1.9 dynamic-slice_bitcast_fusion
  263.6 1.9 collective-permute-start.1
  265.6 1.3 collective-permute-start.17
  266.9 6.1 %collective-permute-done.1 = bf16[128,256]{1,0:T(8,128)(2,1)S(1)} collective-permute-done((bf16[128,256]{1,0:T(8,128)(2,1)S(1)}, bf16[128,256]{1,0:T(8,128)(2,1)S(1)}, u32[]{:S(2)}, u32[]{:S(2)}) %collective-permute-start.1) | collective-permute-done | bytes 65568 | tf_op jit(solution)/shard_map/ppermute | solution.py:207
  273.0 0.7 copy.26
  273.7 18.4 %all-gather.4 = bf16[1024,256]{1,0:T(8,128)(2,1)S(1)} all-gather(bf16[128,256]{1,0:T(8,128)(2,1)S(1)} %broadcast_select_fusion), channel_id=6, replica_groups=mesh['y'=8,'x'=4,'zl'=2,'zh'=4,'c'=2] {'zh','c'}, dimensions={0}, use_global_device_ids=true | all-gather | bytes 589824 | tf_op jit(solution)/shard_map/all_gather | solution.py:175
  292.1 1.6 shard_map.114
  (45 shorter events, 0.2 us)
Async XLA Ops:
  8.0 25.0 %copy-start.2 = (bf16[1,2048,256]{2,1,0:T(8,128)(2,1)S(1)}, bf16[1,2048,256]{2,1,0:T(8,128)(2,1)}, u32[]{:S(2)}) copy-start(bf16[1,2048,256]{2,1,0:T(8,128)(2,1)} %param.13) | copy-start | bytes 3145732
  8.0 81.2 %all-gather.7.cloned.1.call-start = ((), (), s32[]{:S(2)}) async-start(), calls=%async_computation.5 | async-start | bytes 1179648 | tf_op jit(solution)/shard_map/all_gather | solution.py:183
  33.1 1.6 copy-start
  34.6 1.2 copy-start.3
  35.9 0.7 copy-start.8
  36.6 6.9 %copy-start.12 = (bf16[1,128,512]{2,1,0:T(8,128)(2,1)S(1)}, bf16[1,128,512]{2,1,0:T(8,128)(2,1)}, u32[]{:S(2)}) copy-start(bf16[1,128,512]{2,1,0:T(8,128)(2,1)} %param.17) | copy-start | bytes 393220
  36.6 6.9 %copy-start.1 = (bf16[1,2,2048,256]{3,2,1,0:T(8,128)(2,1)S(1)}, bf16[1,2,2048,256]{3,2,1,0:T(8,128)(2,1)}, u32[]{:S(2)}) copy-start(bf16[1,2,2048,256]{3,2,1,0:T(8,128)(2,1)} %param.14) | copy-start | bytes 6291460
  37.8 0.8 copy-start.7
  38.6 19.3 %all-to-all-start = ((bf16[8,128,256]{2,1,0:T(8,128)(2,1)}), bf16[8,128,256]{2,1,0:T(8,128)(2,1)}, u32[]{:S(2)}, u32[]{:S(2)}) async-start(bf16[8,128,256]{2,1,0:T(8,128)(2,1)} %copy-done.7), calls=%async_computation | async-start | bytes 1048576 | tf_op jit(solution)/shard_map/all_to_all | solution.py:178
  43.4 74.4 %reduce-scatter.5.cloned.1.call-start = ((), (), s32[]{:S(2)}) async-start(), calls=%async_computation.4 | async-start | bytes 1179648 | tf_op jit(solution)/shard_map/reduce_scatter | solution.py:167
  43.9 24.4 %copy-start.11 = (bf16[2,256,128]{1,2,0:T(8,128)(2,1)S(1)}, bf16[2,256,128]{1,2,0:T(8,128)(2,1)}, u32[]{:S(2)}) copy-start(bf16[2,256,128]{1,2,0:T(8,128)(2,1)} %copy.22) | copy-start | bytes 393220
  45.4 44.9 %copy-start.9 = (f32[1,2048]{1,0:T(1,128)S(1)}, f32[1,2048]{1,0:T(1,128)}, u32[]{:S(2)}) copy-start(f32[1,2048]{1,0:T(1,128)} %param.11) | copy-start | bytes 24580
  45.4 44.9 %copy-start.10 = (f32[2048]{0:T(1024)S(1)}, f32[2048]{0:T(1024)}, u32[]{:S(2)}) copy-start(f32[2048]{0:T(1024)} %param.12) | copy-start | bytes 24580
  59.0 9.3 %collective-permute-start = (bf16[128,256]{1,0:T(8,128)(2,1)S(1)}, bf16[128,256]{1,0:T(8,128)(2,1)}, u32[]{:S(2)}, u32[]{:S(2)}) collective-permute-start(bf16[128,256]{1,0:T(8,128)(2,1)S(1)} %add_convert_fusion.1), channel_id=1, source_target_pairs={{0,8},{8,16},{16,24},{24,32},{32,40},{40,48},{48,56},{56,64},{64,7... | collective-permute-start | bytes 196616 | tf_op jit(solution)/shard_map/ppermute | solution.py:196
  90.4 1.2 copy-start.4
  91.6 1.0 copy-start.6
  94.5 0.8 copy-start.5
  95.3 24.3 %all-to-all-start.1 = ((bf16[8,128,256]{2,1,0:T(8,128)(2,1)}), bf16[8,128,256]{2,1,0:T(8,128)(2,1)S(1)}, u32[]{:S(2)}, u32[]{:S(2)}) async-start(bf16[8,128,256]{2,1,0:T(8,128)(2,1)} %copy-done.5), calls=%async_computation.1 | async-start | bytes 1048576 | tf_op jit(solution)/shard_map/all_to_all | solution.py:178
  99.1 44.4 %reduce-scatter.7.cloned.1.call-start = ((), (), s32[]{:S(2)}) async-start(), calls=%async_computation.6 | async-start | bytes 163840 | tf_op jit(solution)/shard_map/reduce_scatter | solution.py:168
  99.1 2.7 collective-permute-start.2
  99.7 2.0 collective-permute-start.3
  100.4 1.4 collective-permute-start.4
  101.1 0.7 collective-permute-start.5
  101.8 2.0 collective-permute-start.6
  102.5 1.4 collective-permute-start.7
  103.2 0.7 collective-permute-start.8
  103.9 13.9 %collective-permute-start.9 = (bf16[128,256]{1,0:T(8,128)(2,1)S(1)}, bf16[128,256]{1,0:T(8,128)(2,1)S(1)}, u32[]{:S(2)}, u32[]{:S(2)}) collective-permute-start(bf16[128,256]{1,0:T(8,128)(2,1)S(1)} %select_select_fusion.2), channel_id=1, source_target_pairs={{264,256},{280,272},{296,288},{312,304},{328,320},{344,336},{360,3... | collective-permute-start | bytes 196616 | tf_op jit(solution)/shard_map/ppermute | solution.py:149
  119.5 142.2 %all-reduce.3.cloned.1.call-start = ((), (), s32[]{:S(2)}) async-start(), calls=%async_computation.7 | async-start | bytes 262144
  119.7 25.2 %collective-permute-start.10 = (bf16[128,256]{1,0:T(8,128)(2,1)S(1)}, bf16[128,256]{1,0:T(8,128)(2,1)S(1)}, u32[]{:S(2)}, u32[]{:S(2)}) collective-permute-start(bf16[128,256]{1,0:T(8,128)(2,1)S(1)} %add_convert_fusion), channel_id=1, source_target_pairs={{248,504},{249,505},{250,506},{251,507},{252,508},{253,509},{254,5... | collective-permute-start | bytes 196616 | tf_op jit(solution)/shard_map/ppermute | solution.py:139
  120.4 24.6 %collective-permute-start.11 = (bf16[128,256]{1,0:T(8,128)(2,1)S(1)}, bf16[128,256]{1,0:T(8,128)(2,1)S(1)}, u32[]{:S(2)}, u32[]{:S(2)}) collective-permute-start(bf16[128,256]{1,0:T(8,128)(2,1)S(1)} %add_convert_fusion), channel_id=1, source_target_pairs={{248,440},{249,441},{250,442},{251,443},{252,444},{253,445},{254,4... | collective-permute-start | bytes 196616 | tf_op jit(solution)/shard_map/ppermute | solution.py:139
  121.1 23.9 %collective-permute-start.12 = (bf16[128,256]{1,0:T(8,128)(2,1)S(1)}, bf16[128,256]{1,0:T(8,128)(2,1)S(1)}, u32[]{:S(2)}, u32[]{:S(2)}) collective-permute-start(bf16[128,256]{1,0:T(8,128)(2,1)S(1)} %add_convert_fusion), channel_id=1, source_target_pairs={{248,376},{249,377},{250,378},{251,379},{252,380},{253,381},{254,3... | collective-permute-start | bytes 196616 | tf_op jit(solution)/shard_map/ppermute | solution.py:139
  121.7 23.3 %collective-permute-start.13 = (bf16[128,256]{1,0:T(8,128)(2,1)S(1)}, bf16[128,256]{1,0:T(8,128)(2,1)S(1)}, u32[]{:S(2)}, u32[]{:S(2)}) collective-permute-start(bf16[128,256]{1,0:T(8,128)(2,1)S(1)} %add_convert_fusion), channel_id=1, source_target_pairs={{248,312},{249,313},{250,314},{251,315},{252,316},{253,317},{254,3... | collective-permute-start | bytes 196616 | tf_op jit(solution)/shard_map/ppermute | solution.py:139
  145.0 120.5 %collective-permute-start.14 = (bf16[128,256]{1,0:T(8,128)(2,1)S(1)}, bf16[128,256]{1,0:T(8,128)(2,1)S(1)}, u32[]{:S(2)}, u32[]{:S(2)}) collective-permute-start(bf16[128,256]{1,0:T(8,128)(2,1)S(1)} %select_select_fusion.1), channel_id=1, source_target_pairs={{312,296},{376,360},{440,424},{504,488},{313,297},{377,361},{441,4... | collective-permute-start | bytes 196616 | tf_op jit(solution)/shard_map/ppermute | solution.py:145
  145.7 119.9 %collective-permute-start.15 = (bf16[128,256]{1,0:T(8,128)(2,1)S(1)}, bf16[128,256]{1,0:T(8,128)(2,1)S(1)}, u32[]{:S(2)}, u32[]{:S(2)}) collective-permute-start(bf16[128,256]{1,0:T(8,128)(2,1)S(1)} %select_select_fusion.1), channel_id=1, source_target_pairs={{312,280},{376,344},{440,408},{504,472},{313,281},{377,345},{441,4... | collective-permute-start | bytes 196616 | tf_op jit(solution)/shard_map/ppermute | solution.py:145
  146.4 119.2 %collective-permute-start.16 = (bf16[128,256]{1,0:T(8,128)(2,1)S(1)}, bf16[128,256]{1,0:T(8,128)(2,1)S(1)}, u32[]{:S(2)}, u32[]{:S(2)}) collective-permute-start(bf16[128,256]{1,0:T(8,128)(2,1)S(1)} %select_select_fusion.1), channel_id=1, source_target_pairs={{312,264},{376,328},{440,392},{504,456},{313,265},{377,329},{441,3... | collective-permute-start | bytes 196616 | tf_op jit(solution)/shard_map/ppermute | solution.py:145
  263.6 9.3 %collective-permute-start.1 = (bf16[128,256]{1,0:T(8,128)(2,1)S(1)}, bf16[128,256]{1,0:T(8,128)(2,1)S(1)}, u32[]{:S(2)}, u32[]{:S(2)}) collective-permute-start(bf16[128,256]{1,0:T(8,128)(2,1)S(1)} %add_convert_fusion), channel_id=1, source_target_pairs={{0,8},{8,16},{16,24},{24,32},{32,40},{40,48},{48,56},{56,64},{64,7... | collective-permute-start | bytes 196616 | tf_op jit(solution)/shard_map/ppermute | solution.py:207
  265.6 8.1 %collective-permute-start.17 = (bf16[128,256]{1,0:T(8,128)(2,1)S(1)}, bf16[128,256]{1,0:T(8,128)(2,1)S(1)}, u32[]{:S(2)}, u32[]{:S(2)}) collective-permute-start(bf16[128,256]{1,0:T(8,128)(2,1)S(1)} %select_select_fusion), channel_id=1, source_target_pairs={{264,256},{280,272},{296,288},{312,304},{328,320},{344,336},{360,3... | collective-permute-start | bytes 196616 | tf_op jit(solution)/shard_map/ppermute | solution.py:149
Sparse Core Ops, SparseCore 0:
  11.6 38.7 all-gather.6
Sparse Core Ops, SparseCore 1:
  46.7 35.1 reduce-scatter.4
  119.6 23.8 reduce-scatter.6
  146.4 115.3 all-reduce.2

commit v2 on v1

v2 whole, which is shorter than its diff:
```python
import functools

import jax
import jax.numpy as jnp
from jax import lax
from jax.experimental import pallas as pl
from jax.experimental.pallas import tpu as pltpu
from jax.sharding import Mesh, PartitionSpec as P

TICKS = 2
EPS = 1e-06
PIPE = ("y", "x", "zl")
HEAD = ("zh", "c")
Y, X, ZL, ZH, C = 8, 4, 2, 4, 2
BF, F32 = jnp.bfloat16, jnp.float32


def place(y, x, zl):
    return (y * X + x) * ZL + zl


def norm_into(out, source, scale):
    heads, tokens, width = source.shape
    total = jnp.zeros((tokens, width), F32)
    for h in range(heads):
        wide = source[h].astype(F32)
        total = total + wide * wide
    mean = jnp.sum(total, axis=1, keepdims=True) / (heads * width)
    factor = lax.rsqrt(mean + EPS)
    for h in range(heads):
        wide = source[h].astype(F32)
        out[h] = (wide * factor * scale[:, h * width : (h + 1) * width]).astype(BF)


def project(rows, weight):
    heads, tokens, width = rows.shape
    total = jnp.zeros((tokens, weight.shape[1]), F32)
    for h in range(heads):
        total = total + jnp.dot(
            rows[h], weight[h * width : (h + 1) * width, :], preferred_element_type=F32
        )
    return total.astype(BF)


def attend(query, pair):
    width = query.shape[1]
    scores = lax.dot_general(
        query, pair[:, :width], (((1,), (1,)), ((), ())), preferred_element_type=F32
    )
    scores = scores * width ** (-0.5)
    scores = jnp.exp(scores - jnp.max(scores, axis=-1, keepdims=True))
    probs = (scores / jnp.sum(scores, axis=-1, keepdims=True)).astype(BF)
    return jnp.dot(probs, pair[:, width:], preferred_element_type=F32).astype(BF)


def tick_kernel(tick, half, section, x_hbm, fresh_hbm, gain_hbm, final_hbm, wq_hbm, wkv_hbm, wo_hbm,
                cache_hbm, out_hbm, x, fresh, fresh_rows, gain, final_gain, wq, wkv, wo, pair, normed,
                kv_rows, out, sems):
    heads, tokens, width = x.shape
    here = section[0]
    in_encoder = here < half
    at_half = here == half if tick > 0 else here < 0
    own_pair = jnp.logical_or(in_encoder, at_half)

    def copy(k, source, target):
        return pltpu.make_async_copy(source, target, sems.at[k])

    get_x = copy(0, x_hbm, x)
    get_gain = copy(1, gain_hbm, gain)
    get_wq = copy(2, wq_hbm.at[0], wq)
    get_wkv = copy(3, wkv_hbm.at[0], wkv)
    get_cache = copy(4, cache_hbm.at[0, tick], pair)
    get_wo = copy(5, wo_hbm.at[0], wo)
    get_x.start()
    get_gain.start()
    get_wq.start()
    pl.when(own_pair)(get_wkv.start)
    pl.when(jnp.logical_not(own_pair))(get_cache.start)
    get_wo.start()
    get_x.wait()
    get_gain.wait()
    if tick == 0:
        norm_into(normed, x, gain)
    else:
        get_fresh = copy(6, fresh_hbm.at[:, 1], fresh)
        get_final = copy(7, final_hbm, final_gain)

        @pl.when(at_half)
        def _():
            get_fresh.start()
            get_final.start()
            get_fresh.wait()
            get_final.wait()
            for h in range(heads):
                fresh_rows[h] = fresh[h].T
            norm_into(normed, fresh_rows, gain)
            norm_into(kv_rows, x, final_gain)

        @pl.when(jnp.logical_not(at_half))
        def _():
            norm_into(normed, x, gain)

    get_wq.wait()
    query = project(normed, wq)

    @pl.when(in_encoder)
    def _():
        get_wkv.wait()
        pair[:, :width] = project(normed, wkv.at[0])
        pair[:, width:] = project(normed, wkv.at[1])

    if tick > 0:

        @pl.when(at_half)
        def _():
            get_wkv.wait()
            pair[:, :width] = project(kv_rows, wkv.at[0])
            pair[:, width:] = project(kv_rows, wkv.at[1])

    @pl.when(jnp.logical_not(own_pair))
    def _():
        get_cache.wait()

    attn = attend(query, pair)
    get_wo.wait()
    puts = []
    for h in range(heads):
        out[h] = jnp.dot(
            attn, wo[:, h * width : (h + 1) * width], preferred_element_type=F32
        ).astype(BF)
        puts.append(copy(8 + h, out.at[h], out_hbm.at[h]))
        puts[-1].start()
    for put in puts:
        put.wait()


def memory_kernel(half, section, first_hbm, second_hbm, final_hbm, wkv_hbm, out_hbm, sources, rows,
                  final_gain, wkv, out, sems):
    width = wkv.shape[2]

    def copy(k, source, target):
        return pltpu.make_async_copy(source, target, sems.at[k])

    gets = [
        copy(0, second_hbm, sources.at[1]),
        copy(1, final_hbm, final_gain),
        copy(2, first_hbm.at[:, 0], sources.at[0]),
        copy(3, wkv_hbm.at[0], wkv),
    ]

    @pl.when(section[0] >= half)
    def _():
        for get in gets:
            get.start()
        for get in gets[:3]:
            get.wait()
        for t in range(TICKS):
            norm_into(rows.at[t], sources.at[t], final_gain)
        gets[3].wait()
        for t in range(TICKS):
            out[t, :, :width] = project(rows.at[t], wkv.at[0])
            out[t, :, width:] = project(rows.at[t], wkv.at[1])

    @pl.when(section[0] < half)
    def _():
        out[...] = jnp.zeros_like(out)

    put = copy(4, out, out_hbm.at[0])
    put.start()
    put.wait()


def call(kernel, section, operands, out_shape, scratch, copies, flops):
    return pl.pallas_call(
        kernel,
        out_shape=jax.ShapeDtypeStruct(out_shape, BF),
        in_specs=[pl.BlockSpec(memory_space=pltpu.SMEM)]
        + [pl.BlockSpec(memory_space=pl.ANY)] * len(operands),
        out_specs=pl.BlockSpec(memory_space=pl.ANY),
        scratch_shapes=[pltpu.VMEM(shape, kind) for shape, kind in scratch]
        + [pltpu.SemaphoreType.DMA((copies,))],
        compiler_params=pltpu.CompilerParams(vmem_limit_bytes=40 * 1024 * 1024),
        cost_estimate=pl.CostEstimate(flops=flops, bytes_accessed=5_000_000, transcendentals=0),
    )(section, *operands)


def spread(block, source):
    y, x, zl = lax.axis_index("y"), lax.axis_index("x"), lax.axis_index("zl")
    sy, sx, sz = source // (X * ZL), source // ZL % X, source % ZL
    held = block
    for to in range(sy + 1, Y):
        sent = lax.ppermute(block, PIPE, [(source, place(to, sx, sz))])
        held = jnp.where(y == to, sent, held)
    column = held
    for to in range(X):
        if to != sx:
            pairs = [(place(k, sx, sz), place(k, to, sz)) for k in range(sy + 1, Y)]
            held = jnp.where(x == to, lax.ppermute(column, PIPE, pairs), held)
    pairs = [
        (place(k, to, sz), place(k, to, 1 - sz)) for k in range(sy + 1, Y) for to in range(X)
    ]
    return jnp.where(zl == sz, held, lax.ppermute(held, PIPE, pairs))


def body(stream, fresh, gain, final_gain, w_query, w_kv, w_out, cache_kv, cache_grad):
    pipe_count, heads = Y * X * ZL, ZH * C
    half = pipe_count // 2
    place_here = lax.axis_index(PIPE)
    section = place_here.astype(jnp.int32)[None]
    wkv = w_kv[0]
    depth, width = wkv.shape[1:]
    tokens = stream.shape[2]
    final_scale = final_gain[None]
    rows8 = (heads, tokens, width)
    columns8 = (heads, width, tokens)
    pair_shape = (tokens, 2 * width)
    flops = 2 * tokens * depth * width * 4
    shift = [(i, i + 1) for i in range(pipe_count - 1)]

    def whole(block):
        return lax.all_gather(block, HEAD, axis=0)

    def summed(parts, current):
        parts = lax.all_to_all(parts, HEAD, 0, 0, tiled=True)
        return (current.astype(F32) + jnp.sum(parts.astype(F32), axis=0)).astype(BF)

    def run_tick(tick, gathered):
        return call(
            functools.partial(tick_kernel, tick, half), section,
            (gathered, fresh_whole, gain, final_scale, w_query, w_kv, w_out, cache_kv), rows8,
            ((rows8, BF), (columns8, BF), (rows8, BF), ((1, depth), F32), ((1, depth), F32),
             ((depth, width), BF), ((2, depth, width), BF), ((width, depth), BF),
             (pair_shape, BF), (rows8, BF), (rows8, BF), (rows8, BF)),
            8 + heads, flops,
        )

    fresh_whole = whole(fresh)
    current = stream[0].T
    parts = run_tick(0, whole(current))

    grads, fresh_blocks, parts = lax.optimization_barrier((cache_grad[0], fresh, parts))
    grads = jnp.where(place_here >= half, grads, jnp.zeros_like(grads))
    rows_by = (((1,), (1,)), ((), ()))
    share = lax.dot_general(wkv[0], grads[:, :width], rows_by, preferred_element_type=F32)
    share = share + lax.dot_general(wkv[1], grads[:, width:], rows_by, preferred_element_type=F32)
    share = lax.psum_scatter(share, "y", scatter_dimension=0, tiled=True)
    plane = X * ZL * heads
    share = share.reshape(plane, depth // (pipe_count * heads), tokens)
    fresh_rows = jnp.swapaxes(fresh_blocks, 1, 2)

    output = summed(parts, current)
    passed = lax.ppermute(output, PIPE, shift)
    first_memory = spread(output, half - 1)
    entering = output

    current = jnp.where(place_here == 0, fresh_rows[0], passed)
    parts = run_tick(1, whole(current))
    share, parts = lax.optimization_barrier((share, parts))
    share = lax.all_to_all(share, PIPE[1:] + HEAD, 0, 0, tiled=True)
    memory_grad = jnp.sum(share, axis=0)

    current = jnp.where(place_here == half, fresh_rows[1], current)
    output = summed(parts, current)
    output, first_memory = lax.optimization_barrier((output, first_memory))
    second_memory = spread(output, half - 1)
    first_memory = whole(jnp.stack([first_memory, entering]))
    passed = lax.ppermute(output, PIPE, shift)
    last = jnp.where(place_here == half, jnp.zeros_like(passed), passed)

    new_kv = call(
        functools.partial(memory_kernel, half), section,
        (first_memory, whole(second_memory), final_scale, w_kv),
        (1, TICKS, tokens, 2 * width),
        (((TICKS,) + rows8, BF), ((TICKS,) + rows8, BF), ((1, depth), F32),
         ((2, depth, width), BF), ((TICKS,) + pair_shape, BF)),
        5, flops,
    )
    return (last.T[None], new_kv, memory_grad)


def solution(mesh):
    split = Mesh(mesh.devices.reshape(Y, X, ZL, ZH, C), PIPE + HEAD)
    return jax.shard_map(
        body,
        mesh=split,
        in_specs=(
            P(PIPE, HEAD, None),
            P(None, HEAD, None),
            P(PIPE, None),
            P(),
            P(PIPE, None, HEAD),
            P(PIPE, None, None, HEAD),
            P(PIPE, HEAD, None),
            P(PIPE, None, None, HEAD),
            P(PIPE, None, HEAD),
        ),
        out_specs=(
            P(PIPE, HEAD, None),
            P(PIPE, None, None, HEAD),
            P(PIPE + HEAD, None),
        ),
        check_vma=False,
    )
```

time: 302 us -> 205 us (0.68)
  waiting for transfers between devices: 151 us -> 50.1 us
  Pallas kernels: 4.66 us -> 9.97 us
  starting transfers between devices: 27.1 us -> 30.3 us
    unnamed x5 -> x3, waiting for transfers between devices: 115 us -> 0.71 us
    all_gather x4 -> x3, blocking collectives: 79.2 us -> 55.3 us  [whole(): return lax.all_gather(block, HEAD, axis=0)]
    all_to_all x0 -> x1, blocking collectives: none -> 21.6 us  [summed(): parts = lax.all_to_all(parts, HEAD, 0, 0, tiled=True)]
    all_gather x1 -> x2, waiting for transfers between devices: 0.01 us -> 17.9 us  [whole(): return lax.all_gather(block, HEAD, axis=0)]
    all_to_all x2 -> x1, waiting for transfers between devices: 12.4 us -> 0.01 us  [summed(): parts = lax.all_to_all(parts, HEAD, 0, 0, tiled=True)]
    all_to_all x0 -> x1, starting transfers between devices: none -> 9.98 us  [body(): share = lax.all_to_all(share, PIPE[1:] + HEAD, 0, 0, tiled=True)]
    all_to_all x0 -> x1, waiting for transfers between devices: none -> 8.93 us  [body(): share = lax.all_to_all(share, PIPE[1:] + HEAD, 0, 0, tiled=True)]
    pallas_call x3, Pallas kernels: 4.66 us -> 9.97 us  [call(): pl.pallas_call(kernel, out_shape=jax.ShapeDtypeStruct(out_shape, BF), in_...]
  transfers between devices with their start and end apart: 24 -> 23, of which waited for: 6 -> 5; matrix products, arithmetic and copies ran while one was open for 5% -> 2% of each run, Pallas kernels for 1% -> 2%
where the time goes in v2:
time: 205 us; the launch traced here: 204 us
  blocking collectives  76.9 us (38%)
  waiting for transfers between devices  50.1 us (24%)
  starting transfers between devices  30.3 us (15%)
  local copies, waits for them, and re-layouts  18 us (9%)
  between operations  14.3 us (7%)
  Pallas kernels  9.97 us (5%)
  other arithmetic  2.51 us (1%)
    all_gather x3, blocking collectives, whole(): return lax.all_gather(block, HEAD, axis=0)  55.3 us
    all_to_all x1, blocking collectives, summed(): parts = lax.all_to_all(parts, HEAD, 0, 0, tiled=True)  21.6 us
    all_gather x2, waiting for transfers between devices, whole(): return lax.all_gather(block, HEAD, axis=0)  17.9 us
    unnamed x42, local copies, waits for them, and re-layouts  14.7 us
    ppermute x2, waiting for transfers between devices, body(): passed = lax.ppermute(output, PIPE, shift)  11.3 us
    ppermute x2, waiting for transfers between devices, spread(): return jnp.where(zl == sz, held, lax.ppermute(held, PIPE, pairs))  11.2 us
    all_to_all x1, starting transfers between devices, body(): share = lax.all_to_all(share, PIPE[1:] + HEAD, 0, 0, tiled=True)  9.98 us
    pallas_call x3, Pallas kernels, call(): pl.pallas_call(kernel, out_shape=jax.ShapeDtypeStruct(out_shape, BF), in_...  9.97 us
  transfers between devices with their start and end apart: 23, of which 5 were waited for; matrix products, arithmetic and copies ran while one was open for 2% of the time, Pallas kernels for 2%

profile of v2, /device:TPU:33, one launch (start us, length us, event | category | flops | bytes accessed | tf_op | source)
XLA Modules:
  0.0 204.0 jit_solution(17021108406370087907)
XLA Ops:
  7.2 0.0 all-gather.8.cloned.1.call-start
  7.2 0.7 all-gather.8.cloned.1.call-update
  7.9 0.0 reduce-scatter.2.cloned.1.call-start
  8.0 0.9 copy.21
  8.9 21.3 %all-gather = bf16[1024,256]{1,0:T(8,128)(2,1)S(1)} all-gather(bf16[128,256]{1,0:T(8,128)(2,1)S(1)} %bitcast.47), channel_id=2, replica_groups=mesh['y'=8,'x'=4,'zl'=2,'zh'=4,'c'=2] {'zh','c'}, dimensions={0}, use_global_device_ids=true | all-gather | bytes 589824 | tf_op jit(solution)/shard_map/all_gather | solution.py:221
  30.2 17.9 %all-gather.8.cloned.1.call-done = bf16[16,256,128]{2,1,0:T(8,128)(2,1)} async-done(((bf16[2,256,128]{2,1,0:T(8,128)(2,1)}), bf16[16,256,128]{2,1,0:T(8,128)(2,1)}) %all-gather.8.cloned.1.call-update) | async-done | bytes 1048592 | tf_op jit(solution)/shard_map/all_gather | solution.py:221
  48.0 1.6 copy-done
  49.6 1.2 copy-done.2
  50.9 1.2 copy-done.4
  52.1 1.2 copy-done.6
  53.3 0.9 copy-done.11
  54.3 0.7 copy-done.13
  55.0 0.7 copy-done.15
  55.6 3.6 %shard_map.112 = bf16[8,128,256]{2,1,0:T(8,128)(2,1)S(1)} custom-call(s32[1]{0:T(128)} %bitcast.1.section, bf16[8,128,256]{2,1,0:T(8,128)(2,1)S(1)} %bitcast.41, bf16[8,2,256,128]{3,2,1,0:T(8,128)(2,1)S(1)} %bitcast.38, f32[1,2048]{1,0:T(1,128)S(1)} %copy-done.15, f32[1,2048]{1,0:T(1,128)S(1)} %bitcast.44, bf16[1,2048,256]{2,1,0:T(8,128)(2,1)S(1)} %copy-done.2, ...), custom_call_target="tpu_custom_call" | custom-call | flops 536870912 | bytes 5000000 | tf_op jit(solution)/shard_map/pallas_call | solution.py:174
  59.3 0.5 fusion.2
  59.7 0.3 copy-done.9
  60.0 1.5 fusion
  61.5 0.0 copy-start.16
  61.5 0.0 reduce-scatter.2.cloned.1.call-update
  61.5 21.6 %all_to_all.15 = bf16[8,128,256]{2,1,0:T(8,128)(2,1)S(1)} all-to-all(bf16[8,128,256]{2,1,0:T(8,128)(2,1)} %copy-done.9), channel_id=1, replica_groups=mesh['y'=8,'x'=4,'zl'=2,'zh'=4,'c'=2] {'zh','c'}, dimensions={0} | all-to-all | bytes 1048576 | tf_op jit(solution)/shard_map/all_to_all | solution.py:224
  83.2 0.1 convert_reduce_fusion.1
  83.2 1.9 collective-permute-start
  85.2 1.7 copy.22
  86.9 5.7 %collective-permute-done = bf16[128,256]{1,0:T(8,128)(2,1)S(1)} collective-permute-done((bf16[128,256]{1,0:T(8,128)(2,1)S(1)}, bf16[128,256]{1,0:T(8,128)(2,1)S(1)}, u32[]{:S(2)}, u32[]{:S(2)}) %collective-permute-start) | collective-permute-done | bytes 65568 | tf_op jit(solution)/shard_map/ppermute | solution.py:252
  92.6 0.6 copy-done.19
  93.2 0.9 fusion.8
  94.1 17.4 %all-gather.2 = bf16[1024,256]{1,0:T(8,128)(2,1)S(1)} all-gather(bf16[128,256]{1,0:T(8,128)(2,1)S(1)} %fusion.8), channel_id=4, replica_groups=mesh['y'=8,'x'=4,'zl'=2,'zh'=4,'c'=2] {'zh','c'}, dimensions={0}, use_global_device_ids=true | all-gather | bytes 589824 | tf_op jit(solution)/shard_map/all_gather | solution.py:221
  111.6 0.0 copy-start.5
  111.6 1.2 copy-done.5
  112.8 1.2 copy-done.7
  114.0 4.3 %shard_map.113 = bf16[8,128,256]{2,1,0:T(8,128)(2,1)S(1)} custom-call(s32[1]{0:T(128)} %bitcast.1.section, bf16[8,128,256]{2,1,0:T(8,128)(2,1)S(1)} %bitcast.42, bf16[8,2,256,128]{3,2,1,0:T(8,128)(2,1)S(1)} %bitcast.39, f32[1,2048]{1,0:T(1,128)S(1)} %copy-done.16, f32[1,2048]{1,0:T(1,128)S(1)} %bitcast.45, bf16[1,2048,256]{2,1,0:T(8,128)(2,1)S(1)} %copy-done.3, ...), custom_call_target="tpu_custom_call" | custom-call | flops 536870912 | bytes 5000000 | tf_op jit(solution)/shard_map/pallas_call | solution.py:174
  118.3 0.8 copy-done.8
  119.1 1.7 copy.23
  120.8 4.0 %all-to-all-start.1 = ((bf16[8,128,256]{2,1,0:T(8,128)(2,1)}), bf16[8,128,256]{2,1,0:T(8,128)(2,1)S(1)}, u32[]{:S(2)}, u32[]{:S(2)}) async-start(bf16[8,128,256]{2,1,0:T(8,128)(2,1)} %copy-done.8), calls=%async_computation.2 | async-start | bytes 1048576 | tf_op jit(solution)/shard_map/all_to_all | solution.py:224
  124.8 0.7 collective-permute-start.1
  125.5 0.7 collective-permute-start.2
  126.2 0.7 collective-permute-start.3
  126.8 0.7 collective-permute-start.4
  127.5 0.0 collective-permute-done.1
  127.6 0.7 collective-permute-start.5
  128.3 0.7 collective-permute-start.6
  128.9 0.7 collective-permute-start.7
  129.7 1.3 collective-permute-start.8
  131.0 11.2 %collective-permute-done.8 = bf16[128,256]{1,0:T(8,128)(2,1)S(1)} collective-permute-done((bf16[128,256]{1,0:T(8,128)(2,1)S(1)}, bf16[128,256]{1,0:T(8,128)(2,1)S(1)}, u32[]{:S(2)}, u32[]{:S(2)}) %collective-permute-start.8) | collective-permute-done | bytes 65568 | tf_op jit(solution)/shard_map/ppermute | solution.py:202
  142.2 0.1 convert_reduce_fusion
  142.3 0.7 pad_maximum_fusion
  143.0 0.0 all-gather.10.cloned.1.call-update
  143.0 0.7 collective-permute-start.10
  143.7 0.7 collective-permute-start.11
  144.4 0.7 collective-permute-start.12
  145.1 0.7 collective-permute-start.13
  145.7 10.0 %all-to-all-start.2 = ((f32[64,4,128]{2,1,0:T(4,128)}), f32[64,4,128]{2,1,0:T(4,128)S(1)}, u32[]{:S(2)}, u32[]{:S(2)}) async-start(f32[64,4,128]{2,1,0:T(4,128)} %bitcast.14), calls=%async_computation.3 | async-start | bytes 262144 | tf_op jit(solution)/shard_map/all_to_all | solution.py:259
  155.8 0.7 collective-permute-start.14
  156.5 0.7 collective-permute-start.15
  157.1 0.7 collective-permute-start.16
  157.8 8.9 %all-to-all-done.2 = f32[64,4,128]{2,1,0:T(4,128)S(1)} async-done(((f32[64,4,128]{2,1,0:T(4,128)}), f32[64,4,128]{2,1,0:T(4,128)S(1)}, u32[]{:S(2)}, u32[]{:S(2)}) %all-to-all-start.2) | async-done | bytes 131104 | tf_op jit(solution)/shard_map/all_to_all | solution.py:259
  166.7 0.7 reduce_sum.29
  167.4 2.4 %collective-permute-start.9 = (bf16[128,256]{1,0:T(8,128)(2,1)S(1)}, bf16[128,256]{1,0:T(8,128)(2,1)S(1)}, u32[]{:S(2)}, u32[]{:S(2)}) collective-permute-start(bf16[128,256]{1,0:T(8,128)(2,1)S(1)} %add_convert_fusion), channel_id=1, source_target_pairs={{0,8},{8,16},{16,24},{24,32},{32,40},{40,48},{48,56},{56,64},{64,7... | collective-permute-start | bytes 196616 | tf_op jit(solution)/shard_map/ppermute | solution.py:267
  169.9 1.3 collective-permute-start.17
  171.2 5.6 %collective-permute-done.9 = bf16[128,256]{1,0:T(8,128)(2,1)S(1)} collective-permute-done((bf16[128,256]{1,0:T(8,128)(2,1)S(1)}, bf16[128,256]{1,0:T(8,128)(2,1)S(1)}, u32[]{:S(2)}, u32[]{:S(2)}) %collective-permute-start.9) | collective-permute-done | bytes 65568 | tf_op jit(solution)/shard_map/ppermute | solution.py:267
  176.8 0.7 copy.24
  177.5 16.6 %all-gather.4 = bf16[1024,256]{1,0:T(8,128)(2,1)S(1)} all-gather(bf16[128,256]{1,0:T(8,128)(2,1)S(1)} %broadcast_select_fusion.1), channel_id=6, replica_groups=mesh['y'=8,'x'=4,'zl'=2,'zh'=4,'c'=2] {'zh','c'}, dimensions={0}, use_global_device_ids=true | all-gather | bytes 589824 | tf_op jit(solution)/shard_map/all_gather | solution.py:221
  194.1 1.2 copy-done.10
  195.4 2.1 %shard_map.114 = bf16[1,2,128,512]{3,2,1,0:T(8,128)(2,1)} custom-call(s32[1]{0:T(128)} %bitcast.1.section, bf16[8,2,128,256]{3,2,1,0:T(8,128)(2,1)S(1)} %bitcast.43, bf16[8,128,256]{2,1,0:T(8,128)(2,1)S(1)} %bitcast.40, f32[1,2048]{1,0:T(1,128)S(1)} %bitcast.46, bf16[1,2,2048,256]{3,2,1,0:T(8,128)(2,1)S(1)} %copy-done.1), custom_call_target="tpu_custom_call" | custom-call | flops 536870912 | bytes 5000000 | tf_op jit(solution)/shard_map/pallas_call | solution.py:174
  (53 shorter events, 0.3 us)
Async XLA Ops:
  7.2 40.9 %all-gather.8.cloned.1.call-start = ((), (), s32[]{:S(2)}) async-start(), calls=%async_computation.5 | async-start | bytes 1179648 | tf_op jit(solution)/shard_map/all_gather | solution.py:221
  7.9 111.2 %reduce-scatter.2.cloned.1.call-start = ((), (), s32[]{:S(2)}) async-start(), calls=%async_computation.4 | async-start | bytes 1179648 | tf_op jit(solution)/shard_map/reduce_scatter | solution.py:246
  48.0 1.6 copy-start
  49.6 1.2 copy-start.2
  50.9 1.2 copy-start.4
  52.1 1.2 copy-start.6
  53.3 0.9 copy-start.11
  54.3 0.7 copy-start.13
  54.9 0.7 copy-start.15
  55.6 3.6 %copy-start.18 = (bf16[1,128,512]{2,1,0:T(8,128)(2,1)S(1)}, bf16[1,128,512]{2,1,0:T(8,128)(2,1)}, u32[]{:S(2)}) copy-start(bf16[1,128,512]{2,1,0:T(8,128)(2,1)} %param.17) | copy-start | bytes 393220
  59.2 0.8 copy-start.9
  61.5 50.1 %copy-start.1 = (bf16[1,2,2048,256]{3,2,1,0:T(8,128)(2,1)S(1)}, bf16[1,2,2048,256]{3,2,1,0:T(8,128)(2,1)}, u32[]{:S(2)}) copy-start(bf16[1,2,2048,256]{3,2,1,0:T(8,128)(2,1)} %wkv_hbm.5) | copy-start | bytes 6291460
  61.5 50.1 %copy-start.3 = (bf16[1,2048,256]{2,1,0:T(8,128)(2,1)S(1)}, bf16[1,2048,256]{2,1,0:T(8,128)(2,1)}, u32[]{:S(2)}) copy-start(bf16[1,2048,256]{2,1,0:T(8,128)(2,1)} %wq_hbm.3) | copy-start | bytes 3145732
  61.5 50.1 %copy-start.12 = (bf16[1,2,128,512]{3,2,1,0:T(8,128)(2,1)S(1)}, bf16[1,2,128,512]{3,2,1,0:T(8,128)(2,1)}, u32[]{:S(2)}) copy-start(bf16[1,2,128,512]{3,2,1,0:T(8,128)(2,1)} %cache_hbm.3) | copy-start | bytes 786436
  61.5 50.1 %copy-start.14 = (f32[2048]{0:T(1024)S(1)}, f32[2048]{0:T(1024)}, u32[]{:S(2)}) copy-start(f32[2048]{0:T(1024)} %param.12) | copy-start | bytes 24580
  61.5 50.1 %copy-start.16 = (f32[1,2048]{1,0:T(1,128)S(1)}, f32[1,2048]{1,0:T(1,128)}, u32[]{:S(2)}) copy-start(f32[1,2048]{1,0:T(1,128)} %gain_hbm.3) | copy-start | bytes 24580
  83.2 9.3 %collective-permute-start = (bf16[128,256]{1,0:T(8,128)(2,1)S(1)}, bf16[128,256]{1,0:T(8,128)(2,1)S(1)}, u32[]{:S(2)}, u32[]{:S(2)}) collective-permute-start(bf16[128,256]{1,0:T(8,128)(2,1)S(1)} %add_convert_fusion.1), channel_id=1, source_target_pairs={{0,8},{8,16},{16,24},{24,32},{32,40},{40,48},{48,56},{56,64},{64,7... | collective-permute-start | bytes 196616 | tf_op jit(solution)/shard_map/ppermute | solution.py:252
  92.6 0.6 copy-start.19
  111.6 1.2 copy-start.5
  112.8 1.2 copy-start.7
  118.3 0.8 copy-start.8
  119.1 23.2 %copy-start.17 = (bf16[2,256,128]{1,2,0:T(8,128)(2,1)S(1)}, bf16[2,256,128]{1,2,0:T(8,128)(2,1)}, u32[]{:S(2)}) copy-start(bf16[2,256,128]{1,2,0:T(8,128)(2,1)} %copy.22) | copy-start | bytes 393220
  120.8 21.4 %all-to-all-start.1 = ((bf16[8,128,256]{2,1,0:T(8,128)(2,1)}), bf16[8,128,256]{2,1,0:T(8,128)(2,1)S(1)}, u32[]{:S(2)}, u32[]{:S(2)}) async-start(bf16[8,128,256]{2,1,0:T(8,128)(2,1)} %copy-done.8), calls=%async_computation.2 | async-start | bytes 1048576 | tf_op jit(solution)/shard_map/all_to_all | solution.py:224
  124.8 69.3 %all-gather.10.cloned.1.call-start = ((), (), s32[]{:S(2)}) async-start(), calls=%async_computation.6 | async-start | bytes 1179648 | tf_op jit(solution)/shard_map/all_gather | solution.py:221
  124.8 2.7 %collective-permute-start.1 = (bf16[128,256]{1,0:T(8,128)(2,1)S(1)}, bf16[128,256]{1,0:T(8,128)(2,1)S(1)}, u32[]{:S(2)}, u32[]{:S(2)}) collective-permute-start(bf16[128,256]{1,0:T(8,128)(2,1)S(1)} %add_convert_fusion.1), channel_id=1, source_target_pairs={{248,504},{249,505},{250,506},{251,507},{252,508},{253,509},{254,5... | collective-permute-start | bytes 196616 | tf_op jit(solution)/shard_map/ppermute | solution.py:192
  125.5 2.0 %collective-permute-start.2 = (bf16[128,256]{1,0:T(8,128)(2,1)S(1)}, bf16[128,256]{1,0:T(8,128)(2,1)S(1)}, u32[]{:S(2)}, u32[]{:S(2)}) collective-permute-start(bf16[128,256]{1,0:T(8,128)(2,1)S(1)} %add_convert_fusion.1), channel_id=1, source_target_pairs={{248,440},{249,441},{250,442},{251,443},{252,444},{253,445},{254,4... | collective-permute-start | bytes 196616 | tf_op jit(solution)/shard_map/ppermute | solution.py:192
  126.2 1.4 collective-permute-start.3
  126.8 0.7 collective-permute-start.4
  127.6 2.0 collective-permute-start.5
  128.3 1.4 collective-permute-start.6
  128.9 0.7 collective-permute-start.7
  129.7 12.5 %collective-permute-start.8 = (bf16[128,256]{1,0:T(8,128)(2,1)S(1)}, bf16[128,256]{1,0:T(8,128)(2,1)S(1)}, u32[]{:S(2)}, u32[]{:S(2)}) collective-permute-start(bf16[128,256]{1,0:T(8,128)(2,1)S(1)} %select_select_fusion.2), channel_id=1, source_target_pairs={{264,256},{280,272},{296,288},{312,304},{328,320},{344,336},{360,3... | collective-permute-start | bytes 196616 | tf_op jit(solution)/shard_map/ppermute | solution.py:202
  143.0 12.7 %collective-permute-start.10 = (bf16[128,256]{1,0:T(8,128)(2,1)S(1)}, bf16[128,256]{1,0:T(8,128)(2,1)S(1)}, u32[]{:S(2)}, u32[]{:S(2)}) collective-permute-start(bf16[128,256]{1,0:T(8,128)(2,1)S(1)} %add_convert_fusion), channel_id=1, source_target_pairs={{248,504},{249,505},{250,506},{251,507},{252,508},{253,509},{254,5... | collective-permute-start | bytes 196616 | tf_op jit(solution)/shard_map/ppermute | solution.py:192
  143.7 12.0 %collective-permute-start.11 = (bf16[128,256]{1,0:T(8,128)(2,1)S(1)}, bf16[128,256]{1,0:T(8,128)(2,1)S(1)}, u32[]{:S(2)}, u32[]{:S(2)}) collective-permute-start(bf16[128,256]{1,0:T(8,128)(2,1)S(1)} %add_convert_fusion), channel_id=1, source_target_pairs={{248,440},{249,441},{250,442},{251,443},{252,444},{253,445},{254,4... | collective-permute-start | bytes 196616 | tf_op jit(solution)/shard_map/ppermute | solution.py:192
  144.4 11.4 %collective-permute-start.12 = (bf16[128,256]{1,0:T(8,128)(2,1)S(1)}, bf16[128,256]{1,0:T(8,128)(2,1)S(1)}, u32[]{:S(2)}, u32[]{:S(2)}) collective-permute-start(bf16[128,256]{1,0:T(8,128)(2,1)S(1)} %add_convert_fusion), channel_id=1, source_target_pairs={{248,376},{249,377},{250,378},{251,379},{252,380},{253,381},{254,3... | collective-permute-start | bytes 196616 | tf_op jit(solution)/shard_map/ppermute | solution.py:192
  145.1 10.7 %collective-permute-start.13 = (bf16[128,256]{1,0:T(8,128)(2,1)S(1)}, bf16[128,256]{1,0:T(8,128)(2,1)S(1)}, u32[]{:S(2)}, u32[]{:S(2)}) collective-permute-start(bf16[128,256]{1,0:T(8,128)(2,1)S(1)} %add_convert_fusion), channel_id=1, source_target_pairs={{248,312},{249,313},{250,314},{251,315},{252,316},{253,317},{254,3... | collective-permute-start | bytes 196616 | tf_op jit(solution)/shard_map/ppermute | solution.py:192
  145.7 21.0 %all-to-all-start.2 = ((f32[64,4,128]{2,1,0:T(4,128)}), f32[64,4,128]{2,1,0:T(4,128)S(1)}, u32[]{:S(2)}, u32[]{:S(2)}) async-start(f32[64,4,128]{2,1,0:T(4,128)} %bitcast.14), calls=%async_computation.3 | async-start | bytes 262144 | tf_op jit(solution)/shard_map/all_to_all | solution.py:259
  155.8 14.0 %collective-permute-start.14 = (bf16[128,256]{1,0:T(8,128)(2,1)S(1)}, bf16[128,256]{1,0:T(8,128)(2,1)S(1)}, u32[]{:S(2)}, u32[]{:S(2)}) collective-permute-start(bf16[128,256]{1,0:T(8,128)(2,1)S(1)} %select_select_fusion.1), channel_id=1, source_target_pairs={{312,296},{376,360},{440,424},{504,488},{313,297},{377,361},{441,4... | collective-permute-start | bytes 196616 | tf_op jit(solution)/shard_map/ppermute | solution.py:198
  156.5 13.4 %collective-permute-start.15 = (bf16[128,256]{1,0:T(8,128)(2,1)S(1)}, bf16[128,256]{1,0:T(8,128)(2,1)S(1)}, u32[]{:S(2)}, u32[]{:S(2)}) collective-permute-start(bf16[128,256]{1,0:T(8,128)(2,1)S(1)} %select_select_fusion.1), channel_id=1, source_target_pairs={{312,280},{376,344},{440,408},{504,472},{313,281},{377,345},{441,4... | collective-permute-start | bytes 196616 | tf_op jit(solution)/shard_map/ppermute | solution.py:198
  157.1 12.7 %collective-permute-start.16 = (bf16[128,256]{1,0:T(8,128)(2,1)S(1)}, bf16[128,256]{1,0:T(8,128)(2,1)S(1)}, u32[]{:S(2)}, u32[]{:S(2)}) collective-permute-start(bf16[128,256]{1,0:T(8,128)(2,1)S(1)} %select_select_fusion.1), channel_id=1, source_target_pairs={{312,264},{376,328},{440,392},{504,456},{313,265},{377,329},{441,3... | collective-permute-start | bytes 196616 | tf_op jit(solution)/shard_map/ppermute | solution.py:198
  167.4 9.4 %collective-permute-start.9 = (bf16[128,256]{1,0:T(8,128)(2,1)S(1)}, bf16[128,256]{1,0:T(8,128)(2,1)S(1)}, u32[]{:S(2)}, u32[]{:S(2)}) collective-permute-start(bf16[128,256]{1,0:T(8,128)(2,1)S(1)} %add_convert_fusion), channel_id=1, source_target_pairs={{0,8},{8,16},{16,24},{24,32},{32,40},{40,48},{48,56},{56,64},{64,7... | collective-permute-start | bytes 196616 | tf_op jit(solution)/shard_map/ppermute | solution.py:267
  169.9 7.7 %collective-permute-start.17 = (bf16[128,256]{1,0:T(8,128)(2,1)S(1)}, bf16[128,256]{1,0:T(8,128)(2,1)S(1)}, u32[]{:S(2)}, u32[]{:S(2)}) collective-permute-start(bf16[128,256]{1,0:T(8,128)(2,1)S(1)} %select_select_fusion), channel_id=1, source_target_pairs={{264,256},{280,272},{296,288},{312,304},{328,320},{344,336},{360,3... | collective-permute-start | bytes 196616 | tf_op jit(solution)/shard_map/ppermute | solution.py:202
  194.1 1.2 copy-start.10
Sparse Core Ops, SparseCore 0:
  10.2 37.8 all-gather.7
  61.7 32.9 reduce-scatter.1
  143.2 34.3 all-gather.9

commit v3 on v2

--- a/solution.py
+++ b/solution.py
@@ -54,8 +54,8 @@
 
 
 def tick_kernel(tick, half, section, x_hbm, fresh_hbm, gain_hbm, final_hbm, wq_hbm, wkv_hbm, wo_hbm,
-                cache_hbm, out_hbm, x, fresh, fresh_rows, gain, final_gain, wq, wkv, wo, pair, normed,
-                kv_rows, out, sems):
+                cache_hbm, out_hbm, turned_hbm, x, fresh, turned, gain, final_gain, wq, wkv, wo, pair,
+                normed, kv_rows, out, sems):
     heads, tokens, width = x.shape
     here = section[0]
     in_encoder = here < half
@@ -77,10 +77,18 @@
     pl.when(own_pair)(get_wkv.start)
     pl.when(jnp.logical_not(own_pair))(get_cache.start)
     get_wo.start()
+    if tick == 0:
+        get_fresh = copy(6, fresh_hbm, fresh)
+        get_fresh.start()
     get_x.wait()
     get_gain.wait()
     if tick == 0:
         norm_into(normed, x, gain)
+        get_fresh.wait()
+        for h in range(fresh.shape[0]):
+            turned[h] = fresh[h].T
+        put_turned = copy(7, turned, turned_hbm)
+        put_turned.start()
     else:
         get_fresh = copy(6, fresh_hbm.at[:, 1], fresh)
         get_final = copy(7, final_hbm, final_gain)
@@ -92,8 +100,8 @@
             get_fresh.wait()
             get_final.wait()
             for h in range(heads):
-                fresh_rows[h] = fresh[h].T
-            norm_into(normed, fresh_rows, gain)
+                turned[h] = fresh[h].T
+            norm_into(normed, turned, gain)
             norm_into(kv_rows, x, final_gain)
 
         @pl.when(jnp.logical_not(at_half))
@@ -130,8 +138,19 @@
         ).astype(BF)
         puts.append(copy(8 + h, out.at[h], out_hbm.at[h]))
         puts[-1].start()
+    if tick == 0:
+        put_turned.wait()
     for put in puts:
         put.wait()
+
+
+def first_kernel(half, section, x, fresh, gain, wq, wkv, wo, cache, out, turned, *scratch):
+    scratch = scratch[:4] + (None,) + scratch[4:9] + (None,) + scratch[9:]
+    tick_kernel(0, half, section, x, fresh, gain, None, wq, wkv, wo, cache, out, turned, *scratch)
+
+
+def second_kernel(half, section, x, fresh, gain, final, wq, wkv, wo, cache, out, *scratch):
+    tick_kernel(1, half, section, x, fresh, gain, final, wq, wkv, wo, cache, out, None, *scratch)
 
 
 def memory_kernel(half, section, first_hbm, second_hbm, final_hbm, wkv_hbm, out_hbm, sources, rows,
@@ -170,16 +189,16 @@
     put.wait()
 
 
-def call(kernel, section, operands, out_shape, scratch, copies, flops):
+def call(kernel, section, operands, out_shapes, scratch, copies, flops):
     return pl.pallas_call(
         kernel,
-        out_shape=jax.ShapeDtypeStruct(out_shape, BF),
+        out_shape=[jax.ShapeDtypeStruct(shape, BF) for shape in out_shapes],
         in_specs=[pl.BlockSpec(memory_space=pltpu.SMEM)]
         + [pl.BlockSpec(memory_space=pl.ANY)] * len(operands),
-        out_specs=pl.BlockSpec(memory_space=pl.ANY),
+        out_specs=[pl.BlockSpec(memory_space=pl.ANY)] * len(out_shapes),
         scratch_shapes=[pltpu.VMEM(shape, kind) for shape, kind in scratch]
         + [pltpu.SemaphoreType.DMA((copies,))],
-        compiler_params=pltpu.CompilerParams(vmem_limit_bytes=40 * 1024 * 1024),
+        compiler_params=pltpu.CompilerParams(vmem_limit_bytes=60 * 1024 * 1024),
         cost_estimate=pl.CostEstimate(flops=flops, bytes_accessed=5_000_000, transcendentals=0),
     )(section, *operands)
 
@@ -220,43 +239,49 @@
     def whole(block):
         return lax.all_gather(block, HEAD, axis=0)
 
+    def exchanged(parts):
+        return lax.all_to_all(parts, HEAD, 0, 0, tiled=True)
+
     def summed(parts, current):
-        parts = lax.all_to_all(parts, HEAD, 0, 0, tiled=True)
         return (current.astype(F32) + jnp.sum(parts.astype(F32), axis=0)).astype(BF)
 
-    def run_tick(tick, gathered):
-        return call(
-            functools.partial(tick_kernel, tick, half), section,
-            (gathered, fresh_whole, gain, final_scale, w_query, w_kv, w_out, cache_kv), rows8,
-            ((rows8, BF), (columns8, BF), (rows8, BF), ((1, depth), F32), ((1, depth), F32),
-             ((depth, width), BF), ((2, depth, width), BF), ((width, depth), BF),
-             (pair_shape, BF), (rows8, BF), (rows8, BF), (rows8, BF)),
-            8 + heads, flops,
-        )
-
+    weights = (((depth, width), BF), ((2, depth, width), BF), ((width, depth), BF))
     fresh_whole = whole(fresh)
     current = stream[0].T
-    parts = run_tick(0, whole(current))
-
-    grads, fresh_blocks, parts = lax.optimization_barrier((cache_grad[0], fresh, parts))
-    grads = jnp.where(place_here >= half, grads, jnp.zeros_like(grads))
+    parts, fresh_rows = call(
+        functools.partial(first_kernel, half), section,
+        (whole(current), fresh, gain, w_query, w_kv, w_out, cache_kv),
+        (rows8, (2, tokens, width)),
+        ((rows8, BF), ((2, width, tokens), BF), ((2, tokens, width), BF), ((1, depth), F32))
+        + weights + ((pair_shape, BF), (rows8, BF), (rows8, BF)),
+        8 + heads, flops,
+    )
+
+    grads = jnp.where(place_here >= half, cache_grad[0], jnp.zeros_like(cache_grad[0]))
     rows_by = (((1,), (1,)), ((), ()))
     share = lax.dot_general(wkv[0], grads[:, :width], rows_by, preferred_element_type=F32)
     share = share + lax.dot_general(wkv[1], grads[:, width:], rows_by, preferred_element_type=F32)
     share = lax.psum_scatter(share, "y", scatter_dimension=0, tiled=True)
     plane = X * ZL * heads
     share = share.reshape(plane, depth // (pipe_count * heads), tokens)
-    fresh_rows = jnp.swapaxes(fresh_blocks, 1, 2)
-
-    output = summed(parts, current)
+
+    output = summed(exchanged(parts), current)
     passed = lax.ppermute(output, PIPE, shift)
     first_memory = spread(output, half - 1)
     entering = output
 
     current = jnp.where(place_here == 0, fresh_rows[0], passed)
-    parts = run_tick(1, whole(current))
+    (parts,) = call(
+        functools.partial(second_kernel, half), section,
+        (whole(current), fresh_whole, gain, final_scale, w_query, w_kv, w_out, cache_kv),
+        (rows8,),
+        ((rows8, BF), (columns8, BF), (rows8, BF), ((1, depth), F32), ((1, depth), F32))
+        + weights + ((pair_shape, BF), (rows8, BF), (rows8, BF), (rows8, BF)),
+        8 + heads, flops,
+    )
     share, parts = lax.optimization_barrier((share, parts))
     share = lax.all_to_all(share, PIPE[1:] + HEAD, 0, 0, tiled=True)
+    share, parts = lax.optimization_barrier((share, exchanged(parts)))
     memory_grad = jnp.sum(share, axis=0)
 
     current = jnp.where(place_here == half, fresh_rows[1], current)
@@ -267,10 +292,10 @@
     passed = lax.ppermute(output, PIPE, shift)
     last = jnp.where(place_here == half, jnp.zeros_like(passed), passed)
 
-    new_kv = call(
+    (new_kv,) = call(
         functools.partial(memory_kernel, half), section,
         (first_memory, whole(second_memory), final_scale, w_kv),
-        (1, TICKS, tokens, 2 * width),
+        ((1, TICKS, tokens, 2 * width),),
         (((TICKS,) + rows8, BF), ((TICKS,) + rows8, BF), ((1, depth), F32),
          ((2, depth, width), BF), ((TICKS,) + pair_shape, BF)),
         5, flops,

time: 205 us -> 190 us (0.927)
  the two profiles are of different devices: /device:TPU:33 before, /device:TPU:35 now
where the time goes in v3:
time: 190 us; the launch traced here: 189 us
  blocking collectives  111 us (58%)
  starting transfers between devices  21.9 us (12%)
  waiting for transfers between devices  20.7 us (11%)
  between operations  15.9 us (8%)
  Pallas kernels  10.5 us (6%)
  other arithmetic  3.39 us (2%)
  matrix products  3.15 us (2%)
    all_gather x3, blocking collectives, whole(): return lax.all_gather(block, HEAD, axis=0)  70.7 us
    all_to_all x1, blocking collectives, exchanged(): return lax.all_to_all(parts, HEAD, 0, 0, tiled=True)  21 us
    all_to_all x1, blocking collectives, body(): share = lax.all_to_all(share, PIPE[1:] + HEAD, 0, 0, tiled=True)  19.8 us
    ppermute x2, waiting for transfers between devices, spread(): return jnp.where(zl == sz, held, lax.ppermute(held, PIPE, pairs))  16.2 us
    pallas_call x3, Pallas kernels, call(): pl.pallas_call(kernel, out_shape=[jax.ShapeDtypeStruct(shape, BF) for sha...  10.5 us
    ppermute x2, starting transfers between devices, body(): passed = lax.ppermute(output, PIPE, shift)  6.17 us
    ppermute x8, starting transfers between devices, spread(): sent = lax.ppermute(block, PIPE, [(source, place(to, sx, sz))])  5.31 us
    ppermute x6, starting transfers between devices, spread(): held = jnp.where(x == to, lax.ppermute(column, PIPE, pairs), held)  3.99 us
  transfers between devices with their start and end apart: 22, of which 4 were waited for; matrix products, arithmetic and copies ran while one was open for 3% of the time, Pallas kernels for 4%

profile of v3, /device:TPU:35, one launch (start us, length us, event | category | flops | bytes accessed | tf_op | source)
XLA Modules:
  0.0 188.9 jit_solution(5374963252195799488)
XLA Ops:
  8.0 0.0 copy-start
  8.0 0.0 all-gather.8.cloned.1.call-start
  8.1 0.7 all-gather.8.cloned.1.call-update
  8.7 0.0 reduce-scatter.2.cloned.1.call-start
  8.8 0.9 select_bitcast_fusion
  9.7 1.7 fusion.2
  11.4 0.0 copy-start.2
  11.5 1.5 fusion
  12.9 0.0 reduce-scatter.2.cloned.1.call-update
  12.9 0.1 copy.17
  13.1 22.2 %all-gather = bf16[1024,256]{1,0:T(8,128)(2,1)} all-gather(bf16[128,256]{1,0:T(8,128)(2,1)S(1)} %bitcast.39), channel_id=2, replica_groups=mesh['y'=8,'x'=4,'zl'=2,'zh'=4,'c'=2] {'zh','c'}, dimensions={0}, use_global_device_ids=true | all-gather | bytes 589824 | tf_op jit(solution)/shard_map/all_gather | solution.py:240
  35.2 3.8 %shard_map.112 = (bf16[8,128,256]{2,1,0:T(8,128)(2,1)}, bf16[2,128,256]{2,1,0:T(8,128)(2,1)}) custom-call(s32[1]{0:T(128)} %bitcast.section, bf16[8,128,256]{2,1,0:T(8,128)(2,1)} %bitcast.36, bf16[2,256,128]{2,1,0:T(8,128)(2,1)} %fresh.1, f32[1,2048]{1,0:T(1,128)} %gain.3, bf16[1,2048,256]{2,1,0:T(8,128)(2,1)} %wq.3, bf16[1,2,2048,256]{3,2,1,0:T(8,128)(2,1)} %wkv_hbm.1, ...), custom_call_target="tpu_custom_call" | custom-call | flops 536870912 | bytes 5000000 | tf_op jit(solution)/shard_map/pallas_call | solution.py:193
  39.0 21.0 %all_to_all.15 = bf16[8,128,256]{2,1,0:T(8,128)(2,1)S(1)} all-to-all(bf16[8,128,256]{2,1,0:T(8,128)(2,1)} %get-tuple-element.12), channel_id=1, replica_groups=mesh['y'=8,'x'=4,'zl'=2,'zh'=4,'c'=2] {'zh','c'}, dimensions={0} | all-to-all | bytes 1048576 | tf_op jit(solution)/shard_map/all_to_all | solution.py:243
  60.1 0.1 convert_reduce_fusion.1
  60.2 4.0 %collective-permute-start = (bf16[128,256]{1,0:T(8,128)(2,1)S(1)}, bf16[128,256]{1,0:T(8,128)(2,1)S(1)}, u32[]{:S(2)}, u32[]{:S(2)}) collective-permute-start(bf16[128,256]{1,0:T(8,128)(2,1)S(1)} %add_convert_fusion.1), channel_id=1, source_target_pairs={{0,8},{8,16},{16,24},{24,32},{32,40},{40,48},{48,56},{56,64},{64,7... | collective-permute-start | bytes 196616 | tf_op jit(solution)/shard_map/ppermute | solution.py:269
  64.1 1.9 %collective-permute-done = bf16[128,256]{1,0:T(8,128)(2,1)S(1)} collective-permute-done((bf16[128,256]{1,0:T(8,128)(2,1)S(1)}, bf16[128,256]{1,0:T(8,128)(2,1)S(1)}, u32[]{:S(2)}, u32[]{:S(2)}) %collective-permute-start) | collective-permute-done | bytes 65568 | tf_op jit(solution)/shard_map/ppermute | solution.py:269
  66.1 0.8 bitcast_select_fusion
  66.9 20.7 %all-gather.1 = bf16[1024,256]{1,0:T(8,128)(2,1)} all-gather(bf16[128,256]{1,0:T(8,128)(2,1)S(1)} %bitcast_select_fusion), channel_id=3, replica_groups=mesh['y'=8,'x'=4,'zl'=2,'zh'=4,'c'=2] {'zh','c'}, dimensions={0}, use_global_device_ids=true | all-gather | bytes 589824 | tf_op jit(solution)/shard_map/all_gather | solution.py:240
  87.7 3.3 %shard_map.113 = bf16[8,128,256]{2,1,0:T(8,128)(2,1)} custom-call(s32[1]{0:T(128)} %bitcast.section, bf16[8,128,256]{2,1,0:T(8,128)(2,1)} %bitcast.35, bf16[8,2,256,128]{3,2,1,0:T(8,128)(2,1)} %bitcast.38, f32[1,2048]{1,0:T(1,128)} %gain.3, f32[1,2048]{1,0:T(1,128)} %bitcast.43, bf16[1,2048,256]{2,1,0:T(8,128)(2,1)} %wq.3, ...), custom_call_target="tpu_custom_call" | custom-call | flops 536870912 | bytes 5000000 | tf_op jit(solution)/shard_map/pallas_call | solution.py:193
  91.0 0.0 copy-start.1
  91.0 0.0 reduce-scatter.2.cloned.1.call-done
  91.0 1.0 copy.18
  92.1 19.8 %all_to_all.16 = f32[64,4,128]{2,1,0:T(4,128)S(1)} all-to-all(f32[64,4,128]{2,1,0:T(4,128)S(1)} %bitcast.41), channel_id=1, replica_groups=mesh['y'=8,'x'=4,'zl'=2,'zh'=4,'c'=2] {'x','zl','zh','c'}, dimensions={0} | all-to-all | bytes 262144 | tf_op jit(solution)/shard_map/all_to_all | solution.py:283
  111.8 3.8 %all-to-all-start.2 = ((bf16[8,128,256]{2,1,0:T(8,128)(2,1)}), bf16[8,128,256]{2,1,0:T(8,128)(2,1)S(1)}, u32[]{:S(2)}, u32[]{:S(2)}) async-start(bf16[8,128,256]{2,1,0:T(8,128)(2,1)} %shard_map.113), calls=%async_computation.3 | async-start | bytes 1048576 | tf_op jit(solution)/shard_map/all_to_all | solution.py:243
  115.6 0.7 collective-permute-start.1
  116.3 0.7 collective-permute-start.2
  116.9 0.7 collective-permute-start.3
  117.6 0.7 collective-permute-start.4
  118.3 0.0 collective-permute-done.1
  118.3 0.0 collective-permute-done.2
  118.3 0.0 collective-permute-done.3
  118.3 0.0 collective-permute-done.4
  118.4 0.7 collective-permute-start.5
  119.0 0.7 collective-permute-start.6
  119.7 0.7 collective-permute-start.7
  120.4 0.0 collective-permute-done.5
  120.4 0.0 collective-permute-done.6
  120.4 0.0 collective-permute-done.7
  120.5 1.3 collective-permute-start.8
  121.8 12.0 %collective-permute-done.8 = bf16[128,256]{1,0:T(8,128)(2,1)S(1)} collective-permute-done((bf16[128,256]{1,0:T(8,128)(2,1)S(1)}, bf16[128,256]{1,0:T(8,128)(2,1)S(1)}, u32[]{:S(2)}, u32[]{:S(2)}) %collective-permute-start.8) | collective-permute-done | bytes 65568 | tf_op jit(solution)/shard_map/ppermute | solution.py:221
  133.8 0.0 all-to-all-done.2
  133.8 0.1 convert_reduce_fusion
  133.9 0.7 pad_maximum_fusion
  134.6 0.0 all-gather.10.cloned.1.call-update
  134.6 0.7 collective-permute-start.10
  135.3 0.7 collective-permute-start.11
  136.0 0.7 collective-permute-start.12
  136.7 0.7 collective-permute-start.13
  137.3 0.0 collective-permute-done.10
  137.3 0.0 collective-permute-done.11
  137.4 0.0 collective-permute-done.12
  137.4 0.0 collective-permute-done.13
  137.4 0.7 collective-permute-start.14
  138.1 0.7 collective-permute-start.15
  138.7 0.7 collective-permute-start.16
  139.4 2.2 %collective-permute-start.9 = (bf16[128,256]{1,0:T(8,128)(2,1)S(1)}, bf16[128,256]{1,0:T(8,128)(2,1)S(1)}, u32[]{:S(2)}, u32[]{:S(2)}) collective-permute-start(bf16[128,256]{1,0:T(8,128)(2,1)S(1)} %add_convert_fusion), channel_id=1, source_target_pairs={{0,8},{8,16},{16,24},{24,32},{32,40},{40,48},{48,56},{56,64},{64,7... | collective-permute-start | bytes 196616 | tf_op jit(solution)/shard_map/ppermute | solution.py:292
  141.6 0.7 reduce_sum.29
  142.3 0.0 collective-permute-done.14
  142.3 1.3 collective-permute-start.17
  143.6 1.7 collective-permute-done.9
  145.3 0.7 copy.19
  146.1 4.2 %collective-permute-done.17 = bf16[128,256]{1,0:T(8,128)(2,1)S(1)} collective-permute-done((bf16[128,256]{1,0:T(8,128)(2,1)S(1)}, bf16[128,256]{1,0:T(8,128)(2,1)S(1)}, u32[]{:S(2)}, u32[]{:S(2)}) %collective-permute-start.17) | collective-permute-done | bytes 65568 | tf_op jit(solution)/shard_map/ppermute | solution.py:221
  150.3 27.8 %all-gather.4 = bf16[1024,256]{1,0:T(8,128)(2,1)} all-gather(bf16[128,256]{1,0:T(8,128)(2,1)S(1)} %broadcast_select_fusion), channel_id=6, replica_groups=mesh['y'=8,'x'=4,'zl'=2,'zh'=4,'c'=2] {'zh','c'}, dimensions={0}, use_global_device_ids=true | all-gather | bytes 589824 | tf_op jit(solution)/shard_map/all_gather | solution.py:240
  178.1 3.4 %shard_map.114 = bf16[1,2,128,512]{3,2,1,0:T(8,128)(2,1)} custom-call(s32[1]{0:T(128)} %bitcast.section, bf16[8,2,128,256]{3,2,1,0:T(8,128)(2,1)} %bitcast.37, bf16[8,128,256]{2,1,0:T(8,128)(2,1)} %bitcast.34, f32[1,2048]{1,0:T(1,128)} %bitcast.44, bf16[1,2,2048,256]{3,2,1,0:T(8,128)(2,1)} %wkv_hbm.1), custom_call_target="tpu_custom_call" | custom-call | flops 536870912 | bytes 5000000 | tf_op jit(solution)/shard_map/pallas_call | solution.py:193
  (17 shorter events, 0.2 us)
Async XLA Ops:
  8.0 3.4 %copy-start = (bf16[1,2,2048,256]{3,2,1,0:T(8,128)(2,1)S(1)}, bf16[1,2,2048,256]{3,2,1,0:T(8,128)(2,1)}, u32[]{:S(2)}) copy-start(bf16[1,2,2048,256]{3,2,1,0:T(8,128)(2,1)} %wkv_hbm.1) | copy-start | bytes 6291460
  8.0 79.6 %all-gather.8.cloned.1.call-start = ((), (), s32[]{:S(2)}) async-start(), calls=%async_computation.5 | async-start | bytes 1179648 | tf_op jit(solution)/shard_map/all_gather | solution.py:240
  8.7 82.3 %reduce-scatter.2.cloned.1.call-start = ((), (), s32[]{:S(2)}) async-start(), calls=%async_computation.4 | async-start | bytes 1179648 | tf_op jit(solution)/shard_map/reduce_scatter | solution.py:264
  11.4 1.5 copy-start.2
  60.2 5.9 %collective-permute-start = (bf16[128,256]{1,0:T(8,128)(2,1)S(1)}, bf16[128,256]{1,0:T(8,128)(2,1)S(1)}, u32[]{:S(2)}, u32[]{:S(2)}) collective-permute-start(bf16[128,256]{1,0:T(8,128)(2,1)S(1)} %add_convert_fusion.1), channel_id=1, source_target_pairs={{0,8},{8,16},{16,24},{24,32},{32,40},{40,48},{48,56},{56,64},{64,7... | collective-permute-start | bytes 196616 | tf_op jit(solution)/shard_map/ppermute | solution.py:269
  91.0 42.9 %copy-start.1 = (bf16[2,128,256]{2,1,0:T(8,128)(2,1)S(1)}, bf16[2,128,256]{2,1,0:T(8,128)(2,1)}, u32[]{:S(2)}) copy-start(bf16[2,128,256]{2,1,0:T(8,128)(2,1)} %get-tuple-element.11) | copy-start | bytes 393220
  111.8 22.0 %all-to-all-start.2 = ((bf16[8,128,256]{2,1,0:T(8,128)(2,1)}), bf16[8,128,256]{2,1,0:T(8,128)(2,1)S(1)}, u32[]{:S(2)}, u32[]{:S(2)}) async-start(bf16[8,128,256]{2,1,0:T(8,128)(2,1)} %shard_map.113), calls=%async_computation.3 | async-start | bytes 1048576 | tf_op jit(solution)/shard_map/all_to_all | solution.py:243
  115.6 62.5 %all-gather.10.cloned.1.call-start = ((), (), s32[]{:S(2)}) async-start(), calls=%async_computation.6 | async-start | bytes 1179648 | tf_op jit(solution)/shard_map/all_gather | solution.py:240
  115.6 2.7 %collective-permute-start.1 = (bf16[128,256]{1,0:T(8,128)(2,1)S(1)}, bf16[128,256]{1,0:T(8,128)(2,1)S(1)}, u32[]{:S(2)}, u32[]{:S(2)}) collective-permute-start(bf16[128,256]{1,0:T(8,128)(2,1)S(1)} %add_convert_fusion.1), channel_id=1, source_target_pairs={{248,504},{249,505},{250,506},{251,507},{252,508},{253,509},{254,5... | collective-permute-start | bytes 196616 | tf_op jit(solution)/shard_map/ppermute | solution.py:211
  116.3 2.0 %collective-permute-start.2 = (bf16[128,256]{1,0:T(8,128)(2,1)S(1)}, bf16[128,256]{1,0:T(8,128)(2,1)S(1)}, u32[]{:S(2)}, u32[]{:S(2)}) collective-permute-start(bf16[128,256]{1,0:T(8,128)(2,1)S(1)} %add_convert_fusion.1), channel_id=1, source_target_pairs={{248,440},{249,441},{250,442},{251,443},{252,444},{253,445},{254,4... | collective-permute-start | bytes 196616 | tf_op jit(solution)/shard_map/ppermute | solution.py:211
  116.9 1.4 collective-permute-start.3
  117.6 0.7 collective-permute-start.4
  118.4 2.0 %collective-permute-start.5 = (bf16[128,256]{1,0:T(8,128)(2,1)S(1)}, bf16[128,256]{1,0:T(8,128)(2,1)S(1)}, u32[]{:S(2)}, u32[]{:S(2)}) collective-permute-start(bf16[128,256]{1,0:T(8,128)(2,1)S(1)} %select_select_fusion.3), channel_id=1, source_target_pairs={{312,296},{376,360},{440,424},{504,488},{313,297},{377,361},{441,4... | collective-permute-start | bytes 196616 | tf_op jit(solution)/shard_map/ppermute | solution.py:217
  119.0 1.4 collective-permute-start.6
  119.7 0.7 collective-permute-start.7
  120.5 13.3 %collective-permute-start.8 = (bf16[128,256]{1,0:T(8,128)(2,1)S(1)}, bf16[128,256]{1,0:T(8,128)(2,1)S(1)}, u32[]{:S(2)}, u32[]{:S(2)}) collective-permute-start(bf16[128,256]{1,0:T(8,128)(2,1)S(1)} %select_select_fusion.2), channel_id=1, source_target_pairs={{264,256},{280,272},{296,288},{312,304},{328,320},{344,336},{360,3... | collective-permute-start | bytes 196616 | tf_op jit(solution)/shard_map/ppermute | solution.py:221
  134.6 2.7 %collective-permute-start.10 = (bf16[128,256]{1,0:T(8,128)(2,1)S(1)}, bf16[128,256]{1,0:T(8,128)(2,1)S(1)}, u32[]{:S(2)}, u32[]{:S(2)}) collective-permute-start(bf16[128,256]{1,0:T(8,128)(2,1)S(1)} %add_convert_fusion), channel_id=1, source_target_pairs={{248,504},{249,505},{250,506},{251,507},{252,508},{253,509},{254,5... | collective-permute-start | bytes 196616 | tf_op jit(solution)/shard_map/ppermute | solution.py:211
  135.3 2.0 %collective-permute-start.11 = (bf16[128,256]{1,0:T(8,128)(2,1)S(1)}, bf16[128,256]{1,0:T(8,128)(2,1)S(1)}, u32[]{:S(2)}, u32[]{:S(2)}) collective-permute-start(bf16[128,256]{1,0:T(8,128)(2,1)S(1)} %add_convert_fusion), channel_id=1, source_target_pairs={{248,440},{249,441},{250,442},{251,443},{252,444},{253,445},{254,4... | collective-permute-start | bytes 196616 | tf_op jit(solution)/shard_map/ppermute | solution.py:211
  136.0 1.4 collective-permute-start.12
  136.7 0.7 collective-permute-start.13
  137.4 4.9 %collective-permute-start.14 = (bf16[128,256]{1,0:T(8,128)(2,1)S(1)}, bf16[128,256]{1,0:T(8,128)(2,1)S(1)}, u32[]{:S(2)}, u32[]{:S(2)}) collective-permute-start(bf16[128,256]{1,0:T(8,128)(2,1)S(1)} %select_select_fusion.1), channel_id=1, source_target_pairs={{312,296},{376,360},{440,424},{504,488},{313,297},{377,361},{441,4... | collective-permute-start | bytes 196616 | tf_op jit(solution)/shard_map/ppermute | solution.py:217
  138.1 4.2 %collective-permute-start.15 = (bf16[128,256]{1,0:T(8,128)(2,1)S(1)}, bf16[128,256]{1,0:T(8,128)(2,1)S(1)}, u32[]{:S(2)}, u32[]{:S(2)}) collective-permute-start(bf16[128,256]{1,0:T(8,128)(2,1)S(1)} %select_select_fusion.1), channel_id=1, source_target_pairs={{312,280},{376,344},{440,408},{504,472},{313,281},{377,345},{441,4... | collective-permute-start | bytes 196616 | tf_op jit(solution)/shard_map/ppermute | solution.py:217
  138.7 3.6 %collective-permute-start.16 = (bf16[128,256]{1,0:T(8,128)(2,1)S(1)}, bf16[128,256]{1,0:T(8,128)(2,1)S(1)}, u32[]{:S(2)}, u32[]{:S(2)}) collective-permute-start(bf16[128,256]{1,0:T(8,128)(2,1)S(1)} %select_select_fusion.1), channel_id=1, source_target_pairs={{312,264},{376,328},{440,392},{504,456},{313,265},{377,329},{441,3... | collective-permute-start | bytes 196616 | tf_op jit(solution)/shard_map/ppermute | solution.py:217
  139.4 5.9 %collective-permute-start.9 = (bf16[128,256]{1,0:T(8,128)(2,1)S(1)}, bf16[128,256]{1,0:T(8,128)(2,1)S(1)}, u32[]{:S(2)}, u32[]{:S(2)}) collective-permute-start(bf16[128,256]{1,0:T(8,128)(2,1)S(1)} %add_convert_fusion), channel_id=1, source_target_pairs={{0,8},{8,16},{16,24},{24,32},{32,40},{40,48},{48,56},{56,64},{64,7... | collective-permute-start | bytes 196616 | tf_op jit(solution)/shard_map/ppermute | solution.py:292
  142.3 7.9 %collective-permute-start.17 = (bf16[128,256]{1,0:T(8,128)(2,1)S(1)}, bf16[128,256]{1,0:T(8,128)(2,1)S(1)}, u32[]{:S(2)}, u32[]{:S(2)}) collective-permute-start(bf16[128,256]{1,0:T(8,128)(2,1)S(1)} %select_select_fusion), channel_id=1, source_target_pairs={{264,256},{280,272},{296,288},{312,304},{328,320},{344,336},{360,3... | collective-permute-start | bytes 196616 | tf_op jit(solution)/shard_map/ppermute | solution.py:221
Sparse Core Ops, SparseCore 0:
  11.0 38.4 all-gather.7
  134.8 37.0 all-gather.9
Sparse Core Ops, SparseCore 1:
  13.0 39.2 reduce-scatter.1

commit v4 on v3

--- a/solution.py
+++ b/solution.py
@@ -153,6 +153,37 @@
     tick_kernel(1, half, section, x, fresh, gain, final, wq, wkv, wo, cache, out, None, *scratch)
 
 
+def share_kernel(half, section, grads_hbm, wkv_hbm, out_hbm, grads, wkv, total, out, sems):
+    width = wkv.shape[2]
+    heads, ys, each, xz, _ = out.shape
+
+    @pl.when(section[0] >= half)
+    def _():
+        get_grads = pltpu.make_async_copy(grads_hbm.at[0], grads, sems.at[0])
+        get_wkv = pltpu.make_async_copy(wkv_hbm.at[0], wkv, sems.at[1])
+        get_grads.start()
+        get_wkv.start()
+        get_grads.wait()
+        get_wkv.wait()
+        rows_by = (((1,), (1,)), ((), ()))
+        total[...] = lax.dot_general(
+            wkv[0], grads[:, :width], rows_by, preferred_element_type=F32
+        ) + lax.dot_general(wkv[1], grads[:, width:], rows_by, preferred_element_type=F32)
+        for h in range(heads):
+            for y in range(ys):
+                for i in range(each):
+                    first = y * xz * heads * each + h * each + i
+                    out[h, y, i] = total[pl.ds(first, xz, stride=heads * each), :]
+
+    @pl.when(section[0] < half)
+    def _():
+        out[...] = jnp.zeros_like(out)
+
+    put = pltpu.make_async_copy(out, out_hbm, sems.at[2])
+    put.start()
+    put.wait()
+
+
 def memory_kernel(half, section, first_hbm, second_hbm, final_hbm, wkv_hbm, out_hbm, sources, rows,
                   final_gain, wkv, out, sems):
     width = wkv.shape[2]
@@ -189,14 +220,14 @@
     put.wait()
 
 
-def call(kernel, section, operands, out_shapes, scratch, copies, flops):
+def call(kernel, section, operands, out_shapes, scratch, copies, flops, kind=BF):
     return pl.pallas_call(
         kernel,
-        out_shape=[jax.ShapeDtypeStruct(shape, BF) for shape in out_shapes],
+        out_shape=[jax.ShapeDtypeStruct(shape, kind) for shape in out_shapes],
         in_specs=[pl.BlockSpec(memory_space=pltpu.SMEM)]
         + [pl.BlockSpec(memory_space=pl.ANY)] * len(operands),
         out_specs=[pl.BlockSpec(memory_space=pl.ANY)] * len(out_shapes),
-        scratch_shapes=[pltpu.VMEM(shape, kind) for shape, kind in scratch]
+        scratch_shapes=[pltpu.VMEM(shape, held) for shape, held in scratch]
         + [pltpu.SemaphoreType.DMA((copies,))],
         compiler_params=pltpu.CompilerParams(vmem_limit_bytes=60 * 1024 * 1024),
         cost_estimate=pl.CostEstimate(flops=flops, bytes_accessed=5_000_000, transcendentals=0),
@@ -226,8 +257,7 @@
     half = pipe_count // 2
     place_here = lax.axis_index(PIPE)
     section = place_here.astype(jnp.int32)[None]
-    wkv = w_kv[0]
-    depth, width = wkv.shape[1:]
+    depth, width = w_kv.shape[2:]
     tokens = stream.shape[2]
     final_scale = final_gain[None]
     rows8 = (heads, tokens, width)
@@ -257,13 +287,24 @@
         8 + heads, flops,
     )
 
-    grads = jnp.where(place_here >= half, cache_grad[0], jnp.zeros_like(cache_grad[0]))
-    rows_by = (((1,), (1,)), ((), ()))
-    share = lax.dot_general(wkv[0], grads[:, :width], rows_by, preferred_element_type=F32)
-    share = share + lax.dot_general(wkv[1], grads[:, width:], rows_by, preferred_element_type=F32)
+    each = depth // (pipe_count * heads)
+    shares = (heads, Y, each, X * ZL, tokens)
+    (share,) = call(
+        functools.partial(share_kernel, half), section, (cache_grad, w_kv), (shares,),
+        ((pair_shape, BF), ((2, depth, width), BF), ((depth, tokens), F32), (shares, F32)),
+        3, flops, F32,
+    )
+    share = share.reshape(depth, tokens)
+    share = lax.psum_scatter(share, HEAD, scatter_dimension=0, tiled=True)
     share = lax.psum_scatter(share, "y", scatter_dimension=0, tiled=True)
-    plane = X * ZL * heads
-    share = share.reshape(plane, depth // (pipe_count * heads), tokens)
+    share = share.reshape(each, X, ZL, tokens).transpose(1, 2, 0, 3).reshape(X, 1, ZL * each, tokens)
+    share = jnp.broadcast_to(share, (X, 8, ZL * each, tokens)).reshape(-1, tokens)
+    share = lax.psum_scatter(share, "x", scatter_dimension=0, tiled=True)
+    share = share[: ZL * each].reshape(ZL, each, tokens)
+    at_first = lax.axis_index("zl") == 0
+    kept = jnp.where(at_first, share[0], share[1])
+    given = jnp.where(at_first, share[1], share[0])
+    memory_grad = kept + lax.ppermute(given, "zl", [(0, 1), (1, 0)])
 
     output = summed(exchanged(parts), current)
     passed = lax.ppermute(output, PIPE, shift)
@@ -279,14 +320,8 @@
         + weights + ((pair_shape, BF), (rows8, BF), (rows8, BF), (rows8, BF)),
         8 + heads, flops,
     )
-    share, parts = lax.optimization_barrier((share, parts))
-    share = lax.all_to_all(share, PIPE[1:] + HEAD, 0, 0, tiled=True)
-    share, parts = lax.optimization_barrier((share, exchanged(parts)))
-    memory_grad = jnp.sum(share, axis=0)
-
     current = jnp.where(place_here == half, fresh_rows[1], current)
-    output = summed(parts, current)
-    output, first_memory = lax.optimization_barrier((output, first_memory))
+    output = summed(exchanged(parts), current)
     second_memory = spread(output, half - 1)
     first_memory = whole(jnp.stack([first_memory, entering]))
     passed = lax.ppermute(output, PIPE, shift)

time: 190 us -> 222 us (1.17)
  the two profiles are of different devices: /device:TPU:35 before, /device:TPU:33 now
where the time goes in v4:
time: 222 us; the launch traced here: 221 us
  waiting for transfers between devices  87 us (39%)
  blocking collectives  66.8 us (30%)
  starting transfers between devices  30.5 us (14%)
  Pallas kernels  16.5 us (7%)
  between operations  14.2 us (6%)
  local copies, waits for them, and re-layouts  3.06 us (1%)
  other arithmetic  3.06 us (1%)
    all_gather x3, blocking collectives, whole(): return lax.all_gather(block, HEAD, axis=0)  66.8 us
    reduce_scatter x1, waiting for transfers between devices, body(): share = lax.psum_scatter(share, 'y', scatter_dimension=0, tiled=True)  32.3 us
    reduce_scatter x1, waiting for transfers between devices, body(): share = lax.psum_scatter(share, 'x', scatter_dimension=0, tiled=True)  27.8 us
    pallas_call x4, Pallas kernels, call(): pl.pallas_call(kernel, out_shape=[jax.ShapeDtypeStruct(shape, kind) for s...  16.5 us
    all_to_all x2, waiting for transfers between devices, exchanged(): return lax.all_to_all(parts, HEAD, 0, 0, tiled=True)  13.3 us
    all_to_all x2, starting transfers between devices, exchanged(): return lax.all_to_all(parts, HEAD, 0, 0, tiled=True)  9.19 us
    ppermute x2, waiting for transfers between devices, body(): passed = lax.ppermute(output, PIPE, shift)  8.31 us
    ppermute x2, starting transfers between devices, body(): passed = lax.ppermute(output, PIPE, shift)  6.06 us
  transfers between devices with their start and end apart: 26, of which 6 were waited for; matrix products, arithmetic and copies ran while one was open for 3% of the time, Pallas kernels for 6%

profile of v4, /device:TPU:33, one launch (start us, length us, event | category | flops | bytes accessed | tf_op | source)
XLA Modules:
  0.0 221.2 jit_solution(15708825760618240209)
XLA Ops:
  7.2 0.0 all-gather.8.cloned.1.call-start
  7.2 0.7 all-gather.8.cloned.1.call-update
  7.9 0.9 copy.19
  8.9 22.2 %all-gather = bf16[1024,256]{1,0:T(8,128)(2,1)} all-gather(bf16[128,256]{1,0:T(8,128)(2,1)S(1)} %bitcast.36), channel_id=2, replica_groups=mesh['y'=8,'x'=4,'zl'=2,'zh'=4,'c'=2] {'zh','c'}, dimensions={0}, use_global_device_ids=true | all-gather | bytes 589824 | tf_op jit(solution)/shard_map/all_gather | solution.py:270
  31.0 3.8 %shard_map.112 = (bf16[8,128,256]{2,1,0:T(8,128)(2,1)}, bf16[2,128,256]{2,1,0:T(8,128)(2,1)}) custom-call(s32[1]{0:T(128)} %bitcast.section, bf16[8,128,256]{2,1,0:T(8,128)(2,1)} %bitcast.33, bf16[2,256,128]{2,1,0:T(8,128)(2,1)} %fresh.1, f32[1,2048]{1,0:T(1,128)} %gain.3, bf16[1,2048,256]{2,1,0:T(8,128)(2,1)} %wq.3, bf16[1,2,2048,256]{3,2,1,0:T(8,128)(2,1)} %wkv_hbm.3, ...), custom_call_target="tpu_custom_call" | custom-call | flops 536870912 | bytes 5000000 | tf_op jit(solution)/shard_map/pallas_call | solution.py:224
  34.8 5.3 %all-to-all-start = ((bf16[8,128,256]{2,1,0:T(8,128)(2,1)}), bf16[8,128,256]{2,1,0:T(8,128)(2,1)S(1)}, u32[]{:S(2)}, u32[]{:S(2)}) async-start(bf16[8,128,256]{2,1,0:T(8,128)(2,1)} %get-tuple-element.6), calls=%async_computation | async-start | bytes 1048576 | tf_op jit(solution)/shard_map/all_to_all | solution.py:273
  40.1 3.8 %shard_map.115 = f32[8,8,4,8,128]{4,3,2,1,0:T(8,128)} custom-call(s32[1]{0:T(128)} %bitcast.section, bf16[1,128,512]{2,1,0:T(8,128)(2,1)} %grads_hbm.1, bf16[1,2,2048,256]{3,2,1,0:T(8,128)(2,1)} %wkv_hbm.3), custom_call_target="tpu_custom_call" | custom-call | flops 536870912 | bytes 5000000 | tf_op jit(solution)/shard_map/pallas_call | solution.py:224
  43.9 0.0 reduce-scatter.4.cloned.1.call-update
  43.9 13.3 %all-to-all-done = bf16[8,128,256]{2,1,0:T(8,128)(2,1)S(1)} async-done(((bf16[8,128,256]{2,1,0:T(8,128)(2,1)}), bf16[8,128,256]{2,1,0:T(8,128)(2,1)S(1)}, u32[]{:S(2)}, u32[]{:S(2)}) %all-to-all-start) | async-done | bytes 524320 | tf_op jit(solution)/shard_map/all_to_all | solution.py:273
  57.2 0.1 convert_reduce_fusion.1
  57.3 3.4 %collective-permute-start = (bf16[128,256]{1,0:T(8,128)(2,1)S(1)}, bf16[128,256]{1,0:T(8,128)(2,1)S(1)}, u32[]{:S(2)}, u32[]{:S(2)}) collective-permute-start(bf16[128,256]{1,0:T(8,128)(2,1)S(1)} %add_convert_fusion.1), channel_id=1, source_target_pairs={{0,8},{8,16},{16,24},{24,32},{32,40},{40,48},{48,56},{56,64},{64,7... | collective-permute-start | bytes 196616 | tf_op jit(solution)/shard_map/ppermute | solution.py:310
  60.8 0.7 collective-permute-start.2
  61.4 0.7 collective-permute-start.3
  62.1 0.7 collective-permute-start.4
  62.8 0.7 collective-permute-start.5
  63.5 3.1 %collective-permute-done = bf16[128,256]{1,0:T(8,128)(2,1)S(1)} collective-permute-done((bf16[128,256]{1,0:T(8,128)(2,1)S(1)}, bf16[128,256]{1,0:T(8,128)(2,1)S(1)}, u32[]{:S(2)}, u32[]{:S(2)}) %collective-permute-start) | collective-permute-done | bytes 65568 | tf_op jit(solution)/shard_map/ppermute | solution.py:310
  66.5 19.7 %all-gather.1 = bf16[1024,256]{1,0:T(8,128)(2,1)} all-gather(bf16[128,256]{1,0:T(8,128)(2,1)S(1)} %bitcast_select_fusion), channel_id=3, replica_groups=mesh['y'=8,'x'=4,'zl'=2,'zh'=4,'c'=2] {'zh','c'}, dimensions={0}, use_global_device_ids=true | all-gather | bytes 589824 | tf_op jit(solution)/shard_map/all_gather | solution.py:270
  86.3 5.5 %shard_map.113 = bf16[8,128,256]{2,1,0:T(8,128)(2,1)} custom-call(s32[1]{0:T(128)} %bitcast.section, bf16[8,128,256]{2,1,0:T(8,128)(2,1)} %bitcast.32, bf16[8,2,256,128]{3,2,1,0:T(8,128)(2,1)} %bitcast.35, f32[1,2048]{1,0:T(1,128)} %gain.3, f32[1,2048]{1,0:T(1,128)} %bitcast.40, bf16[1,2048,256]{2,1,0:T(8,128)(2,1)} %wq.3, ...), custom_call_target="tpu_custom_call" | custom-call | flops 536870912 | bytes 5000000 | tf_op jit(solution)/shard_map/pallas_call | solution.py:224
  91.8 3.9 %all-to-all-start.1 = ((bf16[8,128,256]{2,1,0:T(8,128)(2,1)}), bf16[8,128,256]{2,1,0:T(8,128)(2,1)S(1)}, u32[]{:S(2)}, u32[]{:S(2)}) async-start(bf16[8,128,256]{2,1,0:T(8,128)(2,1)} %shard_map.113), calls=%async_computation.1 | async-start | bytes 1048576 | tf_op jit(solution)/shard_map/all_to_all | solution.py:273
  95.8 0.0 collective-permute-done.2
  95.8 0.0 collective-permute-done.3
  95.8 0.0 collective-permute-done.4
  95.8 0.0 collective-permute-done.5
  95.8 0.7 collective-permute-start.6
  96.5 0.7 collective-permute-start.7
  97.2 0.7 collective-permute-start.8
  97.8 4.5 %reduce-scatter.4.cloned.1.call-done = f32[256,128]{1,0:T(8,128)} async-done(((f32[2048,128]{1,0:T(8,128)}), f32[256,128]{1,0:T(8,128)}) %reduce-scatter.4.cloned.1.call-update) | async-done | bytes 131088 | tf_op jit(solution)/shard_map/reduce_scatter | solution.py:298
  102.3 0.0 reduce-scatter.6.cloned.1.call-update
  102.3 0.0 reduce-scatter.8.cloned.1.call-start
  102.4 0.0 collective-permute-done.6
  102.4 0.0 collective-permute-done.7
  102.4 1.3 collective-permute-start.9
  103.8 32.3 %reduce-scatter.6.cloned.1.call-done = f32[32,128]{1,0:T(8,128)} async-done(((f32[256,128]{1,0:T(8,128)}), f32[32,128]{1,0:T(8,128)}) %reduce-scatter.6.cloned.1.call-update) | async-done | bytes 16400 | tf_op jit(solution)/shard_map/reduce_scatter | solution.py:299
  136.1 0.7 copy.20
  136.8 0.7 broadcast_in_dim.24
  137.5 0.0 reduce-scatter.8.cloned.1.call-update
  137.5 0.0 all-gather.10.cloned.1.call-start
  137.6 0.7 pad_maximum_fusion
  138.3 0.0 all-gather.10.cloned.1.call-update
  138.3 0.0 all-to-all-done.1
  138.3 0.1 convert_reduce_fusion
  138.4 0.7 collective-permute-start.10
  139.1 0.7 collective-permute-start.11
  139.7 0.7 collective-permute-start.12
  140.4 0.7 collective-permute-start.13
  141.1 27.8 %reduce-scatter.8.cloned.1.call-done = f32[64,128]{1,0:T(8,128)} async-done(((f32[256,128]{1,0:T(8,128)}), f32[64,128]{1,0:T(8,128)}) %reduce-scatter.8.cloned.1.call-update) | async-done | bytes 32784 | tf_op jit(solution)/shard_map/reduce_scatter | solution.py:302
  168.9 0.8 slice_select_fusion
  169.7 3.3 %collective-permute-start.18 = (f32[4,128]{1,0:T(4,128)S(1)}, f32[4,128]{1,0:T(4,128)S(1)}, u32[]{:S(2)}, u32[]{:S(2)}) collective-permute-start(f32[4,128]{1,0:T(4,128)S(1)} %slice_select_fusion), channel_id=1, source_target_pairs={{0,8},{8,0},{1,9},{9,1},{2,10},{10,2},{3,11},{11,3},{4,12},{12,4},... | collective-permute-start | bytes 6152 | tf_op jit(solution)/shard_map/ppermute | solution.py:307
  172.9 0.0 collective-permute-done.10
  173.0 0.0 collective-permute-done.12
  173.0 0.0 collective-permute-done.13
  173.0 0.7 collective-permute-start.14
  173.7 0.7 collective-permute-start.15
  174.4 0.7 collective-permute-start.16
  175.0 0.0 collective-permute-done.18
  175.0 1.3 select_add_fusion
  176.4 2.6 %collective-permute-start.1 = (bf16[128,256]{1,0:T(8,128)(2,1)S(1)}, bf16[128,256]{1,0:T(8,128)(2,1)S(1)}, u32[]{:S(2)}, u32[]{:S(2)}) collective-permute-start(bf16[128,256]{1,0:T(8,128)(2,1)S(1)} %add_convert_fusion), channel_id=1, source_target_pairs={{0,8},{8,16},{16,24},{24,32},{32,40},{40,48},{48,56},{56,64},{64,7... | collective-permute-start | bytes 196616 | tf_op jit(solution)/shard_map/ppermute | solution.py:327
  179.0 0.0 collective-permute-done.15
  179.0 0.0 collective-permute-done.16
  179.1 1.3 collective-permute-start.17
  180.4 5.2 %collective-permute-done.1 = bf16[128,256]{1,0:T(8,128)(2,1)S(1)} collective-permute-done((bf16[128,256]{1,0:T(8,128)(2,1)S(1)}, bf16[128,256]{1,0:T(8,128)(2,1)S(1)}, u32[]{:S(2)}, u32[]{:S(2)}) %collective-permute-start.1) | collective-permute-done | bytes 65568 | tf_op jit(solution)/shard_map/ppermute | solution.py:327
  185.6 0.7 copy.21
  186.4 24.9 %all-gather.4 = bf16[1024,256]{1,0:T(8,128)(2,1)} all-gather(bf16[128,256]{1,0:T(8,128)(2,1)S(1)} %broadcast_select_fusion), channel_id=6, replica_groups=mesh['y'=8,'x'=4,'zl'=2,'zh'=4,'c'=2] {'zh','c'}, dimensions={0}, use_global_device_ids=true | all-gather | bytes 589824 | tf_op jit(solution)/shard_map/all_gather | solution.py:270
  211.2 3.4 %shard_map.114 = bf16[1,2,128,512]{3,2,1,0:T(8,128)(2,1)} custom-call(s32[1]{0:T(128)} %bitcast.section, bf16[8,2,128,256]{3,2,1,0:T(8,128)(2,1)} %bitcast.34, bf16[8,128,256]{2,1,0:T(8,128)(2,1)} %bitcast.31, f32[1,2048]{1,0:T(1,128)} %bitcast.41, bf16[1,2,2048,256]{3,2,1,0:T(8,128)(2,1)} %wkv_hbm.3), custom_call_target="tpu_custom_call" | custom-call | flops 536870912 | bytes 5000000 | tf_op jit(solution)/shard_map/pallas_call | solution.py:224
  (21 shorter events, 0.2 us)
Async XLA Ops:
  7.2 79.1 %all-gather.8.cloned.1.call-start = ((), (), s32[]{:S(2)}) async-start(), calls=%async_computation.8 | async-start | bytes 1179648 | tf_op jit(solution)/shard_map/all_gather | solution.py:270
  34.8 22.4 %all-to-all-start = ((bf16[8,128,256]{2,1,0:T(8,128)(2,1)}), bf16[8,128,256]{2,1,0:T(8,128)(2,1)S(1)}, u32[]{:S(2)}, u32[]{:S(2)}) async-start(bf16[8,128,256]{2,1,0:T(8,128)(2,1)} %get-tuple-element.6), calls=%async_computation | async-start | bytes 1048576 | tf_op jit(solution)/shard_map/all_to_all | solution.py:273
  40.1 26.5 %copy-start = (bf16[2,128,256]{2,1,0:T(8,128)(2,1)S(1)}, bf16[2,128,256]{2,1,0:T(8,128)(2,1)}, u32[]{:S(2)}) copy-start(bf16[2,128,256]{2,1,0:T(8,128)(2,1)} %get-tuple-element.5) | copy-start | bytes 393220
  40.1 62.2 %reduce-scatter.4.cloned.1.call-start = ((), (), s32[]{:S(2)}) async-start(), calls=%async_computation.5 | async-start | bytes 1179648 | tf_op jit(solution)/shard_map/reduce_scatter | solution.py:298
  57.3 9.2 %collective-permute-start = (bf16[128,256]{1,0:T(8,128)(2,1)S(1)}, bf16[128,256]{1,0:T(8,128)(2,1)S(1)}, u32[]{:S(2)}, u32[]{:S(2)}) collective-permute-start(bf16[128,256]{1,0:T(8,128)(2,1)S(1)} %add_convert_fusion.1), channel_id=1, source_target_pairs={{0,8},{8,16},{16,24},{24,32},{32,40},{40,48},{48,56},{56,64},{64,7... | collective-permute-start | bytes 196616 | tf_op jit(solution)/shard_map/ppermute | solution.py:310
  60.8 35.0 %collective-permute-start.2 = (bf16[128,256]{1,0:T(8,128)(2,1)S(1)}, bf16[128,256]{1,0:T(8,128)(2,1)S(1)}, u32[]{:S(2)}, u32[]{:S(2)}) collective-permute-start(bf16[128,256]{1,0:T(8,128)(2,1)S(1)} %add_convert_fusion.1), channel_id=1, source_target_pairs={{248,504},{249,505},{250,506},{251,507},{252,508},{253,509},{254,5... | collective-permute-start | bytes 196616 | tf_op jit(solution)/shard_map/ppermute | solution.py:242
  61.4 34.3 %collective-permute-start.3 = (bf16[128,256]{1,0:T(8,128)(2,1)S(1)}, bf16[128,256]{1,0:T(8,128)(2,1)S(1)}, u32[]{:S(2)}, u32[]{:S(2)}) collective-permute-start(bf16[128,256]{1,0:T(8,128)(2,1)S(1)} %add_convert_fusion.1), channel_id=1, source_target_pairs={{248,440},{249,441},{250,442},{251,443},{252,444},{253,445},{254,4... | collective-permute-start | bytes 196616 | tf_op jit(solution)/shard_map/ppermute | solution.py:242
  62.1 33.7 %collective-permute-start.4 = (bf16[128,256]{1,0:T(8,128)(2,1)S(1)}, bf16[128,256]{1,0:T(8,128)(2,1)S(1)}, u32[]{:S(2)}, u32[]{:S(2)}) collective-permute-start(bf16[128,256]{1,0:T(8,128)(2,1)S(1)} %add_convert_fusion.1), channel_id=1, source_target_pairs={{248,376},{249,377},{250,378},{251,379},{252,380},{253,381},{254,3... | collective-permute-start | bytes 196616 | tf_op jit(solution)/shard_map/ppermute | solution.py:242
  62.8 33.0 %collective-permute-start.5 = (bf16[128,256]{1,0:T(8,128)(2,1)S(1)}, bf16[128,256]{1,0:T(8,128)(2,1)S(1)}, u32[]{:S(2)}, u32[]{:S(2)}) collective-permute-start(bf16[128,256]{1,0:T(8,128)(2,1)S(1)} %add_convert_fusion.1), channel_id=1, source_target_pairs={{248,312},{249,313},{250,314},{251,315},{252,316},{253,317},{254,3... | collective-permute-start | bytes 196616 | tf_op jit(solution)/shard_map/ppermute | solution.py:242
  91.8 46.4 %all-to-all-start.1 = ((bf16[8,128,256]{2,1,0:T(8,128)(2,1)}), bf16[8,128,256]{2,1,0:T(8,128)(2,1)S(1)}, u32[]{:S(2)}, u32[]{:S(2)}) async-start(bf16[8,128,256]{2,1,0:T(8,128)(2,1)} %shard_map.113), calls=%async_computation.1 | async-start | bytes 1048576 | tf_op jit(solution)/shard_map/all_to_all | solution.py:273
  95.7 40.3 %reduce-scatter.6.cloned.1.call-start = ((), (), s32[]{:S(2)}) async-start(), calls=%async_computation.6 | async-start | bytes 147456 | tf_op jit(solution)/shard_map/reduce_scatter | solution.py:299
  95.8 6.6 %collective-permute-start.6 = (bf16[128,256]{1,0:T(8,128)(2,1)S(1)}, bf16[128,256]{1,0:T(8,128)(2,1)S(1)}, u32[]{:S(2)}, u32[]{:S(2)}) collective-permute-start(bf16[128,256]{1,0:T(8,128)(2,1)S(1)} %select_select_fusion.3), channel_id=1, source_target_pairs={{312,296},{376,360},{440,424},{504,488},{313,297},{377,361},{441,4... | collective-permute-start | bytes 196616 | tf_op jit(solution)/shard_map/ppermute | solution.py:248
  96.5 5.9 %collective-permute-start.7 = (bf16[128,256]{1,0:T(8,128)(2,1)S(1)}, bf16[128,256]{1,0:T(8,128)(2,1)S(1)}, u32[]{:S(2)}, u32[]{:S(2)}) collective-permute-start(bf16[128,256]{1,0:T(8,128)(2,1)S(1)} %select_select_fusion.3), channel_id=1, source_target_pairs={{312,280},{376,344},{440,408},{504,472},{313,281},{377,345},{441,4... | collective-permute-start | bytes 196616 | tf_op jit(solution)/shard_map/ppermute | solution.py:248
  97.2 5.2 %collective-permute-start.8 = (bf16[128,256]{1,0:T(8,128)(2,1)S(1)}, bf16[128,256]{1,0:T(8,128)(2,1)S(1)}, u32[]{:S(2)}, u32[]{:S(2)}) collective-permute-start(bf16[128,256]{1,0:T(8,128)(2,1)S(1)} %select_select_fusion.3), channel_id=1, source_target_pairs={{312,264},{376,328},{440,392},{504,456},{313,265},{377,329},{441,3... | collective-permute-start | bytes 196616 | tf_op jit(solution)/shard_map/ppermute | solution.py:248
  102.3 66.6 %reduce-scatter.8.cloned.1.call-start = ((), (), s32[]{:S(2)}) async-start(), calls=%async_computation.7 | async-start | bytes 163840 | tf_op jit(solution)/shard_map/reduce_scatter | solution.py:302
  102.4 35.1 %collective-permute-start.9 = (bf16[128,256]{1,0:T(8,128)(2,1)S(1)}, bf16[128,256]{1,0:T(8,128)(2,1)S(1)}, u32[]{:S(2)}, u32[]{:S(2)}) collective-permute-start(bf16[128,256]{1,0:T(8,128)(2,1)S(1)} %select_select_fusion.2), channel_id=1, source_target_pairs={{264,256},{280,272},{296,288},{312,304},{328,320},{344,336},{360,3... | collective-permute-start | bytes 196616 | tf_op jit(solution)/shard_map/ppermute | solution.py:252
  137.5 73.7 %all-gather.10.cloned.1.call-start = ((), (), s32[]{:S(2)}) async-start(), calls=%async_computation.9 | async-start | bytes 1179648 | tf_op jit(solution)/shard_map/all_gather | solution.py:270
  138.4 34.6 %collective-permute-start.10 = (bf16[128,256]{1,0:T(8,128)(2,1)S(1)}, bf16[128,256]{1,0:T(8,128)(2,1)S(1)}, u32[]{:S(2)}, u32[]{:S(2)}) collective-permute-start(bf16[128,256]{1,0:T(8,128)(2,1)S(1)} %add_convert_fusion), channel_id=1, source_target_pairs={{248,504},{249,505},{250,506},{251,507},{252,508},{253,509},{254,5... | collective-permute-start | bytes 196616 | tf_op jit(solution)/shard_map/ppermute | solution.py:242
  139.1 33.9 %collective-permute-start.11 = (bf16[128,256]{1,0:T(8,128)(2,1)S(1)}, bf16[128,256]{1,0:T(8,128)(2,1)S(1)}, u32[]{:S(2)}, u32[]{:S(2)}) collective-permute-start(bf16[128,256]{1,0:T(8,128)(2,1)S(1)} %add_convert_fusion), channel_id=1, source_target_pairs={{248,440},{249,441},{250,442},{251,443},{252,444},{253,445},{254,4... | collective-permute-start | bytes 196616 | tf_op jit(solution)/shard_map/ppermute | solution.py:242
  139.7 33.2 %collective-permute-start.12 = (bf16[128,256]{1,0:T(8,128)(2,1)S(1)}, bf16[128,256]{1,0:T(8,128)(2,1)S(1)}, u32[]{:S(2)}, u32[]{:S(2)}) collective-permute-start(bf16[128,256]{1,0:T(8,128)(2,1)S(1)} %add_convert_fusion), channel_id=1, source_target_pairs={{248,376},{249,377},{250,378},{251,379},{252,380},{253,381},{254,3... | collective-permute-start | bytes 196616 | tf_op jit(solution)/shard_map/ppermute | solution.py:242
  140.4 32.6 %collective-permute-start.13 = (bf16[128,256]{1,0:T(8,128)(2,1)S(1)}, bf16[128,256]{1,0:T(8,128)(2,1)S(1)}, u32[]{:S(2)}, u32[]{:S(2)}) collective-permute-start(bf16[128,256]{1,0:T(8,128)(2,1)S(1)} %add_convert_fusion), channel_id=1, source_target_pairs={{248,312},{249,313},{250,314},{251,315},{252,316},{253,317},{254,3... | collective-permute-start | bytes 196616 | tf_op jit(solution)/shard_map/ppermute | solution.py:242
  169.7 5.4 %collective-permute-start.18 = (f32[4,128]{1,0:T(4,128)S(1)}, f32[4,128]{1,0:T(4,128)S(1)}, u32[]{:S(2)}, u32[]{:S(2)}) collective-permute-start(f32[4,128]{1,0:T(4,128)S(1)} %slice_select_fusion), channel_id=1, source_target_pairs={{0,8},{8,0},{1,9},{9,1},{2,10},{10,2},{3,11},{11,3},{4,12},{12,4},... | collective-permute-start | bytes 6152 | tf_op jit(solution)/shard_map/ppermute | solution.py:307
  173.0 6.0 %collective-permute-start.14 = (bf16[128,256]{1,0:T(8,128)(2,1)S(1)}, bf16[128,256]{1,0:T(8,128)(2,1)S(1)}, u32[]{:S(2)}, u32[]{:S(2)}) collective-permute-start(bf16[128,256]{1,0:T(8,128)(2,1)S(1)} %select_select_fusion.1), channel_id=1, source_target_pairs={{312,296},{376,360},{440,424},{504,488},{313,297},{377,361},{441,4... | collective-permute-start | bytes 196616 | tf_op jit(solution)/shard_map/ppermute | solution.py:248
  173.7 5.3 %collective-permute-start.15 = (bf16[128,256]{1,0:T(8,128)(2,1)S(1)}, bf16[128,256]{1,0:T(8,128)(2,1)S(1)}, u32[]{:S(2)}, u32[]{:S(2)}) collective-permute-start(bf16[128,256]{1,0:T(8,128)(2,1)S(1)} %select_select_fusion.1), channel_id=1, source_target_pairs={{312,280},{376,344},{440,408},{504,472},{313,281},{377,345},{441,4... | collective-permute-start | bytes 196616 | tf_op jit(solution)/shard_map/ppermute | solution.py:248
  174.4 4.7 %collective-permute-start.16 = (bf16[128,256]{1,0:T(8,128)(2,1)S(1)}, bf16[128,256]{1,0:T(8,128)(2,1)S(1)}, u32[]{:S(2)}, u32[]{:S(2)}) collective-permute-start(bf16[128,256]{1,0:T(8,128)(2,1)S(1)} %select_select_fusion.1), channel_id=1, source_target_pairs={{312,264},{376,328},{440,392},{504,456},{313,265},{377,329},{441,3... | collective-permute-start | bytes 196616 | tf_op jit(solution)/shard_map/ppermute | solution.py:248
  176.4 9.2 %collective-permute-start.1 = (bf16[128,256]{1,0:T(8,128)(2,1)S(1)}, bf16[128,256]{1,0:T(8,128)(2,1)S(1)}, u32[]{:S(2)}, u32[]{:S(2)}) collective-permute-start(bf16[128,256]{1,0:T(8,128)(2,1)S(1)} %add_convert_fusion), channel_id=1, source_target_pairs={{0,8},{8,16},{16,24},{24,32},{32,40},{40,48},{48,56},{56,64},{64,7... | collective-permute-start | bytes 196616 | tf_op jit(solution)/shard_map/ppermute | solution.py:327
  179.1 7.3 %collective-permute-start.17 = (bf16[128,256]{1,0:T(8,128)(2,1)S(1)}, bf16[128,256]{1,0:T(8,128)(2,1)S(1)}, u32[]{:S(2)}, u32[]{:S(2)}) collective-permute-start(bf16[128,256]{1,0:T(8,128)(2,1)S(1)} %select_select_fusion), channel_id=1, source_target_pairs={{264,256},{280,272},{296,288},{312,304},{328,320},{344,336},{360,3... | collective-permute-start | bytes 196616 | tf_op jit(solution)/shard_map/ppermute | solution.py:252
Sparse Core Ops, SparseCore 0:
  10.1 40.9 all-gather.7
  53.9 48.3 reduce-scatter.3
  105.1 30.9 reduce-scatter.5
  139.0 29.9 reduce-scatter.7
  171.5 37.4 all-gather.9

commit v5 on v4

--- a/solution.py
+++ b/solution.py
@@ -153,9 +153,8 @@
     tick_kernel(1, half, section, x, fresh, gain, final, wq, wkv, wo, cache, out, None, *scratch)
 
 
-def share_kernel(half, section, grads_hbm, wkv_hbm, out_hbm, grads, wkv, total, out, sems):
+def share_kernel(half, section, grads_hbm, wkv_hbm, out_hbm, grads, wkv, out, sems):
     width = wkv.shape[2]
-    heads, ys, each, xz, _ = out.shape
 
     @pl.when(section[0] >= half)
     def _():
@@ -166,14 +165,9 @@
         get_grads.wait()
         get_wkv.wait()
         rows_by = (((1,), (1,)), ((), ()))
-        total[...] = lax.dot_general(
+        out[...] = lax.dot_general(
             wkv[0], grads[:, :width], rows_by, preferred_element_type=F32
         ) + lax.dot_general(wkv[1], grads[:, width:], rows_by, preferred_element_type=F32)
-        for h in range(heads):
-            for y in range(ys):
-                for i in range(each):
-                    first = y * xz * heads * each + h * each + i
-                    out[h, y, i] = total[pl.ds(first, xz, stride=heads * each), :]
 
     @pl.when(section[0] < half)
     def _():
@@ -234,7 +228,7 @@
     )(section, *operands)
 
 
-def spread(block, source):
+def spread(block, source, beside):
     y, x, zl = lax.axis_index("y"), lax.axis_index("x"), lax.axis_index("zl")
     sy, sx, sz = source // (X * ZL), source // ZL % X, source % ZL
     held = block
@@ -246,10 +240,12 @@
         if to != sx:
             pairs = [(place(k, sx, sz), place(k, to, sz)) for k in range(sy + 1, Y)]
             held = jnp.where(x == to, lax.ppermute(column, PIPE, pairs), held)
+    if beside is not None:
+        held, beside = lax.optimization_barrier((held, beside))
     pairs = [
         (place(k, to, sz), place(k, to, 1 - sz)) for k in range(sy + 1, Y) for to in range(X)
     ]
-    return jnp.where(zl == sz, held, lax.ppermute(held, PIPE, pairs))
+    return jnp.where(zl == sz, held, lax.ppermute(held, PIPE, pairs)), beside
 
 
 def body(stream, fresh, gain, final_gain, w_query, w_kv, w_out, cache_kv, cache_grad):
@@ -287,28 +283,18 @@
         8 + heads, flops,
     )
 
-    each = depth // (pipe_count * heads)
-    shares = (heads, Y, each, X * ZL, tokens)
     (share,) = call(
-        functools.partial(share_kernel, half), section, (cache_grad, w_kv), (shares,),
-        ((pair_shape, BF), ((2, depth, width), BF), ((depth, tokens), F32), (shares, F32)),
+        functools.partial(share_kernel, half), section, (cache_grad, w_kv), ((depth, tokens),),
+        ((pair_shape, BF), ((2, depth, width), BF), ((depth, tokens), F32)),
         3, flops, F32,
     )
-    share = share.reshape(depth, tokens)
-    share = lax.psum_scatter(share, HEAD, scatter_dimension=0, tiled=True)
     share = lax.psum_scatter(share, "y", scatter_dimension=0, tiled=True)
-    share = share.reshape(each, X, ZL, tokens).transpose(1, 2, 0, 3).reshape(X, 1, ZL * each, tokens)
-    share = jnp.broadcast_to(share, (X, 8, ZL * each, tokens)).reshape(-1, tokens)
-    share = lax.psum_scatter(share, "x", scatter_dimension=0, tiled=True)
-    share = share[: ZL * each].reshape(ZL, each, tokens)
-    at_first = lax.axis_index("zl") == 0
-    kept = jnp.where(at_first, share[0], share[1])
-    given = jnp.where(at_first, share[1], share[0])
-    memory_grad = kept + lax.ppermute(given, "zl", [(0, 1), (1, 0)])
+    plane = X * ZL * heads
+    share = share.reshape(plane, depth // (pipe_count * heads), tokens)
 
     output = summed(exchanged(parts), current)
     passed = lax.ppermute(output, PIPE, shift)
-    first_memory = spread(output, half - 1)
+    first_memory, _ = spread(output, half - 1, None)
     entering = output
 
     current = jnp.where(place_here == 0, fresh_rows[0], passed)
@@ -321,15 +307,19 @@
         8 + heads, flops,
     )
     current = jnp.where(place_here == half, fresh_rows[1], current)
-    output = summed(exchanged(parts), current)
-    second_memory = spread(output, half - 1)
+    parts, first_memory = lax.optimization_barrier((exchanged(parts), first_memory))
+    output = summed(parts, current)
+    second_memory, share = spread(output, half - 1, share)
+    share = lax.all_to_all(share, PIPE[1:] + HEAD, 0, 0, tiled=True)
     first_memory = whole(jnp.stack([first_memory, entering]))
     passed = lax.ppermute(output, PIPE, shift)
     last = jnp.where(place_here == half, jnp.zeros_like(passed), passed)
+    share, second_memory = lax.optimization_barrier((share, whole(second_memory)))
+    memory_grad = jnp.sum(share, axis=0)
 
     (new_kv,) = call(
         functools.partial(memory_kernel, half), section,
-        (first_memory, whole(second_memory), final_scale, w_kv),
+        (first_memory, second_memory, final_scale, w_kv),
         ((1, TICKS, tokens, 2 * width),),
         (((TICKS,) + rows8, BF), ((TICKS,) + rows8, BF), ((1, depth), F32),
          ((2, depth, width), BF), ((TICKS,) + pair_shape, BF)),

time: 222 us -> 174 us (0.78)
  the two profiles are of different devices: /device:TPU:33 before, /device:TPU:41 now
where the time goes in v5:
time: 174 us; the launch traced here: 173 us
  blocking collectives  60 us (34%)
  waiting for transfers between devices  41.2 us (24%)
  starting transfers between devices  38.6 us (22%)
  between operations  15.9 us (9%)
  Pallas kernels  13.9 us (8%)
    all_gather x3, blocking collectives, whole(): return lax.all_gather(block, HEAD, axis=0)  60 us
    pallas_call x4, Pallas kernels, call(): pl.pallas_call(kernel, out_shape=[jax.ShapeDtypeStruct(shape, kind) for s...  13.9 us
    all_to_all x2, waiting for transfers between devices, exchanged(): return lax.all_to_all(parts, HEAD, 0, 0, tiled=True)  13.5 us
    ppermute x2, waiting for transfers between devices, body(): passed = lax.ppermute(output, PIPE, shift)  13.5 us
    ppermute x2, waiting for transfers between devices, spread(): return (jnp.where(zl == sz, held, lax.ppermute(held, PIPE, pairs)), beside)  13.3 us
    all_to_all x1, starting transfers between devices, body(): share = lax.all_to_all(share, PIPE[1:] + HEAD, 0, 0, tiled=True)  11 us
    all_to_all x2, starting transfers between devices, exchanged(): return lax.all_to_all(parts, HEAD, 0, 0, tiled=True)  9.85 us
    ppermute x2, starting transfers between devices, body(): passed = lax.ppermute(output, PIPE, shift)  5.84 us
  transfers between devices with their start and end apart: 24, of which 4 were waited for; matrix products, arithmetic and copies ran while one was open for 2% of the time, Pallas kernels for 6%

profile of v5, /device:TPU:41, one launch (start us, length us, event | category | flops | bytes accessed | tf_op | source)
XLA Modules:
  0.0 172.9 jit_solution(4244537828869542022)
XLA Ops:
  8.0 0.0 all-gather.8.cloned.1.call-start
  8.0 0.7 all-gather.8.cloned.1.call-update
  8.7 0.9 copy.14
  9.7 22.2 %all-gather = bf16[1024,256]{1,0:T(8,128)(2,1)} all-gather(bf16[128,256]{1,0:T(8,128)(2,1)S(1)} %bitcast.29), channel_id=2, replica_groups=mesh['y'=8,'x'=4,'zl'=2,'zh'=4,'c'=2] {'zh','c'}, dimensions={0}, use_global_device_ids=true | all-gather | bytes 589824 | tf_op jit(solution)/shard_map/all_gather | solution.py:266
  31.9 3.8 %shard_map.112 = (bf16[8,128,256]{2,1,0:T(8,128)(2,1)}, bf16[2,128,256]{2,1,0:T(8,128)(2,1)}) custom-call(s32[1]{0:T(128)} %bitcast.section, bf16[8,128,256]{2,1,0:T(8,128)(2,1)} %bitcast.26, bf16[2,256,128]{2,1,0:T(8,128)(2,1)} %fresh.1, f32[1,2048]{1,0:T(1,128)} %gain.3, bf16[1,2048,256]{2,1,0:T(8,128)(2,1)} %wq.3, bf16[1,2,2048,256]{3,2,1,0:T(8,128)(2,1)} %wkv_hbm.3, ...), custom_call_target="tpu_custom_call" | custom-call | flops 536870912 | bytes 5000000 | tf_op jit(solution)/shard_map/pallas_call | solution.py:218
  35.6 5.3 %all-to-all-start = ((bf16[8,128,256]{2,1,0:T(8,128)(2,1)}), bf16[8,128,256]{2,1,0:T(8,128)(2,1)S(1)}, u32[]{:S(2)}, u32[]{:S(2)}) async-start(bf16[8,128,256]{2,1,0:T(8,128)(2,1)} %get-tuple-element.12), calls=%async_computation | async-start | bytes 1048576 | tf_op jit(solution)/shard_map/all_to_all | solution.py:269
  40.9 0.0 reduce-scatter.2.cloned.1.call-start
  40.9 3.4 %shard_map.114 = f32[2048,128]{1,0:T(8,128)} custom-call(s32[1]{0:T(128)} %bitcast.section, bf16[1,128,512]{2,1,0:T(8,128)(2,1)} %grads_hbm.1, bf16[1,2,2048,256]{3,2,1,0:T(8,128)(2,1)} %wkv_hbm.3), custom_call_target="tpu_custom_call" | custom-call | flops 536870912 | bytes 5000000 | tf_op jit(solution)/shard_map/pallas_call | solution.py:218
  44.3 0.0 reduce-scatter.2.cloned.1.call-update
  44.3 13.5 %all-to-all-done = bf16[8,128,256]{2,1,0:T(8,128)(2,1)S(1)} async-done(((bf16[8,128,256]{2,1,0:T(8,128)(2,1)}), bf16[8,128,256]{2,1,0:T(8,128)(2,1)S(1)}, u32[]{:S(2)}, u32[]{:S(2)}) %all-to-all-start) | async-done | bytes 524320 | tf_op jit(solution)/shard_map/all_to_all | solution.py:269
  57.9 0.1 convert_reduce_fusion.1
  58.0 3.6 %collective-permute-start = (bf16[128,256]{1,0:T(8,128)(2,1)S(1)}, bf16[128,256]{1,0:T(8,128)(2,1)S(1)}, u32[]{:S(2)}, u32[]{:S(2)}) collective-permute-start(bf16[128,256]{1,0:T(8,128)(2,1)S(1)} %add_convert_fusion.1), channel_id=1, source_target_pairs={{0,8},{8,16},{16,24},{24,32},{32,40},{40,48},{48,56},{56,64},{64,7... | collective-permute-start | bytes 196616 | tf_op jit(solution)/shard_map/ppermute | solution.py:296
  61.6 4.7 %collective-permute-done = bf16[128,256]{1,0:T(8,128)(2,1)S(1)} collective-permute-done((bf16[128,256]{1,0:T(8,128)(2,1)S(1)}, bf16[128,256]{1,0:T(8,128)(2,1)S(1)}, u32[]{:S(2)}, u32[]{:S(2)}) %collective-permute-start) | collective-permute-done | bytes 65568 | tf_op jit(solution)/shard_map/ppermute | solution.py:296
  66.3 0.0 copy-done
  66.3 18.7 %all-gather.1 = bf16[1024,256]{1,0:T(8,128)(2,1)} all-gather(bf16[128,256]{1,0:T(8,128)(2,1)S(1)} %bitcast_select_fusion), channel_id=3, replica_groups=mesh['y'=8,'x'=4,'zl'=2,'zh'=4,'c'=2] {'zh','c'}, dimensions={0}, use_global_device_ids=true | all-gather | bytes 589824 | tf_op jit(solution)/shard_map/all_gather | solution.py:266
  85.1 0.0 all-gather.8.cloned.1.call-done
  85.1 3.3 %shard_map.113 = bf16[8,128,256]{2,1,0:T(8,128)(2,1)} custom-call(s32[1]{0:T(128)} %bitcast.section, bf16[8,128,256]{2,1,0:T(8,128)(2,1)} %bitcast.25, bf16[8,2,256,128]{3,2,1,0:T(8,128)(2,1)} %bitcast.28, f32[1,2048]{1,0:T(1,128)} %gain.3, f32[1,2048]{1,0:T(1,128)} %bitcast.33, bf16[1,2048,256]{2,1,0:T(8,128)(2,1)} %wq.3, ...), custom_call_target="tpu_custom_call" | custom-call | flops 536870912 | bytes 5000000 | tf_op jit(solution)/shard_map/pallas_call | solution.py:218
  88.4 4.6 %all-to-all-start.1 = ((bf16[8,128,256]{2,1,0:T(8,128)(2,1)}), bf16[8,128,256]{2,1,0:T(8,128)(2,1)S(1)}, u32[]{:S(2)}, u32[]{:S(2)}) async-start(bf16[8,128,256]{2,1,0:T(8,128)(2,1)} %shard_map.113), calls=%async_computation.1 | async-start | bytes 1048576 | tf_op jit(solution)/shard_map/all_to_all | solution.py:269
  93.0 0.0 all-gather.10.cloned.1.call-start
  93.0 0.7 collective-permute-start.1
  93.6 0.7 collective-permute-start.2
  94.3 0.7 collective-permute-start.3
  95.0 0.7 collective-permute-start.4
  95.7 0.0 collective-permute-done.1
  95.7 0.0 collective-permute-done.2
  95.7 0.0 collective-permute-done.3
  95.7 0.0 collective-permute-done.4
  95.7 0.7 collective-permute-start.5
  96.4 0.7 collective-permute-start.6
  97.1 0.7 collective-permute-start.7
  97.8 0.0 collective-permute-done.5
  97.8 0.0 collective-permute-done.6
  97.8 0.0 collective-permute-done.7
  97.8 1.3 collective-permute-start.8
  99.1 13.3 %collective-permute-done.8 = bf16[128,256]{1,0:T(8,128)(2,1)S(1)} collective-permute-done((bf16[128,256]{1,0:T(8,128)(2,1)S(1)}, bf16[128,256]{1,0:T(8,128)(2,1)S(1)}, u32[]{:S(2)}, u32[]{:S(2)}) %collective-permute-start.8) | collective-permute-done | bytes 65568 | tf_op jit(solution)/shard_map/ppermute | solution.py:248
  112.5 0.0 all-to-all-done.1
  112.5 0.7 pad_maximum_fusion
  113.1 0.0 all-gather.10.cloned.1.call-update
  113.2 0.1 convert_reduce_fusion
  113.3 0.7 collective-permute-start.10
  114.0 0.7 collective-permute-start.11
  114.6 0.7 collective-permute-start.12
  115.3 0.7 collective-permute-start.13
  116.0 0.0 collective-permute-done.10
  116.0 0.0 collective-permute-done.11
  116.0 0.0 collective-permute-done.12
  116.0 0.0 collective-permute-done.13
  116.0 0.7 collective-permute-start.14
  116.7 0.7 collective-permute-start.15
  117.4 0.7 collective-permute-start.16
  118.1 2.2 %collective-permute-start.9 = (bf16[128,256]{1,0:T(8,128)(2,1)S(1)}, bf16[128,256]{1,0:T(8,128)(2,1)S(1)}, u32[]{:S(2)}, u32[]{:S(2)}) collective-permute-start(bf16[128,256]{1,0:T(8,128)(2,1)S(1)} %add_convert_fusion), channel_id=1, source_target_pairs={{0,8},{8,16},{16,24},{24,32},{32,40},{40,48},{48,56},{56,64},{64,7... | collective-permute-start | bytes 196616 | tf_op jit(solution)/shard_map/ppermute | solution.py:315
  120.3 0.0 collective-permute-done.14
  120.3 0.0 collective-permute-done.15
  120.3 0.0 collective-permute-done.16
  120.3 0.0 reduce-scatter.2.cloned.1.call-done
  120.4 1.3 collective-permute-start.17
  121.7 8.8 %collective-permute-done.9 = bf16[128,256]{1,0:T(8,128)(2,1)S(1)} collective-permute-done((bf16[128,256]{1,0:T(8,128)(2,1)S(1)}, bf16[128,256]{1,0:T(8,128)(2,1)S(1)}, u32[]{:S(2)}, u32[]{:S(2)}) %collective-permute-start.9) | collective-permute-done | bytes 65568 | tf_op jit(solution)/shard_map/ppermute | solution.py:315
  130.5 0.7 copy.15
  131.2 11.0 %all-to-all-start.2 = ((f32[64,4,128]{2,1,0:T(4,128)}), f32[64,4,128]{2,1,0:T(4,128)S(1)}, u32[]{:S(2)}, u32[]{:S(2)}) async-start(f32[64,4,128]{2,1,0:T(4,128)} %bitcast.32), calls=%async_computation.3 | async-start | bytes 262144 | tf_op jit(solution)/shard_map/all_to_all | solution.py:313
  142.2 0.0 collective-permute-done.17
  142.2 19.1 %all-gather.4 = bf16[1024,256]{1,0:T(8,128)(2,1)} all-gather(bf16[128,256]{1,0:T(8,128)(2,1)S(1)} %broadcast_select_fusion), channel_id=6, replica_groups=mesh['y'=8,'x'=4,'zl'=2,'zh'=4,'c'=2] {'zh','c'}, dimensions={0}, use_global_device_ids=true | all-gather | bytes 589824 | tf_op jit(solution)/shard_map/all_gather | solution.py:266
  161.4 0.0 all-to-all-done.2
  161.4 0.7 reduce_sum.29
  162.0 3.4 %shard_map.115 = bf16[1,2,128,512]{3,2,1,0:T(8,128)(2,1)} custom-call(s32[1]{0:T(128)} %bitcast.section, bf16[8,2,128,256]{3,2,1,0:T(8,128)(2,1)} %bitcast.27, bf16[8,128,256]{2,1,0:T(8,128)(2,1)} %bitcast.24, f32[1,2048]{1,0:T(1,128)} %bitcast.34, bf16[1,2,2048,256]{3,2,1,0:T(8,128)(2,1)} %wkv_hbm.3), custom_call_target="tpu_custom_call" | custom-call | flops 536870912 | bytes 5000000 | tf_op jit(solution)/shard_map/pallas_call | solution.py:218
  (12 shorter events, 0.2 us)
Async XLA Ops:
  8.0 77.1 %all-gather.8.cloned.1.call-start = ((), (), s32[]{:S(2)}) async-start(), calls=%async_computation.5 | async-start | bytes 1179648 | tf_op jit(solution)/shard_map/all_gather | solution.py:266
  35.6 22.2 %all-to-all-start = ((bf16[8,128,256]{2,1,0:T(8,128)(2,1)}), bf16[8,128,256]{2,1,0:T(8,128)(2,1)S(1)}, u32[]{:S(2)}, u32[]{:S(2)}) async-start(bf16[8,128,256]{2,1,0:T(8,128)(2,1)} %get-tuple-element.12), calls=%async_computation | async-start | bytes 1048576 | tf_op jit(solution)/shard_map/all_to_all | solution.py:269
  40.9 25.4 %copy-start = (bf16[2,128,256]{2,1,0:T(8,128)(2,1)S(1)}, bf16[2,128,256]{2,1,0:T(8,128)(2,1)}, u32[]{:S(2)}) copy-start(bf16[2,128,256]{2,1,0:T(8,128)(2,1)} %get-tuple-element.11) | copy-start | bytes 393220
  40.9 79.5 %reduce-scatter.2.cloned.1.call-start = ((), (), s32[]{:S(2)}) async-start(), calls=%async_computation.4 | async-start | bytes 1179648 | tf_op jit(solution)/shard_map/reduce_scatter | solution.py:291
  58.0 8.3 %collective-permute-start = (bf16[128,256]{1,0:T(8,128)(2,1)S(1)}, bf16[128,256]{1,0:T(8,128)(2,1)S(1)}, u32[]{:S(2)}, u32[]{:S(2)}) collective-permute-start(bf16[128,256]{1,0:T(8,128)(2,1)S(1)} %add_convert_fusion.1), channel_id=1, source_target_pairs={{0,8},{8,16},{16,24},{24,32},{32,40},{40,48},{48,56},{56,64},{64,7... | collective-permute-start | bytes 196616 | tf_op jit(solution)/shard_map/ppermute | solution.py:296
  88.4 24.1 %all-to-all-start.1 = ((bf16[8,128,256]{2,1,0:T(8,128)(2,1)}), bf16[8,128,256]{2,1,0:T(8,128)(2,1)S(1)}, u32[]{:S(2)}, u32[]{:S(2)}) async-start(bf16[8,128,256]{2,1,0:T(8,128)(2,1)} %shard_map.113), calls=%async_computation.1 | async-start | bytes 1048576 | tf_op jit(solution)/shard_map/all_to_all | solution.py:269
  93.0 69.0 %all-gather.10.cloned.1.call-start = ((), (), s32[]{:S(2)}) async-start(), calls=%async_computation.6 | async-start | bytes 1179648 | tf_op jit(solution)/shard_map/all_gather | solution.py:266
  93.0 2.7 %collective-permute-start.1 = (bf16[128,256]{1,0:T(8,128)(2,1)S(1)}, bf16[128,256]{1,0:T(8,128)(2,1)S(1)}, u32[]{:S(2)}, u32[]{:S(2)}) collective-permute-start(bf16[128,256]{1,0:T(8,128)(2,1)S(1)} %add_convert_fusion.1), channel_id=1, source_target_pairs={{248,504},{249,505},{250,506},{251,507},{252,508},{253,509},{254,5... | collective-permute-start | bytes 196616 | tf_op jit(solution)/shard_map/ppermute | solution.py:236
  93.6 2.0 %collective-permute-start.2 = (bf16[128,256]{1,0:T(8,128)(2,1)S(1)}, bf16[128,256]{1,0:T(8,128)(2,1)S(1)}, u32[]{:S(2)}, u32[]{:S(2)}) collective-permute-start(bf16[128,256]{1,0:T(8,128)(2,1)S(1)} %add_convert_fusion.1), channel_id=1, source_target_pairs={{248,440},{249,441},{250,442},{251,443},{252,444},{253,445},{254,4... | collective-permute-start | bytes 196616 | tf_op jit(solution)/shard_map/ppermute | solution.py:236
  94.3 1.4 collective-permute-start.3
  95.0 0.7 collective-permute-start.4
  95.7 2.0 %collective-permute-start.5 = (bf16[128,256]{1,0:T(8,128)(2,1)S(1)}, bf16[128,256]{1,0:T(8,128)(2,1)S(1)}, u32[]{:S(2)}, u32[]{:S(2)}) collective-permute-start(bf16[128,256]{1,0:T(8,128)(2,1)S(1)} %select_select_fusion.3), channel_id=1, source_target_pairs={{312,296},{376,360},{440,424},{504,488},{313,297},{377,361},{441,4... | collective-permute-start | bytes 196616 | tf_op jit(solution)/shard_map/ppermute | solution.py:242
  96.4 1.4 collective-permute-start.6
  97.1 0.7 collective-permute-start.7
  97.8 14.6 %collective-permute-start.8 = (bf16[128,256]{1,0:T(8,128)(2,1)S(1)}, bf16[128,256]{1,0:T(8,128)(2,1)S(1)}, u32[]{:S(2)}, u32[]{:S(2)}) collective-permute-start(bf16[128,256]{1,0:T(8,128)(2,1)S(1)} %select_select_fusion.2), channel_id=1, source_target_pairs={{264,256},{280,272},{296,288},{312,304},{328,320},{344,336},{360,3... | collective-permute-start | bytes 196616 | tf_op jit(solution)/shard_map/ppermute | solution.py:248
  113.3 2.7 %collective-permute-start.10 = (bf16[128,256]{1,0:T(8,128)(2,1)S(1)}, bf16[128,256]{1,0:T(8,128)(2,1)S(1)}, u32[]{:S(2)}, u32[]{:S(2)}) collective-permute-start(bf16[128,256]{1,0:T(8,128)(2,1)S(1)} %add_convert_fusion), channel_id=1, source_target_pairs={{248,504},{249,505},{250,506},{251,507},{252,508},{253,509},{254,5... | collective-permute-start | bytes 196616 | tf_op jit(solution)/shard_map/ppermute | solution.py:236
  114.0 2.0 %collective-permute-start.11 = (bf16[128,256]{1,0:T(8,128)(2,1)S(1)}, bf16[128,256]{1,0:T(8,128)(2,1)S(1)}, u32[]{:S(2)}, u32[]{:S(2)}) collective-permute-start(bf16[128,256]{1,0:T(8,128)(2,1)S(1)} %add_convert_fusion), channel_id=1, source_target_pairs={{248,440},{249,441},{250,442},{251,443},{252,444},{253,445},{254,4... | collective-permute-start | bytes 196616 | tf_op jit(solution)/shard_map/ppermute | solution.py:236
  114.6 1.4 collective-permute-start.12
  115.3 0.7 collective-permute-start.13
  116.0 4.2 %collective-permute-start.14 = (bf16[128,256]{1,0:T(8,128)(2,1)S(1)}, bf16[128,256]{1,0:T(8,128)(2,1)S(1)}, u32[]{:S(2)}, u32[]{:S(2)}) collective-permute-start(bf16[128,256]{1,0:T(8,128)(2,1)S(1)} %select_select_fusion.1), channel_id=1, source_target_pairs={{312,296},{376,360},{440,424},{504,488},{313,297},{377,361},{441,4... | collective-permute-start | bytes 196616 | tf_op jit(solution)/shard_map/ppermute | solution.py:242
  116.7 3.6 %collective-permute-start.15 = (bf16[128,256]{1,0:T(8,128)(2,1)S(1)}, bf16[128,256]{1,0:T(8,128)(2,1)S(1)}, u32[]{:S(2)}, u32[]{:S(2)}) collective-permute-start(bf16[128,256]{1,0:T(8,128)(2,1)S(1)} %select_select_fusion.1), channel_id=1, source_target_pairs={{312,280},{376,344},{440,408},{504,472},{313,281},{377,345},{441,4... | collective-permute-start | bytes 196616 | tf_op jit(solution)/shard_map/ppermute | solution.py:242
  117.4 2.9 %collective-permute-start.16 = (bf16[128,256]{1,0:T(8,128)(2,1)S(1)}, bf16[128,256]{1,0:T(8,128)(2,1)S(1)}, u32[]{:S(2)}, u32[]{:S(2)}) collective-permute-start(bf16[128,256]{1,0:T(8,128)(2,1)S(1)} %select_select_fusion.1), channel_id=1, source_target_pairs={{312,264},{376,328},{440,392},{504,456},{313,265},{377,329},{441,3... | collective-permute-start | bytes 196616 | tf_op jit(solution)/shard_map/ppermute | solution.py:242
  118.1 12.4 %collective-permute-start.9 = (bf16[128,256]{1,0:T(8,128)(2,1)S(1)}, bf16[128,256]{1,0:T(8,128)(2,1)S(1)}, u32[]{:S(2)}, u32[]{:S(2)}) collective-permute-start(bf16[128,256]{1,0:T(8,128)(2,1)S(1)} %add_convert_fusion), channel_id=1, source_target_pairs={{0,8},{8,16},{16,24},{24,32},{32,40},{40,48},{48,56},{56,64},{64,7... | collective-permute-start | bytes 196616 | tf_op jit(solution)/shard_map/ppermute | solution.py:315
  120.4 21.8 %collective-permute-start.17 = (bf16[128,256]{1,0:T(8,128)(2,1)S(1)}, bf16[128,256]{1,0:T(8,128)(2,1)S(1)}, u32[]{:S(2)}, u32[]{:S(2)}) collective-permute-start(bf16[128,256]{1,0:T(8,128)(2,1)S(1)} %select_select_fusion), channel_id=1, source_target_pairs={{264,256},{280,272},{296,288},{312,304},{328,320},{344,336},{360,3... | collective-permute-start | bytes 196616 | tf_op jit(solution)/shard_map/ppermute | solution.py:248
  131.2 30.1 %all-to-all-start.2 = ((f32[64,4,128]{2,1,0:T(4,128)}), f32[64,4,128]{2,1,0:T(4,128)S(1)}, u32[]{:S(2)}, u32[]{:S(2)}) async-start(f32[64,4,128]{2,1,0:T(4,128)} %bitcast.32), calls=%async_computation.3 | async-start | bytes 262144 | tf_op jit(solution)/shard_map/all_to_all | solution.py:313
Sparse Core Ops, SparseCore 0:
  11.0 42.5 all-gather.7
  113.3 36.0 all-gather.9
Sparse Core Ops, SparseCore 1:
  44.4 35.2 reduce-scatter.1

commit v6 on v5

--- a/solution.py
+++ b/solution.py
@@ -228,23 +228,21 @@
     )(section, *operands)
 
 
-def spread(block, source, beside):
+def spread(block, source, rows, beside):
     y, x, zl = lax.axis_index("y"), lax.axis_index("x"), lax.axis_index("zl")
     sy, sx, sz = source // (X * ZL), source // ZL % X, source % ZL
     held = block
-    for to in range(sy + 1, Y):
-        sent = lax.ppermute(block, PIPE, [(source, place(to, sx, sz))])
-        held = jnp.where(y == to, sent, held)
-    column = held
+    for to in rows:
+        if to != sy:
+            sent = lax.ppermute(block, PIPE, [(source, place(to, sx, sz))])
+            held = jnp.where(y == to, sent, held)
+    column, beside = lax.optimization_barrier((held, beside))
+    held = column
     for to in range(X):
         if to != sx:
-            pairs = [(place(k, sx, sz), place(k, to, sz)) for k in range(sy + 1, Y)]
+            pairs = [(place(k, sx, sz), place(k, to, sz)) for k in rows]
             held = jnp.where(x == to, lax.ppermute(column, PIPE, pairs), held)
-    if beside is not None:
-        held, beside = lax.optimization_barrier((held, beside))
-    pairs = [
-        (place(k, to, sz), place(k, to, 1 - sz)) for k in range(sy + 1, Y) for to in range(X)
-    ]
+    pairs = [(place(k, to, sz), place(k, to, 1 - sz)) for k in rows for to in range(X)]
     return jnp.where(zl == sz, held, lax.ppermute(held, PIPE, pairs)), beside
 
 
@@ -294,10 +292,11 @@
 
     output = summed(exchanged(parts), current)
     passed = lax.ppermute(output, PIPE, shift)
-    first_memory, _ = spread(output, half - 1, None)
     entering = output
 
+    rows = range(half // (X * ZL), Y)
     current = jnp.where(place_here == 0, fresh_rows[0], passed)
+    first_memory, current = spread(passed, half, rows, current)
     (parts,) = call(
         functools.partial(second_kernel, half), section,
         (whole(current), fresh_whole, gain, final_scale, w_query, w_kv, w_out, cache_kv),
@@ -309,7 +308,7 @@
     current = jnp.where(place_here == half, fresh_rows[1], current)
     parts, first_memory = lax.optimization_barrier((exchanged(parts), first_memory))
     output = summed(parts, current)
-    second_memory, share = spread(output, half - 1, share)
+    second_memory, share = spread(output, half - 1, rows, share)
     share = lax.all_to_all(share, PIPE[1:] + HEAD, 0, 0, tiled=True)
     first_memory = whole(jnp.stack([first_memory, entering]))
     passed = lax.ppermute(output, PIPE, shift)

time: 174 us -> 179 us (1.029)
  the two profiles are of different devices: /device:TPU:41 before, /device:TPU:39 now
where the time goes in v6:
time: 179 us; the launch traced here: 178 us
  blocking collectives  59.7 us (33%)
  starting transfers between devices  53.4 us (30%)
  waiting for transfers between devices  32 us (18%)
  between operations  15.9 us (9%)
  Pallas kernels  13.9 us (8%)
    all_gather x3, blocking collectives, whole(): return lax.all_gather(block, HEAD, axis=0)  59.7 us
    all_to_all x1, starting transfers between devices, body(): share = lax.all_to_all(share, PIPE[1:] + HEAD, 0, 0, tiled=True)  17 us
    ppermute x2, starting transfers between devices, body(): passed = lax.ppermute(output, PIPE, shift)  14.9 us
    pallas_call x4, Pallas kernels, call(): pl.pallas_call(kernel, out_shape=[jax.ShapeDtypeStruct(shape, kind) for s...  13.9 us
    ppermute x6, waiting for transfers between devices, spread(): held = jnp.where(x == to, lax.ppermute(column, PIPE, pairs), held)  13.6 us
    all_to_all x2, waiting for transfers between devices, exchanged(): return lax.all_to_all(parts, HEAD, 0, 0, tiled=True)  13.5 us
    all_to_all x2, starting transfers between devices, exchanged(): return lax.all_to_all(parts, HEAD, 0, 0, tiled=True)  9.57 us
    ppermute x7, starting transfers between devices, spread(): sent = lax.ppermute(block, PIPE, [(source, place(to, sx, sz))])  4.64 us
  transfers between devices with their start and end apart: 23, of which 4 were waited for; matrix products, arithmetic and copies ran while one was open for 2% of the time, Pallas kernels for 6%

profile of v6, /device:TPU:39, one launch (start us, length us, event | category | flops | bytes accessed | tf_op | source)
XLA Modules:
  0.0 178.2 jit_solution(17683438752981194751)
XLA Ops:
  8.0 0.0 all-gather.8.cloned.1.call-start
  8.0 0.7 all-gather.8.cloned.1.call-update
  8.7 0.9 copy.14
  9.7 22.2 %all-gather = bf16[1024,256]{1,0:T(8,128)(2,1)} all-gather(bf16[128,256]{1,0:T(8,128)(2,1)S(1)} %bitcast.29), channel_id=2, replica_groups=mesh['y'=8,'x'=4,'zl'=2,'zh'=4,'c'=2] {'zh','c'}, dimensions={0}, use_global_device_ids=true | all-gather | bytes 589824 | tf_op jit(solution)/shard_map/all_gather | solution.py:264
  31.9 3.8 %shard_map.112 = (bf16[8,128,256]{2,1,0:T(8,128)(2,1)}, bf16[2,128,256]{2,1,0:T(8,128)(2,1)}) custom-call(s32[1]{0:T(128)} %bitcast.section, bf16[8,128,256]{2,1,0:T(8,128)(2,1)} %bitcast.26, bf16[2,256,128]{2,1,0:T(8,128)(2,1)} %fresh.1, f32[1,2048]{1,0:T(1,128)} %gain.3, bf16[1,2048,256]{2,1,0:T(8,128)(2,1)} %wq.3, bf16[1,2,2048,256]{3,2,1,0:T(8,128)(2,1)} %wkv_hbm.3, ...), custom_call_target="tpu_custom_call" | custom-call | flops 536870912 | bytes 5000000 | tf_op jit(solution)/shard_map/pallas_call | solution.py:218
  35.6 5.3 %all-to-all-start = ((bf16[8,128,256]{2,1,0:T(8,128)(2,1)}), bf16[8,128,256]{2,1,0:T(8,128)(2,1)S(1)}, u32[]{:S(2)}, u32[]{:S(2)}) async-start(bf16[8,128,256]{2,1,0:T(8,128)(2,1)} %get-tuple-element.14), calls=%async_computation | async-start | bytes 1048576 | tf_op jit(solution)/shard_map/all_to_all | solution.py:267
  40.9 0.0 copy-start
  40.9 0.0 reduce-scatter.2.cloned.1.call-start
  40.9 3.4 %shard_map.114 = f32[2048,128]{1,0:T(8,128)} custom-call(s32[1]{0:T(128)} %bitcast.section, bf16[1,128,512]{2,1,0:T(8,128)(2,1)} %grads_hbm.1, bf16[1,2,2048,256]{3,2,1,0:T(8,128)(2,1)} %wkv_hbm.3), custom_call_target="tpu_custom_call" | custom-call | flops 536870912 | bytes 5000000 | tf_op jit(solution)/shard_map/pallas_call | solution.py:218
  44.3 0.0 reduce-scatter.2.cloned.1.call-update
  44.3 13.5 %all-to-all-done = bf16[8,128,256]{2,1,0:T(8,128)(2,1)S(1)} async-done(((bf16[8,128,256]{2,1,0:T(8,128)(2,1)}), bf16[8,128,256]{2,1,0:T(8,128)(2,1)S(1)}, u32[]{:S(2)}, u32[]{:S(2)}) %all-to-all-start) | async-done | bytes 524320 | tf_op jit(solution)/shard_map/all_to_all | solution.py:267
  57.9 0.1 convert_reduce_fusion.1
  58.0 3.1 %collective-permute-start = (bf16[128,256]{1,0:T(8,128)(2,1)S(1)}, bf16[128,256]{1,0:T(8,128)(2,1)S(1)}, u32[]{:S(2)}, u32[]{:S(2)}) collective-permute-start(bf16[128,256]{1,0:T(8,128)(2,1)S(1)} %add_convert_fusion.1), channel_id=1, source_target_pairs={{0,8},{8,16},{16,24},{24,32},{32,40},{40,48},{48,56},{56,64},{64,7... | collective-permute-start | bytes 196616 | tf_op jit(solution)/shard_map/ppermute | solution.py:294
  61.1 2.8 %collective-permute-done = bf16[128,256]{1,0:T(8,128)(2,1)S(1)} collective-permute-done((bf16[128,256]{1,0:T(8,128)(2,1)S(1)}, bf16[128,256]{1,0:T(8,128)(2,1)S(1)}, u32[]{:S(2)}, u32[]{:S(2)}) %collective-permute-start) | collective-permute-done | bytes 65568 | tf_op jit(solution)/shard_map/ppermute | solution.py:294
  63.9 0.7 collective-permute-start.1
  64.5 0.7 collective-permute-start.2
  65.2 0.7 collective-permute-start.3
  65.9 0.0 collective-permute-done.1
  65.9 0.0 collective-permute-done.2
  65.9 0.0 collective-permute-done.3
  65.9 0.0 copy-done
  66.0 18.5 %all-gather.1 = bf16[1024,256]{1,0:T(8,128)(2,1)} all-gather(bf16[128,256]{1,0:T(8,128)(2,1)S(1)} %get-tuple-element.15), channel_id=3, replica_groups=mesh['y'=8,'x'=4,'zl'=2,'zh'=4,'c'=2] {'zh','c'}, dimensions={0}, use_global_device_ids=true | all-gather | bytes 589824 | tf_op jit(solution)/shard_map/all_gather | solution.py:264
  84.5 0.0 all-gather.8.cloned.1.call-done
  84.5 3.3 %shard_map.113 = bf16[8,128,256]{2,1,0:T(8,128)(2,1)} custom-call(s32[1]{0:T(128)} %bitcast.section, bf16[8,128,256]{2,1,0:T(8,128)(2,1)} %bitcast.25, bf16[8,2,256,128]{3,2,1,0:T(8,128)(2,1)} %bitcast.28, f32[1,2048]{1,0:T(1,128)} %gain.3, f32[1,2048]{1,0:T(1,128)} %bitcast.33, bf16[1,2048,256]{2,1,0:T(8,128)(2,1)} %wq.3, ...), custom_call_target="tpu_custom_call" | custom-call | flops 536870912 | bytes 5000000 | tf_op jit(solution)/shard_map/pallas_call | solution.py:218
  87.9 4.3 %all-to-all-start.1 = ((bf16[8,128,256]{2,1,0:T(8,128)(2,1)}), bf16[8,128,256]{2,1,0:T(8,128)(2,1)S(1)}, u32[]{:S(2)}, u32[]{:S(2)}) async-start(bf16[8,128,256]{2,1,0:T(8,128)(2,1)} %shard_map.113), calls=%async_computation.1 | async-start | bytes 1048576 | tf_op jit(solution)/shard_map/all_to_all | solution.py:267
  92.2 0.0 all-gather.10.cloned.1.call-start
  92.2 1.3 collective-permute-start.4
  93.5 0.7 collective-permute-start.5
  94.1 0.7 collective-permute-start.6
  94.8 13.6 %collective-permute-done.4 = bf16[128,256]{1,0:T(8,128)(2,1)S(1)} collective-permute-done((bf16[128,256]{1,0:T(8,128)(2,1)S(1)}, bf16[128,256]{1,0:T(8,128)(2,1)S(1)}, u32[]{:S(2)}, u32[]{:S(2)}) %collective-permute-start.4) | collective-permute-done | bytes 65568 | tf_op jit(solution)/shard_map/ppermute | solution.py:244
  108.4 0.0 collective-permute-done.5
  108.4 0.0 collective-permute-done.6
  108.5 1.3 collective-permute-start.7
  109.8 1.3 collective-permute-done.7
  111.1 0.0 all-to-all-done.1
  111.1 0.7 pad_maximum_fusion
  111.8 0.0 all-gather.10.cloned.1.call-update
  111.8 0.1 convert_reduce_fusion
  111.9 0.7 collective-permute-start.9
  112.6 0.7 collective-permute-start.10
  113.3 0.7 collective-permute-start.11
  113.9 0.7 collective-permute-start.12
  114.6 0.0 collective-permute-done.9
  114.6 0.0 collective-permute-done.10
  114.6 0.0 collective-permute-done.11
  114.6 0.0 collective-permute-done.12
  114.7 0.0 reduce-scatter.2.cloned.1.call-done
  114.7 0.7 collective-permute-start.13
  115.4 0.7 collective-permute-start.14
  116.1 0.7 collective-permute-start.15
  116.7 11.8 %collective-permute-start.8 = (bf16[128,256]{1,0:T(8,128)(2,1)S(1)}, bf16[128,256]{1,0:T(8,128)(2,1)S(1)}, u32[]{:S(2)}, u32[]{:S(2)}) collective-permute-start(bf16[128,256]{1,0:T(8,128)(2,1)S(1)} %add_convert_fusion), channel_id=1, source_target_pairs={{0,8},{8,16},{16,24},{24,32},{32,40},{40,48},{48,56},{56,64},{64,7... | collective-permute-start | bytes 196616 | tf_op jit(solution)/shard_map/ppermute | solution.py:314
  128.5 0.0 collective-permute-done.13
  128.5 0.0 collective-permute-done.14
  128.6 0.0 collective-permute-done.15
  128.6 1.3 collective-permute-start.16
  129.9 0.0 collective-permute-done.8
  129.9 0.7 copy.15
  130.7 17.0 %all-to-all-start.2 = ((f32[64,4,128]{2,1,0:T(4,128)}), f32[64,4,128]{2,1,0:T(4,128)S(1)}, u32[]{:S(2)}, u32[]{:S(2)}) async-start(f32[64,4,128]{2,1,0:T(4,128)} %bitcast.32), calls=%async_computation.3 | async-start | bytes 262144 | tf_op jit(solution)/shard_map/all_to_all | solution.py:312
  147.7 0.0 collective-permute-done.16
  147.7 18.9 %all-gather.4 = bf16[1024,256]{1,0:T(8,128)(2,1)} all-gather(bf16[128,256]{1,0:T(8,128)(2,1)S(1)} %broadcast_select_fusion), channel_id=6, replica_groups=mesh['y'=8,'x'=4,'zl'=2,'zh'=4,'c'=2] {'zh','c'}, dimensions={0}, use_global_device_ids=true | all-gather | bytes 589824 | tf_op jit(solution)/shard_map/all_gather | solution.py:264
  166.6 0.0 all-to-all-done.2
  166.6 0.7 reduce_sum.29
  167.3 0.0 all-gather.10.cloned.1.call-done
  167.3 3.4 %shard_map.115 = bf16[1,2,128,512]{3,2,1,0:T(8,128)(2,1)} custom-call(s32[1]{0:T(128)} %bitcast.section, bf16[8,2,128,256]{3,2,1,0:T(8,128)(2,1)} %bitcast.27, bf16[8,128,256]{2,1,0:T(8,128)(2,1)} %bitcast.24, f32[1,2048]{1,0:T(1,128)} %bitcast.34, bf16[1,2,2048,256]{3,2,1,0:T(8,128)(2,1)} %wkv_hbm.3), custom_call_target="tpu_custom_call" | custom-call | flops 536870912 | bytes 5000000 | tf_op jit(solution)/shard_map/pallas_call | solution.py:218
  (9 shorter events, 0.2 us)
Async XLA Ops:
  8.0 76.5 %all-gather.8.cloned.1.call-start = ((), (), s32[]{:S(2)}) async-start(), calls=%async_computation.5 | async-start | bytes 1179648 | tf_op jit(solution)/shard_map/all_gather | solution.py:264
  35.6 22.2 %all-to-all-start = ((bf16[8,128,256]{2,1,0:T(8,128)(2,1)}), bf16[8,128,256]{2,1,0:T(8,128)(2,1)S(1)}, u32[]{:S(2)}, u32[]{:S(2)}) async-start(bf16[8,128,256]{2,1,0:T(8,128)(2,1)} %get-tuple-element.14), calls=%async_computation | async-start | bytes 1048576 | tf_op jit(solution)/shard_map/all_to_all | solution.py:267
  40.9 25.0 %copy-start = (bf16[2,128,256]{2,1,0:T(8,128)(2,1)S(1)}, bf16[2,128,256]{2,1,0:T(8,128)(2,1)}, u32[]{:S(2)}) copy-start(bf16[2,128,256]{2,1,0:T(8,128)(2,1)} %get-tuple-element.13) | copy-start | bytes 393220
  40.9 73.8 %reduce-scatter.2.cloned.1.call-start = ((), (), s32[]{:S(2)}) async-start(), calls=%async_computation.4 | async-start | bytes 1179648 | tf_op jit(solution)/shard_map/reduce_scatter | solution.py:289
  58.0 5.9 %collective-permute-start = (bf16[128,256]{1,0:T(8,128)(2,1)S(1)}, bf16[128,256]{1,0:T(8,128)(2,1)S(1)}, u32[]{:S(2)}, u32[]{:S(2)}) collective-permute-start(bf16[128,256]{1,0:T(8,128)(2,1)S(1)} %add_convert_fusion.1), channel_id=1, source_target_pairs={{0,8},{8,16},{16,24},{24,32},{32,40},{40,48},{48,56},{56,64},{64,7... | collective-permute-start | bytes 196616 | tf_op jit(solution)/shard_map/ppermute | solution.py:294
  63.9 2.0 %collective-permute-start.1 = (bf16[128,256]{1,0:T(8,128)(2,1)S(1)}, bf16[128,256]{1,0:T(8,128)(2,1)S(1)}, u32[]{:S(2)}, u32[]{:S(2)}) collective-permute-start(bf16[128,256]{1,0:T(8,128)(2,1)S(1)} %collective-permute-done), channel_id=1, source_target_pairs={{256,448},{257,449},{258,450},{259,451},{260,452},{261,453},{262,4... | collective-permute-start | bytes 196616 | tf_op jit(solution)/shard_map/ppermute | solution.py:237
  64.5 1.4 collective-permute-start.2
  65.2 0.7 collective-permute-start.3
  87.9 23.2 %all-to-all-start.1 = ((bf16[8,128,256]{2,1,0:T(8,128)(2,1)}), bf16[8,128,256]{2,1,0:T(8,128)(2,1)S(1)}, u32[]{:S(2)}, u32[]{:S(2)}) async-start(bf16[8,128,256]{2,1,0:T(8,128)(2,1)} %shard_map.113), calls=%async_computation.1 | async-start | bytes 1048576 | tf_op jit(solution)/shard_map/all_to_all | solution.py:267
  92.2 75.1 %all-gather.10.cloned.1.call-start = ((), (), s32[]{:S(2)}) async-start(), calls=%async_computation.6 | async-start | bytes 1179648 | tf_op jit(solution)/shard_map/all_gather | solution.py:264
  92.2 16.3 %collective-permute-start.4 = (bf16[128,256]{1,0:T(8,128)(2,1)S(1)}, bf16[128,256]{1,0:T(8,128)(2,1)S(1)}, u32[]{:S(2)}, u32[]{:S(2)}) collective-permute-start(bf16[128,256]{1,0:T(8,128)(2,1)S(1)} %get-tuple-element.16), channel_id=1, source_target_pairs={{256,304},{320,368},{384,432},{448,496},{257,305},{321,369},{385,4... | collective-permute-start | bytes 196616 | tf_op jit(solution)/shard_map/ppermute | solution.py:244
  93.5 15.0 %collective-permute-start.5 = (bf16[128,256]{1,0:T(8,128)(2,1)S(1)}, bf16[128,256]{1,0:T(8,128)(2,1)S(1)}, u32[]{:S(2)}, u32[]{:S(2)}) collective-permute-start(bf16[128,256]{1,0:T(8,128)(2,1)S(1)} %get-tuple-element.16), channel_id=1, source_target_pairs={{256,288},{320,352},{384,416},{448,480},{257,289},{321,353},{385,4... | collective-permute-start | bytes 196616 | tf_op jit(solution)/shard_map/ppermute | solution.py:244
  94.1 14.3 %collective-permute-start.6 = (bf16[128,256]{1,0:T(8,128)(2,1)S(1)}, bf16[128,256]{1,0:T(8,128)(2,1)S(1)}, u32[]{:S(2)}, u32[]{:S(2)}) collective-permute-start(bf16[128,256]{1,0:T(8,128)(2,1)S(1)} %get-tuple-element.16), channel_id=1, source_target_pairs={{256,272},{320,336},{384,400},{448,464},{257,273},{321,337},{385,4... | collective-permute-start | bytes 196616 | tf_op jit(solution)/shard_map/ppermute | solution.py:244
  108.5 2.6 %collective-permute-start.7 = (bf16[128,256]{1,0:T(8,128)(2,1)S(1)}, bf16[128,256]{1,0:T(8,128)(2,1)S(1)}, u32[]{:S(2)}, u32[]{:S(2)}) collective-permute-start(bf16[128,256]{1,0:T(8,128)(2,1)S(1)} %select_select_fusion.2), channel_id=1, source_target_pairs={{256,264},{272,280},{288,296},{304,312},{320,328},{336,344},{352,3... | collective-permute-start | bytes 196616 | tf_op jit(solution)/shard_map/ppermute | solution.py:246
  111.9 2.7 %collective-permute-start.9 = (bf16[128,256]{1,0:T(8,128)(2,1)S(1)}, bf16[128,256]{1,0:T(8,128)(2,1)S(1)}, u32[]{:S(2)}, u32[]{:S(2)}) collective-permute-start(bf16[128,256]{1,0:T(8,128)(2,1)S(1)} %add_convert_fusion), channel_id=1, source_target_pairs={{248,504},{249,505},{250,506},{251,507},{252,508},{253,509},{254,5... | collective-permute-start | bytes 196616 | tf_op jit(solution)/shard_map/ppermute | solution.py:237
  112.6 2.0 %collective-permute-start.10 = (bf16[128,256]{1,0:T(8,128)(2,1)S(1)}, bf16[128,256]{1,0:T(8,128)(2,1)S(1)}, u32[]{:S(2)}, u32[]{:S(2)}) collective-permute-start(bf16[128,256]{1,0:T(8,128)(2,1)S(1)} %add_convert_fusion), channel_id=1, source_target_pairs={{248,440},{249,441},{250,442},{251,443},{252,444},{253,445},{254,4... | collective-permute-start | bytes 196616 | tf_op jit(solution)/shard_map/ppermute | solution.py:237
  113.3 1.4 collective-permute-start.11
  113.9 0.7 collective-permute-start.12
  114.7 13.8 %collective-permute-start.13 = (bf16[128,256]{1,0:T(8,128)(2,1)S(1)}, bf16[128,256]{1,0:T(8,128)(2,1)S(1)}, u32[]{:S(2)}, u32[]{:S(2)}) collective-permute-start(bf16[128,256]{1,0:T(8,128)(2,1)S(1)} %select_select_fusion.1), channel_id=1, source_target_pairs={{312,296},{376,360},{440,424},{504,488},{313,297},{377,361},{441,4... | collective-permute-start | bytes 196616 | tf_op jit(solution)/shard_map/ppermute | solution.py:244
  115.4 13.2 %collective-permute-start.14 = (bf16[128,256]{1,0:T(8,128)(2,1)S(1)}, bf16[128,256]{1,0:T(8,128)(2,1)S(1)}, u32[]{:S(2)}, u32[]{:S(2)}) collective-permute-start(bf16[128,256]{1,0:T(8,128)(2,1)S(1)} %select_select_fusion.1), channel_id=1, source_target_pairs={{312,280},{376,344},{440,408},{504,472},{313,281},{377,345},{441,4... | collective-permute-start | bytes 196616 | tf_op jit(solution)/shard_map/ppermute | solution.py:244
  116.1 12.5 %collective-permute-start.15 = (bf16[128,256]{1,0:T(8,128)(2,1)S(1)}, bf16[128,256]{1,0:T(8,128)(2,1)S(1)}, u32[]{:S(2)}, u32[]{:S(2)}) collective-permute-start(bf16[128,256]{1,0:T(8,128)(2,1)S(1)} %select_select_fusion.1), channel_id=1, source_target_pairs={{312,264},{376,328},{440,392},{504,456},{313,265},{377,329},{441,3... | collective-permute-start | bytes 196616 | tf_op jit(solution)/shard_map/ppermute | solution.py:244
  116.7 13.2 %collective-permute-start.8 = (bf16[128,256]{1,0:T(8,128)(2,1)S(1)}, bf16[128,256]{1,0:T(8,128)(2,1)S(1)}, u32[]{:S(2)}, u32[]{:S(2)}) collective-permute-start(bf16[128,256]{1,0:T(8,128)(2,1)S(1)} %add_convert_fusion), channel_id=1, source_target_pairs={{0,8},{8,16},{16,24},{24,32},{32,40},{40,48},{48,56},{56,64},{64,7... | collective-permute-start | bytes 196616 | tf_op jit(solution)/shard_map/ppermute | solution.py:314
  128.6 19.1 %collective-permute-start.16 = (bf16[128,256]{1,0:T(8,128)(2,1)S(1)}, bf16[128,256]{1,0:T(8,128)(2,1)S(1)}, u32[]{:S(2)}, u32[]{:S(2)}) collective-permute-start(bf16[128,256]{1,0:T(8,128)(2,1)S(1)} %select_select_fusion), channel_id=1, source_target_pairs={{264,256},{280,272},{296,288},{312,304},{328,320},{344,336},{360,3... | collective-permute-start | bytes 196616 | tf_op jit(solution)/shard_map/ppermute | solution.py:246
  130.7 36.0 %all-to-all-start.2 = ((f32[64,4,128]{2,1,0:T(4,128)}), f32[64,4,128]{2,1,0:T(4,128)S(1)}, u32[]{:S(2)}, u32[]{:S(2)}) async-start(f32[64,4,128]{2,1,0:T(4,128)} %bitcast.32), calls=%async_computation.3 | async-start | bytes 262144 | tf_op jit(solution)/shard_map/all_to_all | solution.py:312
Sparse Core Ops, SparseCore 0:
  11.0 42.6 all-gather.7
  111.9 37.4 all-gather.9
Sparse Core Ops, SparseCore 1:
  44.4 34.7 reduce-scatter.1

commit v7 on v5

--- a/solution.py
+++ b/solution.py
@@ -181,6 +181,7 @@
 def memory_kernel(half, section, first_hbm, second_hbm, final_hbm, wkv_hbm, out_hbm, sources, rows,
                   final_gain, wkv, out, sems):
     width = wkv.shape[2]
+    heads = sources.shape[1]
 
     def copy(k, source, target):
         return pltpu.make_async_copy(source, target, sems.at[k])
@@ -188,7 +189,7 @@
     gets = [
         copy(0, second_hbm, sources.at[1]),
         copy(1, final_hbm, final_gain),
-        copy(2, first_hbm.at[:, 0], sources.at[0]),
+        copy(2, first_hbm.at[pl.ds((half - 1) % ZL * heads, heads)], sources.at[0]),
         copy(3, wkv_hbm.at[0], wkv),
     ]
 
@@ -228,8 +229,8 @@
     )(section, *operands)
 
 
-def spread(block, source, beside):
-    y, x, zl = lax.axis_index("y"), lax.axis_index("x"), lax.axis_index("zl")
+def spread(block, source):
+    y, x = lax.axis_index("y"), lax.axis_index("x")
     sy, sx, sz = source // (X * ZL), source // ZL % X, source % ZL
     held = block
     for to in range(sy + 1, Y):
@@ -240,12 +241,15 @@
         if to != sx:
             pairs = [(place(k, sx, sz), place(k, to, sz)) for k in range(sy + 1, Y)]
             held = jnp.where(x == to, lax.ppermute(column, PIPE, pairs), held)
-    if beside is not None:
-        held, beside = lax.optimization_barrier((held, beside))
+    return held
+
+
+def spread_zl(held, source):
+    sy, sz = source // (X * ZL), source % ZL
     pairs = [
         (place(k, to, sz), place(k, to, 1 - sz)) for k in range(sy + 1, Y) for to in range(X)
     ]
-    return jnp.where(zl == sz, held, lax.ppermute(held, PIPE, pairs)), beside
+    return jnp.where(lax.axis_index("zl") == sz, held, lax.ppermute(held, PIPE, pairs))
 
 
 def body(stream, fresh, gain, final_gain, w_query, w_kv, w_out, cache_kv, cache_grad):
@@ -294,8 +298,7 @@
 
     output = summed(exchanged(parts), current)
     passed = lax.ppermute(output, PIPE, shift)
-    first_memory, _ = spread(output, half - 1, None)
-    entering = output
+    first_memory = spread(output, half - 1)
 
     current = jnp.where(place_here == 0, fresh_rows[0], passed)
     (parts,) = call(
@@ -309,12 +312,12 @@
     current = jnp.where(place_here == half, fresh_rows[1], current)
     parts, first_memory = lax.optimization_barrier((exchanged(parts), first_memory))
     output = summed(parts, current)
-    second_memory, share = spread(output, half - 1, share)
-    share = lax.all_to_all(share, PIPE[1:] + HEAD, 0, 0, tiled=True)
-    first_memory = whole(jnp.stack([first_memory, entering]))
+    first_memory = lax.all_gather(first_memory, ("zl",) + HEAD, axis=0)
+    second_memory = whole(spread_zl(spread(output, half - 1), half - 1))
     passed = lax.ppermute(output, PIPE, shift)
     last = jnp.where(place_here == half, jnp.zeros_like(passed), passed)
-    share, second_memory = lax.optimization_barrier((share, whole(second_memory)))
+    share, second_memory = lax.optimization_barrier((share, second_memory))
+    share = lax.all_to_all(share, PIPE[1:] + HEAD, 0, 0, tiled=True)
     memory_grad = jnp.sum(share, axis=0)
 
     (new_kv,) = call(

time: 174 us -> 192 us (1.10)
  the two profiles are of different devices: /device:TPU:41 before, /device:TPU:98 now
where the time goes in v7:
time: 192 us; the launch traced here: 191 us
  waiting for transfers between devices  66 us (34%)
  blocking collectives  55.6 us (29%)
  starting transfers between devices  36.6 us (19%)
  between operations  15.9 us (8%)
  Pallas kernels  13.9 us (7%)
    all_gather x3, blocking collectives, whole(): return lax.all_gather(block, HEAD, axis=0)  55.6 us
    ppermute x6, waiting for transfers between devices, spread(): held = jnp.where(x == to, lax.ppermute(column, PIPE, pairs), held)  24.2 us
    all_gather x1, waiting for transfers between devices, body(): first_memory = lax.all_gather(first_memory, ('zl',) + HEAD, axis=0)  14.9 us
    all_to_all x2, waiting for transfers between devices, exchanged(): return lax.all_to_all(parts, HEAD, 0, 0, tiled=True)  14.6 us
    pallas_call x4, Pallas kernels, call(): pl.pallas_call(kernel, out_shape=[jax.ShapeDtypeStruct(shape, kind) for s...  13.9 us
    all_to_all x1, starting transfers between devices, body(): share = lax.all_to_all(share, PIPE[1:] + HEAD, 0, 0, tiled=True)  9.83 us
    all_to_all x1, waiting for transfers between devices, body(): share = lax.all_to_all(share, PIPE[1:] + HEAD, 0, 0, tiled=True)  9.22 us
    all_to_all x2, starting transfers between devices, exchanged(): return lax.all_to_all(parts, HEAD, 0, 0, tiled=True)  8.74 us
  transfers between devices with their start and end apart: 23, of which 7 were waited for; matrix products, arithmetic and copies ran while one was open for 2% of the time, Pallas kernels for 5%

profile of v7, /device:TPU:98, one launch (start us, length us, event | category | flops | bytes accessed | tf_op | source)
XLA Modules:
  0.0 191.2 jit_solution(482472448912409747)
XLA Ops:
  8.0 0.0 all-gather.8.cloned.1.call-start
  8.0 0.7 all-gather.8.cloned.1.call-update
  8.7 0.9 copy.14
  9.7 21.1 %all-gather = bf16[1024,256]{1,0:T(8,128)(2,1)} all-gather(bf16[128,256]{1,0:T(8,128)(2,1)S(1)} %bitcast.27), channel_id=2, replica_groups=mesh['y'=8,'x'=4,'zl'=2,'zh'=4,'c'=2] {'zh','c'}, dimensions={0}, use_global_device_ids=true | all-gather | bytes 589824 | tf_op jit(solution)/shard_map/all_gather | solution.py:270
  30.8 3.8 %shard_map.112 = (bf16[8,128,256]{2,1,0:T(8,128)(2,1)}, bf16[2,128,256]{2,1,0:T(8,128)(2,1)}) custom-call(s32[1]{0:T(128)} %bitcast.section, bf16[8,128,256]{2,1,0:T(8,128)(2,1)} %bitcast.24, bf16[2,256,128]{2,1,0:T(8,128)(2,1)} %fresh.1, f32[1,2048]{1,0:T(1,128)} %gain.3, bf16[1,2048,256]{2,1,0:T(8,128)(2,1)} %wq.3, bf16[1,2,2048,256]{3,2,1,0:T(8,128)(2,1)} %wkv_hbm.3, ...), custom_call_target="tpu_custom_call" | custom-call | flops 536870912 | bytes 5000000 | tf_op jit(solution)/shard_map/pallas_call | solution.py:219
  34.6 4.7 %all-to-all-start = ((bf16[8,128,256]{2,1,0:T(8,128)(2,1)}), bf16[8,128,256]{2,1,0:T(8,128)(2,1)S(1)}, u32[]{:S(2)}, u32[]{:S(2)}) async-start(bf16[8,128,256]{2,1,0:T(8,128)(2,1)} %get-tuple-element.10), calls=%async_computation | async-start | bytes 1048576 | tf_op jit(solution)/shard_map/all_to_all | solution.py:273
  39.3 0.0 copy-start
  39.3 0.0 reduce-scatter.2.cloned.1.call-start
  39.4 3.4 %shard_map.114 = f32[2048,128]{1,0:T(8,128)} custom-call(s32[1]{0:T(128)} %bitcast.section, bf16[1,128,512]{2,1,0:T(8,128)(2,1)} %grads_hbm.1, bf16[1,2,2048,256]{3,2,1,0:T(8,128)(2,1)} %wkv_hbm.3), custom_call_target="tpu_custom_call" | custom-call | flops 536870912 | bytes 5000000 | tf_op jit(solution)/shard_map/pallas_call | solution.py:219
  42.8 0.0 reduce-scatter.2.cloned.1.call-update
  42.8 14.6 %all-to-all-done = bf16[8,128,256]{2,1,0:T(8,128)(2,1)S(1)} async-done(((bf16[8,128,256]{2,1,0:T(8,128)(2,1)}), bf16[8,128,256]{2,1,0:T(8,128)(2,1)S(1)}, u32[]{:S(2)}, u32[]{:S(2)}) %all-to-all-start) | async-done | bytes 524320 | tf_op jit(solution)/shard_map/all_to_all | solution.py:273
  57.4 0.1 convert_reduce_fusion.1
  57.5 4.1 %collective-permute-start = (bf16[128,256]{1,0:T(8,128)(2,1)S(1)}, bf16[128,256]{1,0:T(8,128)(2,1)S(1)}, u32[]{:S(2)}, u32[]{:S(2)}) collective-permute-start(bf16[128,256]{1,0:T(8,128)(2,1)S(1)} %add_convert_fusion.1), channel_id=1, source_target_pairs={{0,8},{8,16},{16,24},{24,32},{32,40},{40,48},{48,56},{56,64},{64,7... | collective-permute-start | bytes 196616 | tf_op jit(solution)/shard_map/ppermute | solution.py:300
  61.6 2.1 %collective-permute-done = bf16[128,256]{1,0:T(8,128)(2,1)S(1)} collective-permute-done((bf16[128,256]{1,0:T(8,128)(2,1)S(1)}, bf16[128,256]{1,0:T(8,128)(2,1)S(1)}, u32[]{:S(2)}, u32[]{:S(2)}) %collective-permute-start) | collective-permute-done | bytes 65568 | tf_op jit(solution)/shard_map/ppermute | solution.py:300
  63.7 0.0 copy-done
  63.7 16.0 %all-gather.1 = bf16[1024,256]{1,0:T(8,128)(2,1)} all-gather(bf16[128,256]{1,0:T(8,128)(2,1)S(1)} %bitcast_select_fusion), channel_id=3, replica_groups=mesh['y'=8,'x'=4,'zl'=2,'zh'=4,'c'=2] {'zh','c'}, dimensions={0}, use_global_device_ids=true | all-gather | bytes 589824 | tf_op jit(solution)/shard_map/all_gather | solution.py:270
  79.7 0.0 all-gather.8.cloned.1.call-done
  79.7 3.3 %shard_map.113 = bf16[8,128,256]{2,1,0:T(8,128)(2,1)} custom-call(s32[1]{0:T(128)} %bitcast.section, bf16[8,128,256]{2,1,0:T(8,128)(2,1)} %bitcast.23, bf16[8,2,256,128]{3,2,1,0:T(8,128)(2,1)} %bitcast.26, f32[1,2048]{1,0:T(1,128)} %gain.3, f32[1,2048]{1,0:T(1,128)} %bitcast.29, bf16[1,2048,256]{2,1,0:T(8,128)(2,1)} %wq.3, ...), custom_call_target="tpu_custom_call" | custom-call | flops 536870912 | bytes 5000000 | tf_op jit(solution)/shard_map/pallas_call | solution.py:219
  83.0 4.0 %all-to-all-start.1 = ((bf16[8,128,256]{2,1,0:T(8,128)(2,1)}), bf16[8,128,256]{2,1,0:T(8,128)(2,1)S(1)}, u32[]{:S(2)}, u32[]{:S(2)}) async-start(bf16[8,128,256]{2,1,0:T(8,128)(2,1)} %shard_map.113), calls=%async_computation.1 | async-start | bytes 1048576 | tf_op jit(solution)/shard_map/all_to_all | solution.py:273
  87.0 0.0 all-gather.10.cloned.1.call-start
  87.1 0.7 collective-permute-start.1
  87.8 0.7 collective-permute-start.2
  88.4 0.7 collective-permute-start.3
  89.1 0.7 collective-permute-start.4
  89.8 0.0 collective-permute-done.1
  89.8 0.0 collective-permute-done.2
  89.8 0.0 collective-permute-done.3
  89.8 0.0 collective-permute-done.4
  89.9 0.7 collective-permute-start.5
  90.5 1.3 collective-permute-start.6
  91.8 0.7 collective-permute-start.7
  92.5 0.0 collective-permute-done.5
  92.5 14.6 %collective-permute-done.6 = bf16[128,256]{1,0:T(8,128)(2,1)S(1)} collective-permute-done((bf16[128,256]{1,0:T(8,128)(2,1)S(1)}, bf16[128,256]{1,0:T(8,128)(2,1)S(1)}, u32[]{:S(2)}, u32[]{:S(2)}) %collective-permute-start.6) | collective-permute-done | bytes 65568 | tf_op jit(solution)/shard_map/ppermute | solution.py:243
  107.1 0.0 collective-permute-done.7
  107.1 0.6 select_select_fusion.2
  107.8 0.0 all-to-all-done.1
  107.8 0.0 all-gather.10.cloned.1.call-update
  107.8 0.1 convert_reduce_fusion
  107.9 0.7 collective-permute-start.10
  108.6 0.7 collective-permute-start.11
  109.2 0.7 collective-permute-start.12
  109.9 0.7 collective-permute-start.9
  110.6 0.0 collective-permute-done.10
  110.6 0.0 collective-permute-done.11
  110.6 0.0 collective-permute-done.12
  110.6 0.0 collective-permute-done.9
  110.7 0.7 collective-permute-start.13
  111.3 1.3 collective-permute-start.14
  112.6 0.7 collective-permute-start.15
  113.3 0.0 collective-permute-done.13
  113.3 9.6 %collective-permute-done.14 = bf16[128,256]{1,0:T(8,128)(2,1)S(1)} collective-permute-done((bf16[128,256]{1,0:T(8,128)(2,1)S(1)}, bf16[128,256]{1,0:T(8,128)(2,1)S(1)}, u32[]{:S(2)}, u32[]{:S(2)}) %collective-permute-start.14) | collective-permute-done | bytes 65568 | tf_op jit(solution)/shard_map/ppermute | solution.py:243
  123.0 0.0 collective-permute-done.15
  123.0 1.3 collective-permute-start.16
  124.3 1.9 %collective-permute-start.8 = (bf16[128,256]{1,0:T(8,128)(2,1)S(1)}, bf16[128,256]{1,0:T(8,128)(2,1)S(1)}, u32[]{:S(2)}, u32[]{:S(2)}) collective-permute-start(bf16[128,256]{1,0:T(8,128)(2,1)S(1)} %add_convert_fusion), channel_id=1, source_target_pairs={{0,8},{8,16},{16,24},{24,32},{32,40},{40,48},{48,56},{56,64},{64,7... | collective-permute-start | bytes 196616 | tf_op jit(solution)/shard_map/ppermute | solution.py:317
  126.2 0.2 collective-permute-done.16
  126.4 18.5 %all-gather.4 = bf16[1024,256]{1,0:T(8,128)(2,1)} all-gather(bf16[128,256]{1,0:T(8,128)(2,1)S(1)} %broadcast_select_fusion), channel_id=6, replica_groups=mesh['y'=8,'x'=4,'zl'=2,'zh'=4,'c'=2] {'zh','c'}, dimensions={0}, use_global_device_ids=true | all-gather | bytes 589824 | tf_op jit(solution)/shard_map/all_gather | solution.py:270
  144.9 0.0 reduce-scatter.2.cloned.1.call-done
  144.9 9.8 %all-to-all-start.2 = ((f32[64,4,128]{2,1,0:T(4,128)}), f32[64,4,128]{2,1,0:T(4,128)S(1)}, u32[]{:S(2)}, u32[]{:S(2)}) async-start(f32[64,4,128]{2,1,0:T(4,128)} %bitcast.28), calls=%async_computation.3 | async-start | bytes 262144 | tf_op jit(solution)/shard_map/all_to_all | solution.py:320
  154.8 0.0 collective-permute-done.8
  154.8 0.7 copy.15
  155.5 9.2 %all-to-all-done.2 = f32[64,4,128]{2,1,0:T(4,128)S(1)} async-done(((f32[64,4,128]{2,1,0:T(4,128)}), f32[64,4,128]{2,1,0:T(4,128)S(1)}, u32[]{:S(2)}, u32[]{:S(2)}) %all-to-all-start.2) | async-done | bytes 131104 | tf_op jit(solution)/shard_map/all_to_all | solution.py:320
  164.8 0.7 reduce_sum.29
  165.4 14.9 %all-gather.10.cloned.1.call-done = bf16[2048,256]{1,0:T(8,128)(2,1)} async-done(((bf16[128,256]{1,0:T(8,128)(2,1)}), bf16[2048,256]{1,0:T(8,128)(2,1)}) %all-gather.10.cloned.1.call-update) | async-done | bytes 1048592 | tf_op jit(solution)/shard_map/all_gather | solution.py:315
  180.3 3.4 %shard_map.115 = bf16[1,2,128,512]{3,2,1,0:T(8,128)(2,1)} custom-call(s32[1]{0:T(128)} %bitcast.section, bf16[16,128,256]{2,1,0:T(8,128)(2,1)} %bitcast.25, bf16[8,128,256]{2,1,0:T(8,128)(2,1)} %bitcast.22, f32[1,2048]{1,0:T(1,128)} %bitcast.30, bf16[1,2,2048,256]{3,2,1,0:T(8,128)(2,1)} %wkv_hbm.3), custom_call_target="tpu_custom_call" | custom-call | flops 536870912 | bytes 5000000 | tf_op jit(solution)/shard_map/pallas_call | solution.py:219
  (8 shorter events, 0.1 us)
Async XLA Ops:
  8.0 71.7 %all-gather.8.cloned.1.call-start = ((), (), s32[]{:S(2)}) async-start(), calls=%async_computation.5 | async-start | bytes 1179648 | tf_op jit(solution)/shard_map/all_gather | solution.py:270
  34.6 22.8 %all-to-all-start = ((bf16[8,128,256]{2,1,0:T(8,128)(2,1)}), bf16[8,128,256]{2,1,0:T(8,128)(2,1)S(1)}, u32[]{:S(2)}, u32[]{:S(2)}) async-start(bf16[8,128,256]{2,1,0:T(8,128)(2,1)} %get-tuple-element.10), calls=%async_computation | async-start | bytes 1048576 | tf_op jit(solution)/shard_map/all_to_all | solution.py:273
  39.3 24.4 %copy-start = (bf16[2,128,256]{2,1,0:T(8,128)(2,1)S(1)}, bf16[2,128,256]{2,1,0:T(8,128)(2,1)}, u32[]{:S(2)}) copy-start(bf16[2,128,256]{2,1,0:T(8,128)(2,1)} %get-tuple-element.9) | copy-start | bytes 393220
  39.3 105.6 %reduce-scatter.2.cloned.1.call-start = ((), (), s32[]{:S(2)}) async-start(), calls=%async_computation.4 | async-start | bytes 1179648 | tf_op jit(solution)/shard_map/reduce_scatter | solution.py:295
  57.5 6.2 %collective-permute-start = (bf16[128,256]{1,0:T(8,128)(2,1)S(1)}, bf16[128,256]{1,0:T(8,128)(2,1)S(1)}, u32[]{:S(2)}, u32[]{:S(2)}) collective-permute-start(bf16[128,256]{1,0:T(8,128)(2,1)S(1)} %add_convert_fusion.1), channel_id=1, source_target_pairs={{0,8},{8,16},{16,24},{24,32},{32,40},{40,48},{48,56},{56,64},{64,7... | collective-permute-start | bytes 196616 | tf_op jit(solution)/shard_map/ppermute | solution.py:300
  83.0 24.7 %all-to-all-start.1 = ((bf16[8,128,256]{2,1,0:T(8,128)(2,1)}), bf16[8,128,256]{2,1,0:T(8,128)(2,1)S(1)}, u32[]{:S(2)}, u32[]{:S(2)}) async-start(bf16[8,128,256]{2,1,0:T(8,128)(2,1)} %shard_map.113), calls=%async_computation.1 | async-start | bytes 1048576 | tf_op jit(solution)/shard_map/all_to_all | solution.py:273
  87.0 93.3 %all-gather.10.cloned.1.call-start = ((), (), s32[]{:S(2)}) async-start(), calls=%async_computation.6 | async-start | bytes 1114112 | tf_op jit(solution)/shard_map/all_gather | solution.py:315
  87.1 2.7 %collective-permute-start.1 = (bf16[128,256]{1,0:T(8,128)(2,1)S(1)}, bf16[128,256]{1,0:T(8,128)(2,1)S(1)}, u32[]{:S(2)}, u32[]{:S(2)}) collective-permute-start(bf16[128,256]{1,0:T(8,128)(2,1)S(1)} %add_convert_fusion.1), channel_id=1, source_target_pairs={{248,504},{249,505},{250,506},{251,507},{252,508},{253,509},{254,5... | collective-permute-start | bytes 196616 | tf_op jit(solution)/shard_map/ppermute | solution.py:237
  87.8 2.0 %collective-permute-start.2 = (bf16[128,256]{1,0:T(8,128)(2,1)S(1)}, bf16[128,256]{1,0:T(8,128)(2,1)S(1)}, u32[]{:S(2)}, u32[]{:S(2)}) collective-permute-start(bf16[128,256]{1,0:T(8,128)(2,1)S(1)} %add_convert_fusion.1), channel_id=1, source_target_pairs={{248,440},{249,441},{250,442},{251,443},{252,444},{253,445},{254,4... | collective-permute-start | bytes 196616 | tf_op jit(solution)/shard_map/ppermute | solution.py:237
  88.4 1.4 collective-permute-start.3
  89.1 0.7 collective-permute-start.4
  89.9 2.7 %collective-permute-start.5 = (bf16[128,256]{1,0:T(8,128)(2,1)S(1)}, bf16[128,256]{1,0:T(8,128)(2,1)S(1)}, u32[]{:S(2)}, u32[]{:S(2)}) collective-permute-start(bf16[128,256]{1,0:T(8,128)(2,1)S(1)} %select_select_fusion.3), channel_id=1, source_target_pairs={{312,296},{376,360},{440,424},{504,488},{313,297},{377,361},{441,4... | collective-permute-start | bytes 196616 | tf_op jit(solution)/shard_map/ppermute | solution.py:243
  90.5 16.6 %collective-permute-start.6 = (bf16[128,256]{1,0:T(8,128)(2,1)S(1)}, bf16[128,256]{1,0:T(8,128)(2,1)S(1)}, u32[]{:S(2)}, u32[]{:S(2)}) collective-permute-start(bf16[128,256]{1,0:T(8,128)(2,1)S(1)} %select_select_fusion.3), channel_id=1, source_target_pairs={{312,280},{376,344},{440,408},{504,472},{313,281},{377,345},{441,4... | collective-permute-start | bytes 196616 | tf_op jit(solution)/shard_map/ppermute | solution.py:243
  91.8 15.3 %collective-permute-start.7 = (bf16[128,256]{1,0:T(8,128)(2,1)S(1)}, bf16[128,256]{1,0:T(8,128)(2,1)S(1)}, u32[]{:S(2)}, u32[]{:S(2)}) collective-permute-start(bf16[128,256]{1,0:T(8,128)(2,1)S(1)} %select_select_fusion.3), channel_id=1, source_target_pairs={{312,264},{376,328},{440,392},{504,456},{313,265},{377,329},{441,3... | collective-permute-start | bytes 196616 | tf_op jit(solution)/shard_map/ppermute | solution.py:243
  107.9 2.7 %collective-permute-start.10 = (bf16[128,256]{1,0:T(8,128)(2,1)S(1)}, bf16[128,256]{1,0:T(8,128)(2,1)S(1)}, u32[]{:S(2)}, u32[]{:S(2)}) collective-permute-start(bf16[128,256]{1,0:T(8,128)(2,1)S(1)} %add_convert_fusion), channel_id=1, source_target_pairs={{248,440},{249,441},{250,442},{251,443},{252,444},{253,445},{254,4... | collective-permute-start | bytes 196616 | tf_op jit(solution)/shard_map/ppermute | solution.py:237
  108.6 2.0 %collective-permute-start.11 = (bf16[128,256]{1,0:T(8,128)(2,1)S(1)}, bf16[128,256]{1,0:T(8,128)(2,1)S(1)}, u32[]{:S(2)}, u32[]{:S(2)}) collective-permute-start(bf16[128,256]{1,0:T(8,128)(2,1)S(1)} %add_convert_fusion), channel_id=1, source_target_pairs={{248,376},{249,377},{250,378},{251,379},{252,380},{253,381},{254,3... | collective-permute-start | bytes 196616 | tf_op jit(solution)/shard_map/ppermute | solution.py:237
  109.2 1.4 collective-permute-start.12
  109.9 0.7 collective-permute-start.9
  110.7 2.6 %collective-permute-start.13 = (bf16[128,256]{1,0:T(8,128)(2,1)S(1)}, bf16[128,256]{1,0:T(8,128)(2,1)S(1)}, u32[]{:S(2)}, u32[]{:S(2)}) collective-permute-start(bf16[128,256]{1,0:T(8,128)(2,1)S(1)} %select_select_fusion.1), channel_id=1, source_target_pairs={{312,296},{376,360},{440,424},{504,488},{313,297},{377,361},{441,4... | collective-permute-start | bytes 196616 | tf_op jit(solution)/shard_map/ppermute | solution.py:243
  111.3 11.6 %collective-permute-start.14 = (bf16[128,256]{1,0:T(8,128)(2,1)S(1)}, bf16[128,256]{1,0:T(8,128)(2,1)S(1)}, u32[]{:S(2)}, u32[]{:S(2)}) collective-permute-start(bf16[128,256]{1,0:T(8,128)(2,1)S(1)} %select_select_fusion.1), channel_id=1, source_target_pairs={{312,280},{376,344},{440,408},{504,472},{313,281},{377,345},{441,4... | collective-permute-start | bytes 196616 | tf_op jit(solution)/shard_map/ppermute | solution.py:243
  112.6 10.3 %collective-permute-start.15 = (bf16[128,256]{1,0:T(8,128)(2,1)S(1)}, bf16[128,256]{1,0:T(8,128)(2,1)S(1)}, u32[]{:S(2)}, u32[]{:S(2)}) collective-permute-start(bf16[128,256]{1,0:T(8,128)(2,1)S(1)} %select_select_fusion.1), channel_id=1, source_target_pairs={{312,264},{376,328},{440,392},{504,456},{313,265},{377,329},{441,3... | collective-permute-start | bytes 196616 | tf_op jit(solution)/shard_map/ppermute | solution.py:243
  123.0 3.4 %collective-permute-start.16 = (bf16[128,256]{1,0:T(8,128)(2,1)S(1)}, bf16[128,256]{1,0:T(8,128)(2,1)S(1)}, u32[]{:S(2)}, u32[]{:S(2)}) collective-permute-start(bf16[128,256]{1,0:T(8,128)(2,1)S(1)} %select_select_fusion), channel_id=1, source_target_pairs={{264,256},{280,272},{296,288},{312,304},{328,320},{344,336},{360,3... | collective-permute-start | bytes 196616 | tf_op jit(solution)/shard_map/ppermute | solution.py:252
  124.3 30.5 %collective-permute-start.8 = (bf16[128,256]{1,0:T(8,128)(2,1)S(1)}, bf16[128,256]{1,0:T(8,128)(2,1)S(1)}, u32[]{:S(2)}, u32[]{:S(2)}) collective-permute-start(bf16[128,256]{1,0:T(8,128)(2,1)S(1)} %add_convert_fusion), channel_id=1, source_target_pairs={{0,8},{8,16},{16,24},{24,32},{32,40},{40,48},{48,56},{56,64},{64,7... | collective-permute-start | bytes 196616 | tf_op jit(solution)/shard_map/ppermute | solution.py:317
  144.9 19.8 %all-to-all-start.2 = ((f32[64,4,128]{2,1,0:T(4,128)}), f32[64,4,128]{2,1,0:T(4,128)S(1)}, u32[]{:S(2)}, u32[]{:S(2)}) async-start(f32[64,4,128]{2,1,0:T(4,128)} %bitcast.28), calls=%async_computation.3 | async-start | bytes 262144 | tf_op jit(solution)/shard_map/all_to_all | solution.py:320
Sparse Core Ops, SparseCore 0:
  11.0 37.6 all-gather.7
  107.9 72.3 all-gather.9
Sparse Core Ops, SparseCore 1:
  42.9 39.9 reduce-scatter.1

commit v8 on v5

--- a/solution.py
+++ b/solution.py
@@ -272,6 +272,14 @@
         return (current.astype(F32) + jnp.sum(parts.astype(F32), axis=0)).astype(BF)
 
     weights = (((depth, width), BF), ((2, depth, width), BF), ((width, depth), BF))
+    (share,) = call(
+        functools.partial(share_kernel, half), section, (cache_grad, w_kv), ((depth, tokens),),
+        ((pair_shape, BF), ((2, depth, width), BF), ((depth, tokens), F32)),
+        3, flops, F32,
+    )
+    share, stream = lax.optimization_barrier((share, stream))
+    share = lax.psum_scatter(share, "y", scatter_dimension=0, tiled=True)
+
     fresh_whole = whole(fresh)
     current = stream[0].T
     parts, fresh_rows = call(
@@ -283,17 +291,10 @@
         8 + heads, flops,
     )
 
-    (share,) = call(
-        functools.partial(share_kernel, half), section, (cache_grad, w_kv), ((depth, tokens),),
-        ((pair_shape, BF), ((2, depth, width), BF), ((depth, tokens), F32)),
-        3, flops, F32,
-    )
-    share = lax.psum_scatter(share, "y", scatter_dimension=0, tiled=True)
-    plane = X * ZL * heads
-    share = share.reshape(plane, depth // (pipe_count * heads), tokens)
-
     output = summed(exchanged(parts), current)
-    passed = lax.ppermute(output, PIPE, shift)
+    share, passed = lax.optimization_barrier((share, lax.ppermute(output, PIPE, shift)))
+    share = lax.psum_scatter(share, "x", scatter_dimension=0, tiled=True)
+    share = share.reshape(ZL * heads, depth // (pipe_count * heads), tokens)
     first_memory, _ = spread(output, half - 1, None)
     entering = output
 
@@ -310,7 +311,7 @@
     parts, first_memory = lax.optimization_barrier((exchanged(parts), first_memory))
     output = summed(parts, current)
     second_memory, share = spread(output, half - 1, share)
-    share = lax.all_to_all(share, PIPE[1:] + HEAD, 0, 0, tiled=True)
+    share = lax.all_to_all(share, ("zl",) + HEAD, 0, 0, tiled=True)
     first_memory = whole(jnp.stack([first_memory, entering]))
     passed = lax.ppermute(output, PIPE, shift)
     last = jnp.where(place_here == half, jnp.zeros_like(passed), passed)

time: 174 us -> 181 us (1.040)
  the two profiles are of different devices: /device:TPU:41 before, /device:TPU:33 now
where the time goes in v8:
time: 181 us; the launch traced here: 180 us
  blocking collectives  82.2 us (45%)
  starting transfers between devices  32.4 us (18%)
  waiting for transfers between devices  30.2 us (17%)
  Pallas kernels  16.1 us (9%)
  between operations  15.9 us (9%)
  other arithmetic  2.44 us (1%)
    all_gather x3, blocking collectives, whole(): return lax.all_gather(block, HEAD, axis=0)  58.8 us
    all_to_all x1, blocking collectives, exchanged(): return lax.all_to_all(parts, HEAD, 0, 0, tiled=True)  23.3 us
    reduce_scatter x1, waiting for transfers between devices, body(): share = lax.psum_scatter(share, 'x', scatter_dimension=0, tiled=True)  16.5 us
    pallas_call x4, Pallas kernels, call(): pl.pallas_call(kernel, out_shape=[jax.ShapeDtypeStruct(shape, kind) for s...  16.1 us
    all_to_all x1, starting transfers between devices, body(): share = lax.all_to_all(share, ('zl',) + HEAD, 0, 0, tiled=True)  11.5 us
    ppermute x1, waiting for transfers between devices, body(): lax.ppermute(output, PIPE, shift)  6.18 us
    ppermute x8, starting transfers between devices, spread(): sent = lax.ppermute(block, PIPE, [(source, place(to, sx, sz))])  5.31 us
    all_to_all x1, starting transfers between devices, exchanged(): return lax.all_to_all(parts, HEAD, 0, 0, tiled=True)  4 us
  transfers between devices with their start and end apart: 24, of which 4 were waited for; matrix products, arithmetic and copies ran while one was open for 2% of the time, Pallas kernels for 2%

profile of v8, /device:TPU:33, one launch (start us, length us, event | category | flops | bytes accessed | tf_op | source)
XLA Modules:
  0.0 180.1 jit_solution(8626377890076937484)
XLA Ops:
  8.0 0.0 reduce-scatter.3.cloned.1.call-start
  8.1 3.4 %shard_map.112 = f32[2048,128]{1,0:T(8,128)} custom-call(s32[1]{0:T(128)} %bitcast.section, bf16[1,128,512]{2,1,0:T(8,128)(2,1)} %grads_hbm.1, bf16[1,2,2048,256]{3,2,1,0:T(8,128)(2,1)} %wkv_hbm.3), custom_call_target="tpu_custom_call" | custom-call | flops 536870912 | bytes 5000000 | tf_op jit(solution)/shard_map/pallas_call | solution.py:218
  11.5 0.0 reduce-scatter.3.cloned.1.call-update
  11.5 0.0 all-gather.8.cloned.1.call-start
  11.6 0.5 all-gather.8.cloned.1.call-update
  12.1 0.1 copy.14
  12.2 22.2 %all-gather = bf16[1024,256]{1,0:T(8,128)(2,1)} all-gather(bf16[128,256]{1,0:T(8,128)(2,1)S(1)} %bitcast.29), channel_id=2, replica_groups=mesh['y'=8,'x'=4,'zl'=2,'zh'=4,'c'=2] {'zh','c'}, dimensions={0}, use_global_device_ids=true | all-gather | bytes 589824 | tf_op jit(solution)/shard_map/all_gather | solution.py:266
  34.4 3.8 %shard_map.113 = (bf16[8,128,256]{2,1,0:T(8,128)(2,1)}, bf16[2,128,256]{2,1,0:T(8,128)(2,1)}) custom-call(s32[1]{0:T(128)} %bitcast.section, bf16[8,128,256]{2,1,0:T(8,128)(2,1)} %bitcast.26, bf16[2,256,128]{2,1,0:T(8,128)(2,1)} %fresh.1, f32[1,2048]{1,0:T(1,128)} %gain.3, bf16[1,2048,256]{2,1,0:T(8,128)(2,1)} %wq.3, bf16[1,2,2048,256]{3,2,1,0:T(8,128)(2,1)} %wkv_hbm.3, ...), custom_call_target="tpu_custom_call" | custom-call | flops 536870912 | bytes 5000000 | tf_op jit(solution)/shard_map/pallas_call | solution.py:218
  38.2 23.3 %all_to_all.15 = bf16[8,128,256]{2,1,0:T(8,128)(2,1)S(1)} all-to-all(bf16[8,128,256]{2,1,0:T(8,128)(2,1)} %get-tuple-element.18), channel_id=1, replica_groups=mesh['y'=8,'x'=4,'zl'=2,'zh'=4,'c'=2] {'zh','c'}, dimensions={0} | all-to-all | bytes 1048576 | tf_op jit(solution)/shard_map/all_to_all | solution.py:269
  61.5 0.1 convert_reduce_fusion.1
  61.6 3.0 %collective-permute-start = (bf16[128,256]{1,0:T(8,128)(2,1)S(1)}, bf16[128,256]{1,0:T(8,128)(2,1)S(1)}, u32[]{:S(2)}, u32[]{:S(2)}) collective-permute-start(bf16[128,256]{1,0:T(8,128)(2,1)S(1)} %add_convert_fusion.1), channel_id=1, source_target_pairs={{0,8},{8,16},{16,24},{24,32},{32,40},{40,48},{48,56},{56,64},{64,7... | collective-permute-start | bytes 196616 | tf_op jit(solution)/shard_map/ppermute | solution.py:295
  64.6 6.2 %collective-permute-done = bf16[128,256]{1,0:T(8,128)(2,1)S(1)} collective-permute-done((bf16[128,256]{1,0:T(8,128)(2,1)S(1)}, bf16[128,256]{1,0:T(8,128)(2,1)S(1)}, u32[]{:S(2)}, u32[]{:S(2)}) %collective-permute-start) | collective-permute-done | bytes 65568 | tf_op jit(solution)/shard_map/ppermute | solution.py:295
  70.8 0.8 bitcast_select_fusion
  71.7 18.0 %all-gather.1 = bf16[1024,256]{1,0:T(8,128)(2,1)} all-gather(bf16[128,256]{1,0:T(8,128)(2,1)S(1)} %bitcast_select_fusion), channel_id=3, replica_groups=mesh['y'=8,'x'=4,'zl'=2,'zh'=4,'c'=2] {'zh','c'}, dimensions={0}, use_global_device_ids=true | all-gather | bytes 589824 | tf_op jit(solution)/shard_map/all_gather | solution.py:266
  89.7 5.5 %shard_map.114 = bf16[8,128,256]{2,1,0:T(8,128)(2,1)} custom-call(s32[1]{0:T(128)} %bitcast.section, bf16[8,128,256]{2,1,0:T(8,128)(2,1)} %bitcast.25, bf16[8,2,256,128]{3,2,1,0:T(8,128)(2,1)} %bitcast.28, f32[1,2048]{1,0:T(1,128)} %gain.3, f32[1,2048]{1,0:T(1,128)} %bitcast.32, bf16[1,2048,256]{2,1,0:T(8,128)(2,1)} %wq.3, ...), custom_call_target="tpu_custom_call" | custom-call | flops 536870912 | bytes 5000000 | tf_op jit(solution)/shard_map/pallas_call | solution.py:218
  95.2 0.0 copy-start
  95.2 4.0 %all-to-all-start.1 = ((bf16[8,128,256]{2,1,0:T(8,128)(2,1)}), bf16[8,128,256]{2,1,0:T(8,128)(2,1)S(1)}, u32[]{:S(2)}, u32[]{:S(2)}) async-start(bf16[8,128,256]{2,1,0:T(8,128)(2,1)} %shard_map.114), calls=%async_computation.2 | async-start | bytes 1048576 | tf_op jit(solution)/shard_map/all_to_all | solution.py:269
  99.3 0.7 collective-permute-start.4
  99.9 0.7 collective-permute-start.3
  100.6 0.7 collective-permute-start.2
  101.3 0.7 collective-permute-start.1
  101.9 0.0 collective-permute-done.4
  102.0 0.0 collective-permute-done.3
  102.0 0.0 collective-permute-done.2
  102.0 0.0 collective-permute-done.1
  102.0 0.7 collective-permute-start.7
  102.7 0.7 collective-permute-start.6
  103.4 0.7 collective-permute-start.5
  104.0 0.0 collective-permute-done.7
  104.0 0.0 collective-permute-done.6
  104.1 0.0 collective-permute-done.5
  104.1 1.3 collective-permute-start.8
  105.4 0.0 reduce-scatter.5.cloned.1.call-update
  105.4 0.0 all-gather.10.cloned.1.call-start
  105.5 3.6 %collective-permute-done.8 = bf16[128,256]{1,0:T(8,128)(2,1)S(1)} collective-permute-done((bf16[128,256]{1,0:T(8,128)(2,1)S(1)}, bf16[128,256]{1,0:T(8,128)(2,1)S(1)}, u32[]{:S(2)}, u32[]{:S(2)}) %collective-permute-start.8) | collective-permute-done | bytes 65568 | tf_op jit(solution)/shard_map/ppermute | solution.py:248
  109.1 3.3 %all-to-all-done.1 = bf16[8,128,256]{2,1,0:T(8,128)(2,1)S(1)} async-done(((bf16[8,128,256]{2,1,0:T(8,128)(2,1)}), bf16[8,128,256]{2,1,0:T(8,128)(2,1)S(1)}, u32[]{:S(2)}, u32[]{:S(2)}) %all-to-all-start.1) | async-done | bytes 524320 | tf_op jit(solution)/shard_map/all_to_all | solution.py:269
  112.4 0.7 pad_maximum_fusion
  113.1 0.0 all-gather.10.cloned.1.call-update
  113.1 0.1 convert_reduce_fusion
  113.2 0.7 collective-permute-start.13
  113.9 0.7 collective-permute-start.12
  114.6 0.7 collective-permute-start.11
  115.2 0.7 collective-permute-start.10
  115.9 0.0 collective-permute-done.13
  115.9 0.0 collective-permute-done.12
  115.9 0.0 collective-permute-done.11
  115.9 0.0 collective-permute-done.10
  116.0 0.7 collective-permute-start.16
  116.7 0.7 collective-permute-start.15
  117.3 0.7 collective-permute-start.14
  118.0 1.9 %collective-permute-start.9 = (bf16[128,256]{1,0:T(8,128)(2,1)S(1)}, bf16[128,256]{1,0:T(8,128)(2,1)S(1)}, u32[]{:S(2)}, u32[]{:S(2)}) collective-permute-start(bf16[128,256]{1,0:T(8,128)(2,1)S(1)} %add_convert_fusion), channel_id=1, source_target_pairs={{0,8},{8,16},{16,24},{24,32},{32,40},{40,48},{48,56},{56,64},{64,7... | collective-permute-start | bytes 196616 | tf_op jit(solution)/shard_map/ppermute | solution.py:316
  119.9 0.0 collective-permute-done.16
  119.9 0.0 collective-permute-done.15
  120.0 0.0 collective-permute-done.14
  120.0 16.5 %reduce-scatter.5.cloned.1.call-done = f32[64,128]{1,0:T(8,128)} async-done(((f32[256,128]{1,0:T(8,128)}), f32[64,128]{1,0:T(8,128)}) %reduce-scatter.5.cloned.1.call-update) | async-done | bytes 32784 | tf_op jit(solution)/shard_map/reduce_scatter | solution.py:296
  136.4 1.3 collective-permute-start.17
  137.7 0.0 collective-permute-done.9
  137.8 0.7 copy.15
  138.5 11.5 %all-to-all-start.2 = ((f32[16,4,128]{2,1,0:T(4,128)}), f32[16,4,128]{2,1,0:T(4,128)S(1)}, u32[]{:S(2)}, u32[]{:S(2)}) async-start(f32[16,4,128]{2,1,0:T(4,128)} %bitcast.34), calls=%async_computation.4 | async-start | bytes 65536 | tf_op jit(solution)/shard_map/all_to_all | solution.py:314
  149.9 0.0 collective-permute-done.17
  150.0 18.6 %all-gather.4 = bf16[1024,256]{1,0:T(8,128)(2,1)} all-gather(bf16[128,256]{1,0:T(8,128)(2,1)S(1)} %broadcast_select_fusion), channel_id=6, replica_groups=mesh['y'=8,'x'=4,'zl'=2,'zh'=4,'c'=2] {'zh','c'}, dimensions={0}, use_global_device_ids=true | all-gather | bytes 589824 | tf_op jit(solution)/shard_map/all_gather | solution.py:266
  168.6 0.0 all-to-all-done.2
  168.6 0.6 reduce_sum.29
  169.2 3.4 %shard_map.115 = bf16[1,2,128,512]{3,2,1,0:T(8,128)(2,1)} custom-call(s32[1]{0:T(128)} %bitcast.section, bf16[8,2,128,256]{3,2,1,0:T(8,128)(2,1)} %bitcast.27, bf16[8,128,256]{2,1,0:T(8,128)(2,1)} %bitcast.24, f32[1,2048]{1,0:T(1,128)} %bitcast.33, bf16[1,2,2048,256]{3,2,1,0:T(8,128)(2,1)} %wkv_hbm.3), custom_call_target="tpu_custom_call" | custom-call | flops 536870912 | bytes 5000000 | tf_op jit(solution)/shard_map/pallas_call | solution.py:218
  (16 shorter events, 0.2 us)
Async XLA Ops:
  8.0 62.8 %reduce-scatter.3.cloned.1.call-start = ((), (), s32[]{:S(2)}) async-start(), calls=%async_computation.5 | async-start | bytes 1179648 | tf_op jit(solution)/shard_map/reduce_scatter | solution.py:281
  8.1 4.0 %copy-start.1 = (bf16[1,256,128]{2,1,0:T(8,128)(2,1)S(1)}, bf16[1,256,128]{2,1,0:T(8,128)(2,1)}, u32[]{:S(2)}) copy-start(bf16[1,256,128]{2,1,0:T(8,128)(2,1)} %param.9) | copy-start | bytes 196612
  11.5 78.2 %all-gather.8.cloned.1.call-start = ((), (), s32[]{:S(2)}) async-start(), calls=%async_computation.7 | async-start | bytes 1179648 | tf_op jit(solution)/shard_map/all_gather | solution.py:266
  61.6 9.2 %collective-permute-start = (bf16[128,256]{1,0:T(8,128)(2,1)S(1)}, bf16[128,256]{1,0:T(8,128)(2,1)S(1)}, u32[]{:S(2)}, u32[]{:S(2)}) collective-permute-start(bf16[128,256]{1,0:T(8,128)(2,1)S(1)} %add_convert_fusion.1), channel_id=1, source_target_pairs={{0,8},{8,16},{16,24},{24,32},{32,40},{40,48},{48,56},{56,64},{64,7... | collective-permute-start | bytes 196616 | tf_op jit(solution)/shard_map/ppermute | solution.py:295
  95.2 18.0 %copy-start = (bf16[2,128,256]{2,1,0:T(8,128)(2,1)S(1)}, bf16[2,128,256]{2,1,0:T(8,128)(2,1)}, u32[]{:S(2)}) copy-start(bf16[2,128,256]{2,1,0:T(8,128)(2,1)} %get-tuple-element.16) | copy-start | bytes 393220
  95.2 17.1 %all-to-all-start.1 = ((bf16[8,128,256]{2,1,0:T(8,128)(2,1)}), bf16[8,128,256]{2,1,0:T(8,128)(2,1)S(1)}, u32[]{:S(2)}, u32[]{:S(2)}) async-start(bf16[8,128,256]{2,1,0:T(8,128)(2,1)} %shard_map.114), calls=%async_computation.2 | async-start | bytes 1048576 | tf_op jit(solution)/shard_map/all_to_all | solution.py:269
  99.2 37.2 %reduce-scatter.5.cloned.1.call-start = ((), (), s32[]{:S(2)}) async-start(), calls=%async_computation.6 | async-start | bytes 163840 | tf_op jit(solution)/shard_map/reduce_scatter | solution.py:296
  99.3 2.7 %collective-permute-start.4 = (bf16[128,256]{1,0:T(8,128)(2,1)S(1)}, bf16[128,256]{1,0:T(8,128)(2,1)S(1)}, u32[]{:S(2)}, u32[]{:S(2)}) collective-permute-start(bf16[128,256]{1,0:T(8,128)(2,1)S(1)} %add_convert_fusion.1), channel_id=1, source_target_pairs={{248,312},{249,313},{250,314},{251,315},{252,316},{253,317},{254,3... | collective-permute-start | bytes 196616 | tf_op jit(solution)/shard_map/ppermute | solution.py:236
  99.9 2.0 %collective-permute-start.3 = (bf16[128,256]{1,0:T(8,128)(2,1)S(1)}, bf16[128,256]{1,0:T(8,128)(2,1)S(1)}, u32[]{:S(2)}, u32[]{:S(2)}) collective-permute-start(bf16[128,256]{1,0:T(8,128)(2,1)S(1)} %add_convert_fusion.1), channel_id=1, source_target_pairs={{248,376},{249,377},{250,378},{251,379},{252,380},{253,381},{254,3... | collective-permute-start | bytes 196616 | tf_op jit(solution)/shard_map/ppermute | solution.py:236
  100.6 1.4 collective-permute-start.2
  101.3 0.7 collective-permute-start.1
  102.0 2.0 %collective-permute-start.7 = (bf16[128,256]{1,0:T(8,128)(2,1)S(1)}, bf16[128,256]{1,0:T(8,128)(2,1)S(1)}, u32[]{:S(2)}, u32[]{:S(2)}) collective-permute-start(bf16[128,256]{1,0:T(8,128)(2,1)S(1)} %select_select_fusion.3), channel_id=1, source_target_pairs={{312,264},{376,328},{440,392},{504,456},{313,265},{377,329},{441,3... | collective-permute-start | bytes 196616 | tf_op jit(solution)/shard_map/ppermute | solution.py:242
  102.7 1.4 collective-permute-start.6
  103.4 0.7 collective-permute-start.5
  104.1 5.0 %collective-permute-start.8 = (bf16[128,256]{1,0:T(8,128)(2,1)S(1)}, bf16[128,256]{1,0:T(8,128)(2,1)S(1)}, u32[]{:S(2)}, u32[]{:S(2)}) collective-permute-start(bf16[128,256]{1,0:T(8,128)(2,1)S(1)} %select_select_fusion.2), channel_id=1, source_target_pairs={{264,256},{280,272},{296,288},{312,304},{328,320},{344,336},{360,3... | collective-permute-start | bytes 196616 | tf_op jit(solution)/shard_map/ppermute | solution.py:248
  105.4 63.8 %all-gather.10.cloned.1.call-start = ((), (), s32[]{:S(2)}) async-start(), calls=%async_computation.8 | async-start | bytes 1179648 | tf_op jit(solution)/shard_map/all_gather | solution.py:266
  113.2 2.7 %collective-permute-start.13 = (bf16[128,256]{1,0:T(8,128)(2,1)S(1)}, bf16[128,256]{1,0:T(8,128)(2,1)S(1)}, u32[]{:S(2)}, u32[]{:S(2)}) collective-permute-start(bf16[128,256]{1,0:T(8,128)(2,1)S(1)} %add_convert_fusion), channel_id=1, source_target_pairs={{248,312},{249,313},{250,314},{251,315},{252,316},{253,317},{254,3... | collective-permute-start | bytes 196616 | tf_op jit(solution)/shard_map/ppermute | solution.py:236
  113.9 2.0 %collective-permute-start.12 = (bf16[128,256]{1,0:T(8,128)(2,1)S(1)}, bf16[128,256]{1,0:T(8,128)(2,1)S(1)}, u32[]{:S(2)}, u32[]{:S(2)}) collective-permute-start(bf16[128,256]{1,0:T(8,128)(2,1)S(1)} %add_convert_fusion), channel_id=1, source_target_pairs={{248,376},{249,377},{250,378},{251,379},{252,380},{253,381},{254,3... | collective-permute-start | bytes 196616 | tf_op jit(solution)/shard_map/ppermute | solution.py:236
  114.6 1.4 collective-permute-start.11
  115.2 0.7 collective-permute-start.10
  116.0 3.9 %collective-permute-start.16 = (bf16[128,256]{1,0:T(8,128)(2,1)S(1)}, bf16[128,256]{1,0:T(8,128)(2,1)S(1)}, u32[]{:S(2)}, u32[]{:S(2)}) collective-permute-start(bf16[128,256]{1,0:T(8,128)(2,1)S(1)} %select_select_fusion.1), channel_id=1, source_target_pairs={{312,264},{376,328},{440,392},{504,456},{313,265},{377,329},{441,3... | collective-permute-start | bytes 196616 | tf_op jit(solution)/shard_map/ppermute | solution.py:242
  116.7 3.3 %collective-permute-start.15 = (bf16[128,256]{1,0:T(8,128)(2,1)S(1)}, bf16[128,256]{1,0:T(8,128)(2,1)S(1)}, u32[]{:S(2)}, u32[]{:S(2)}) collective-permute-start(bf16[128,256]{1,0:T(8,128)(2,1)S(1)} %select_select_fusion.1), channel_id=1, source_target_pairs={{312,280},{376,344},{440,408},{504,472},{313,281},{377,345},{441,4... | collective-permute-start | bytes 196616 | tf_op jit(solution)/shard_map/ppermute | solution.py:242
  117.3 2.6 %collective-permute-start.14 = (bf16[128,256]{1,0:T(8,128)(2,1)S(1)}, bf16[128,256]{1,0:T(8,128)(2,1)S(1)}, u32[]{:S(2)}, u32[]{:S(2)}) collective-permute-start(bf16[128,256]{1,0:T(8,128)(2,1)S(1)} %select_select_fusion.1), channel_id=1, source_target_pairs={{312,296},{376,360},{440,424},{504,488},{313,297},{377,361},{441,4... | collective-permute-start | bytes 196616 | tf_op jit(solution)/shard_map/ppermute | solution.py:242
  118.0 19.7 %collective-permute-start.9 = (bf16[128,256]{1,0:T(8,128)(2,1)S(1)}, bf16[128,256]{1,0:T(8,128)(2,1)S(1)}, u32[]{:S(2)}, u32[]{:S(2)}) collective-permute-start(bf16[128,256]{1,0:T(8,128)(2,1)S(1)} %add_convert_fusion), channel_id=1, source_target_pairs={{0,8},{8,16},{16,24},{24,32},{32,40},{40,48},{48,56},{56,64},{64,7... | collective-permute-start | bytes 196616 | tf_op jit(solution)/shard_map/ppermute | solution.py:316
  136.4 13.5 %collective-permute-start.17 = (bf16[128,256]{1,0:T(8,128)(2,1)S(1)}, bf16[128,256]{1,0:T(8,128)(2,1)S(1)}, u32[]{:S(2)}, u32[]{:S(2)}) collective-permute-start(bf16[128,256]{1,0:T(8,128)(2,1)S(1)} %select_select_fusion), channel_id=1, source_target_pairs={{264,256},{280,272},{296,288},{312,304},{328,320},{344,336},{360,3... | collective-permute-start | bytes 196616 | tf_op jit(solution)/shard_map/ppermute | solution.py:248
  138.5 30.1 %all-to-all-start.2 = ((f32[16,4,128]{2,1,0:T(4,128)}), f32[16,4,128]{2,1,0:T(4,128)S(1)}, u32[]{:S(2)}, u32[]{:S(2)}) async-start(f32[16,4,128]{2,1,0:T(4,128)} %bitcast.34), calls=%async_computation.4 | async-start | bytes 65536 | tf_op jit(solution)/shard_map/all_to_all | solution.py:314
Sparse Core Ops, SparseCore 0:
  11.7 39.3 reduce-scatter.2
  105.5 30.8 reduce-scatter.4
Sparse Core Ops, SparseCore 1:
  14.1 41.9 all-gather.7
  113.2 37.7 all-gather.9

commit v9 on v5

--- a/solution.py
+++ b/solution.py
@@ -84,11 +84,6 @@
     get_gain.wait()
     if tick == 0:
         norm_into(normed, x, gain)
-        get_fresh.wait()
-        for h in range(fresh.shape[0]):
-            turned[h] = fresh[h].T
-        put_turned = copy(7, turned, turned_hbm)
-        put_turned.start()
     else:
         get_fresh = copy(6, fresh_hbm.at[:, 1], fresh)
         get_final = copy(7, final_hbm, final_gain)
@@ -136,10 +131,14 @@
         out[h] = jnp.dot(
             attn, wo[:, h * width : (h + 1) * width], preferred_element_type=F32
         ).astype(BF)
-        puts.append(copy(8 + h, out.at[h], out_hbm.at[h]))
+        puts.append(copy(8 + h, out.at[h], out_hbm.at[h % C * ZH + h // C]))
         puts[-1].start()
     if tick == 0:
-        put_turned.wait()
+        get_fresh.wait()
+        for h in range(fresh.shape[0]):
+            turned[h] = fresh[h].T
+        puts.append(copy(7, turned, turned_hbm))
+        puts[-1].start()
     for put in puts:
         put.wait()
 
@@ -181,6 +180,7 @@
 def memory_kernel(half, section, first_hbm, second_hbm, final_hbm, wkv_hbm, out_hbm, sources, rows,
                   final_gain, wkv, out, sems):
     width = wkv.shape[2]
+    tokens = sources.shape[2]
 
     def copy(k, source, target):
         return pltpu.make_async_copy(source, target, sems.at[k])
@@ -199,11 +199,12 @@
         for get in gets[:3]:
             get.wait()
         for t in range(TICKS):
-            norm_into(rows.at[t], sources.at[t], final_gain)
+            norm_into(rows.at[:, t * tokens : (t + 1) * tokens], sources.at[t], final_gain)
         gets[3].wait()
-        for t in range(TICKS):
-            out[t, :, :width] = project(rows.at[t], wkv.at[0])
-            out[t, :, width:] = project(rows.at[t], wkv.at[1])
+        for part in range(2):
+            both = project(rows, wkv.at[part])
+            for t in range(TICKS):
+                out[t, :, part * width : (part + 1) * width] = both[t * tokens : (t + 1) * tokens]
 
     @pl.when(section[0] < half)
     def _():
@@ -266,7 +267,9 @@
         return lax.all_gather(block, HEAD, axis=0)
 
     def exchanged(parts):
-        return lax.all_to_all(parts, HEAD, 0, 0, tiled=True)
+        parts = lax.all_to_all(parts.reshape((C, ZH) + parts.shape[1:]), "c", 0, 0, tiled=True)
+        parts = jnp.sum(parts.astype(F32), axis=0).astype(BF)
+        return lax.all_to_all(parts, "zh", 0, 0, tiled=True)
 
     def summed(parts, current):
         return (current.astype(F32) + jnp.sum(parts.astype(F32), axis=0)).astype(BF)
@@ -321,7 +324,7 @@
         functools.partial(memory_kernel, half), section,
         (first_memory, second_memory, final_scale, w_kv),
         ((1, TICKS, tokens, 2 * width),),
-        (((TICKS,) + rows8, BF), ((TICKS,) + rows8, BF), ((1, depth), F32),
+        (((TICKS,) + rows8, BF), ((heads, TICKS * tokens, width), BF), ((1, depth), F32),
          ((2, depth, width), BF), ((TICKS,) + pair_shape, BF)),
         5, flops,
     )

time: 174 us -> 176 us (1.011)
  the two profiles are of different devices: /device:TPU:41 before, /device:TPU:47 now
where the time goes in v9:
time: 176 us; the launch traced here: 175 us
  blocking collectives  70.2 us (40%)
  starting transfers between devices  52.2 us (30%)
  waiting for transfers between devices  18.5 us (11%)
  between operations  15.9 us (9%)
  Pallas kernels  13.6 us (8%)
  other arithmetic  3.24 us (2%)
    all_gather x3, blocking collectives, whole(): return lax.all_gather(block, HEAD, axis=0)  60.2 us
    ppermute x2, starting transfers between devices, body(): passed = lax.ppermute(output, PIPE, shift)  17.9 us
    all_to_all x1, starting transfers between devices, body(): share = lax.all_to_all(share, PIPE[1:] + HEAD, 0, 0, tiled=True)  14 us
    pallas_call x4, Pallas kernels, call(): pl.pallas_call(kernel, out_shape=[jax.ShapeDtypeStruct(shape, kind) for s...  13.6 us
    ppermute x2, waiting for transfers between devices, spread(): return (jnp.where(zl == sz, held, lax.ppermute(held, PIPE, pairs)), beside)  12.5 us
    all_to_all x2, blocking collectives, exchanged(): lax.all_to_all(parts.reshape((C, ZH) + parts.shape[1:]), 'c', 0, 0, tiled...  10 us
    all_to_all x2, starting transfers between devices, exchanged(): return lax.all_to_all(parts, 'zh', 0, 0, tiled=True)  8.41 us
    ppermute x8, starting transfers between devices, spread(): sent = lax.ppermute(block, PIPE, [(source, place(to, sx, sz))])  5.32 us
  transfers between devices with their start and end apart: 24, of which 2 were waited for; matrix products, arithmetic and copies ran while one was open for 3% of the time, Pallas kernels for 6%

profile of v9, /device:TPU:47, one launch (start us, length us, event | category | flops | bytes accessed | tf_op | source)
XLA Modules:
  0.0 175.4 jit_solution(10274280595438352660)
XLA Ops:
  8.0 0.0 all-gather.8.cloned.1.call-start
  8.0 0.7 all-gather.8.cloned.1.call-update
  8.7 0.9 copy.16
  9.7 22.2 %all-gather = bf16[1024,256]{1,0:T(8,128)(2,1)} all-gather(bf16[128,256]{1,0:T(8,128)(2,1)S(1)} %bitcast.32), channel_id=2, replica_groups=mesh['y'=8,'x'=4,'zl'=2,'zh'=4,'c'=2] {'zh','c'}, dimensions={0}, use_global_device_ids=true | all-gather | bytes 589824 | tf_op jit(solution)/shard_map/all_gather | solution.py:267
  31.9 3.4 %shard_map.112 = (bf16[8,128,256]{2,1,0:T(8,128)(2,1)}, bf16[2,128,256]{2,1,0:T(8,128)(2,1)}) custom-call(s32[1]{0:T(128)} %bitcast.section, bf16[8,128,256]{2,1,0:T(8,128)(2,1)} %bitcast.28, bf16[2,256,128]{2,1,0:T(8,128)(2,1)} %fresh.1, f32[1,2048]{1,0:T(1,128)} %gain.3, bf16[1,2048,256]{2,1,0:T(8,128)(2,1)} %wq.3, bf16[1,2,2048,256]{3,2,1,0:T(8,128)(2,1)} %wkv_hbm.3, ...), custom_call_target="tpu_custom_call" | custom-call | flops 536870912 | bytes 5000000 | tf_op jit(solution)/shard_map/pallas_call | solution.py:219
  35.3 5.0 %all_to_all.25 = bf16[2,4,128,256]{3,2,1,0:T(8,128)(2,1)S(1)} all-to-all(bf16[2,4,128,256]{3,2,1,0:T(8,128)(2,1)} %bitcast.34), channel_id=1, replica_groups=mesh['y'=8,'x'=4,'zl'=2,'zh'=4,'c'=2] {'c'}, dimensions={0} | all-to-all | bytes 1048576 | tf_op jit(solution)/shard_map/all_to_all | solution.py:270
  40.3 0.8 reduce_sum.51
  41.1 4.8 %all-to-all-start.1 = ((bf16[4,128,256]{2,1,0:T(8,128)(2,1)}), bf16[4,128,256]{2,1,0:T(8,128)(2,1)S(1)}, u32[]{:S(2)}, u32[]{:S(2)}) async-start(bf16[4,128,256]{2,1,0:T(8,128)(2,1)} %reduce_sum.51), calls=%async_computation.1 | async-start | bytes 524288 | tf_op jit(solution)/shard_map/all_to_all | solution.py:272
  46.0 0.0 reduce-scatter.2.cloned.1.call-start
  46.0 3.4 %shard_map.114 = f32[2048,128]{1,0:T(8,128)} custom-call(s32[1]{0:T(128)} %bitcast.section, bf16[1,128,512]{2,1,0:T(8,128)(2,1)} %grads_hbm.1, bf16[1,2,2048,256]{3,2,1,0:T(8,128)(2,1)} %wkv_hbm.3), custom_call_target="tpu_custom_call" | custom-call | flops 536870912 | bytes 5000000 | tf_op jit(solution)/shard_map/pallas_call | solution.py:219
  49.4 0.0 reduce-scatter.2.cloned.1.call-update
  49.4 5.2 %all-to-all-done.1 = bf16[4,128,256]{2,1,0:T(8,128)(2,1)S(1)} async-done(((bf16[4,128,256]{2,1,0:T(8,128)(2,1)}), bf16[4,128,256]{2,1,0:T(8,128)(2,1)S(1)}, u32[]{:S(2)}, u32[]{:S(2)}) %all-to-all-start.1) | async-done | bytes 262176 | tf_op jit(solution)/shard_map/all_to_all | solution.py:272
  54.7 0.7 collective-permute-start.1
  55.4 0.7 collective-permute-start.2
  56.0 0.7 collective-permute-start.3
  56.7 0.7 collective-permute-start.4
  57.4 5.1 %collective-permute-start = (bf16[128,256]{1,0:T(8,128)(2,1)S(1)}, bf16[128,256]{1,0:T(8,128)(2,1)S(1)}, u32[]{:S(2)}, u32[]{:S(2)}) collective-permute-start(bf16[128,256]{1,0:T(8,128)(2,1)S(1)} %add_convert_fusion.1), channel_id=1, source_target_pairs={{0,8},{8,16},{16,24},{24,32},{32,40},{40,48},{48,56},{56,64},{64,7... | collective-permute-start | bytes 196616 | tf_op jit(solution)/shard_map/ppermute | solution.py:299
  62.5 0.0 collective-permute-done.1
  62.6 0.0 collective-permute-done.2
  62.6 0.0 collective-permute-done.3
  62.6 0.0 collective-permute-done.4
  62.6 0.7 collective-permute-start.5
  63.3 0.7 collective-permute-start.6
  64.0 0.7 collective-permute-start.7
  64.6 0.0 collective-permute-done
  64.6 0.0 copy-done
  64.7 19.1 %all-gather.1 = bf16[1024,256]{1,0:T(8,128)(2,1)} all-gather(bf16[128,256]{1,0:T(8,128)(2,1)S(1)} %bitcast_select_fusion), channel_id=3, replica_groups=mesh['y'=8,'x'=4,'zl'=2,'zh'=4,'c'=2] {'zh','c'}, dimensions={0}, use_global_device_ids=true | all-gather | bytes 589824 | tf_op jit(solution)/shard_map/all_gather | solution.py:267
  83.7 3.3 %shard_map.113 = bf16[8,128,256]{2,1,0:T(8,128)(2,1)} custom-call(s32[1]{0:T(128)} %bitcast.section, bf16[8,128,256]{2,1,0:T(8,128)(2,1)} %bitcast.27, bf16[8,2,256,128]{3,2,1,0:T(8,128)(2,1)} %bitcast.30, f32[1,2048]{1,0:T(1,128)} %gain.3, f32[1,2048]{1,0:T(1,128)} %bitcast.37, bf16[1,2048,256]{2,1,0:T(8,128)(2,1)} %wq.3, ...), custom_call_target="tpu_custom_call" | custom-call | flops 536870912 | bytes 5000000 | tf_op jit(solution)/shard_map/pallas_call | solution.py:219
  87.1 5.0 %all_to_all.26 = bf16[2,4,128,256]{3,2,1,0:T(8,128)(2,1)S(1)} all-to-all(bf16[2,4,128,256]{3,2,1,0:T(8,128)(2,1)} %bitcast.29), channel_id=1, replica_groups=mesh['y'=8,'x'=4,'zl'=2,'zh'=4,'c'=2] {'c'}, dimensions={0} | all-to-all | bytes 1048576 | tf_op jit(solution)/shard_map/all_to_all | solution.py:270
  92.1 0.8 reduce_sum.53
  92.9 3.6 %all-to-all-start.3 = ((bf16[4,128,256]{2,1,0:T(8,128)(2,1)}), bf16[4,128,256]{2,1,0:T(8,128)(2,1)S(1)}, u32[]{:S(2)}, u32[]{:S(2)}) async-start(bf16[4,128,256]{2,1,0:T(8,128)(2,1)} %reduce_sum.53), calls=%async_computation.3 | async-start | bytes 524288 | tf_op jit(solution)/shard_map/all_to_all | solution.py:272
  96.5 0.0 collective-permute-done.5
  96.5 0.0 collective-permute-done.6
  96.5 0.0 collective-permute-done.7
  96.6 1.3 collective-permute-start.8
  97.9 12.5 %collective-permute-done.8 = bf16[128,256]{1,0:T(8,128)(2,1)S(1)} collective-permute-done((bf16[128,256]{1,0:T(8,128)(2,1)S(1)}, bf16[128,256]{1,0:T(8,128)(2,1)S(1)}, u32[]{:S(2)}, u32[]{:S(2)}) %collective-permute-start.8) | collective-permute-done | bytes 65568 | tf_op jit(solution)/shard_map/ppermute | solution.py:249
  110.4 0.0 all-to-all-done.3
  110.4 0.7 pad_maximum_fusion
  111.1 0.0 all-gather.10.cloned.1.call-update
  111.2 0.7 collective-permute-start.10
  111.9 0.7 collective-permute-start.11
  112.6 0.7 collective-permute-start.12
  113.2 0.7 collective-permute-start.13
  113.9 0.0 collective-permute-done.10
  113.9 0.0 collective-permute-done.11
  113.9 0.0 collective-permute-done.12
  113.9 0.0 collective-permute-done.13
  114.0 0.7 collective-permute-start.14
  114.6 0.7 collective-permute-start.15
  115.3 0.7 collective-permute-start.16
  116.0 12.7 %collective-permute-start.9 = (bf16[128,256]{1,0:T(8,128)(2,1)S(1)}, bf16[128,256]{1,0:T(8,128)(2,1)S(1)}, u32[]{:S(2)}, u32[]{:S(2)}) collective-permute-start(bf16[128,256]{1,0:T(8,128)(2,1)S(1)} %add_convert_fusion), channel_id=1, source_target_pairs={{0,8},{8,16},{16,24},{24,32},{32,40},{40,48},{48,56},{56,64},{64,7... | collective-permute-start | bytes 196616 | tf_op jit(solution)/shard_map/ppermute | solution.py:318
  128.7 0.0 collective-permute-done.14
  128.7 0.0 collective-permute-done.15
  128.8 0.0 collective-permute-done.16
  128.8 0.0 reduce-scatter.2.cloned.1.call-done
  128.8 1.3 collective-permute-start.17
  130.1 0.0 collective-permute-done.9
  130.2 0.7 copy.17
  130.9 14.0 %all-to-all-start.4 = ((f32[64,4,128]{2,1,0:T(4,128)}), f32[64,4,128]{2,1,0:T(4,128)S(1)}, u32[]{:S(2)}, u32[]{:S(2)}) async-start(f32[64,4,128]{2,1,0:T(4,128)} %bitcast.36), calls=%async_computation.5 | async-start | bytes 262144 | tf_op jit(solution)/shard_map/all_to_all | solution.py:316
  144.9 0.0 collective-permute-done.17
  145.0 18.9 %all-gather.4 = bf16[1024,256]{1,0:T(8,128)(2,1)} all-gather(bf16[128,256]{1,0:T(8,128)(2,1)S(1)} %broadcast_select_fusion), channel_id=6, replica_groups=mesh['y'=8,'x'=4,'zl'=2,'zh'=4,'c'=2] {'zh','c'}, dimensions={0}, use_global_device_ids=true | all-gather | bytes 589824 | tf_op jit(solution)/shard_map/all_gather | solution.py:267
  163.9 0.0 all-to-all-done.4
  163.9 0.7 reduce_sum.55
  164.6 3.4 %shard_map.115 = bf16[1,2,128,512]{3,2,1,0:T(8,128)(2,1)} custom-call(s32[1]{0:T(128)} %bitcast.section, bf16[8,2,128,256]{3,2,1,0:T(8,128)(2,1)} %bitcast.31, bf16[8,128,256]{2,1,0:T(8,128)(2,1)} %bitcast.26, f32[1,2048]{1,0:T(1,128)} %bitcast.38, bf16[1,2,2048,256]{3,2,1,0:T(8,128)(2,1)} %wkv_hbm.3), custom_call_target="tpu_custom_call" | custom-call | flops 536870912 | bytes 5000000 | tf_op jit(solution)/shard_map/pallas_call | solution.py:219
  (16 shorter events, 0.3 us)
Async XLA Ops:
  8.0 75.7 %all-gather.8.cloned.1.call-start = ((), (), s32[]{:S(2)}) async-start(), calls=%async_computation.7 | async-start | bytes 1179648 | tf_op jit(solution)/shard_map/all_gather | solution.py:267
  41.1 13.5 %all-to-all-start.1 = ((bf16[4,128,256]{2,1,0:T(8,128)(2,1)}), bf16[4,128,256]{2,1,0:T(8,128)(2,1)S(1)}, u32[]{:S(2)}, u32[]{:S(2)}) async-start(bf16[4,128,256]{2,1,0:T(8,128)(2,1)} %reduce_sum.51), calls=%async_computation.1 | async-start | bytes 524288 | tf_op jit(solution)/shard_map/all_to_all | solution.py:272
  46.0 18.7 %copy-start = (bf16[2,128,256]{2,1,0:T(8,128)(2,1)S(1)}, bf16[2,128,256]{2,1,0:T(8,128)(2,1)}, u32[]{:S(2)}) copy-start(bf16[2,128,256]{2,1,0:T(8,128)(2,1)} %get-tuple-element.11) | copy-start | bytes 393220
  46.0 82.9 %reduce-scatter.2.cloned.1.call-start = ((), (), s32[]{:S(2)}) async-start(), calls=%async_computation.6 | async-start | bytes 1179648 | tf_op jit(solution)/shard_map/reduce_scatter | solution.py:294
  54.7 7.9 %collective-permute-start.1 = (bf16[128,256]{1,0:T(8,128)(2,1)S(1)}, bf16[128,256]{1,0:T(8,128)(2,1)S(1)}, u32[]{:S(2)}, u32[]{:S(2)}) collective-permute-start(bf16[128,256]{1,0:T(8,128)(2,1)S(1)} %add_convert_fusion.1), channel_id=1, source_target_pairs={{248,504},{249,505},{250,506},{251,507},{252,508},{253,509},{254,5... | collective-permute-start | bytes 196616 | tf_op jit(solution)/shard_map/ppermute | solution.py:237
  55.4 7.2 %collective-permute-start.2 = (bf16[128,256]{1,0:T(8,128)(2,1)S(1)}, bf16[128,256]{1,0:T(8,128)(2,1)S(1)}, u32[]{:S(2)}, u32[]{:S(2)}) collective-permute-start(bf16[128,256]{1,0:T(8,128)(2,1)S(1)} %add_convert_fusion.1), channel_id=1, source_target_pairs={{248,440},{249,441},{250,442},{251,443},{252,444},{253,445},{254,4... | collective-permute-start | bytes 196616 | tf_op jit(solution)/shard_map/ppermute | solution.py:237
  56.0 6.5 %collective-permute-start.3 = (bf16[128,256]{1,0:T(8,128)(2,1)S(1)}, bf16[128,256]{1,0:T(8,128)(2,1)S(1)}, u32[]{:S(2)}, u32[]{:S(2)}) collective-permute-start(bf16[128,256]{1,0:T(8,128)(2,1)S(1)} %add_convert_fusion.1), channel_id=1, source_target_pairs={{248,376},{249,377},{250,378},{251,379},{252,380},{253,381},{254,3... | collective-permute-start | bytes 196616 | tf_op jit(solution)/shard_map/ppermute | solution.py:237
  56.7 5.9 %collective-permute-start.4 = (bf16[128,256]{1,0:T(8,128)(2,1)S(1)}, bf16[128,256]{1,0:T(8,128)(2,1)S(1)}, u32[]{:S(2)}, u32[]{:S(2)}) collective-permute-start(bf16[128,256]{1,0:T(8,128)(2,1)S(1)} %add_convert_fusion.1), channel_id=1, source_target_pairs={{248,312},{249,313},{250,314},{251,315},{252,316},{253,317},{254,3... | collective-permute-start | bytes 196616 | tf_op jit(solution)/shard_map/ppermute | solution.py:237
  57.4 7.2 %collective-permute-start = (bf16[128,256]{1,0:T(8,128)(2,1)S(1)}, bf16[128,256]{1,0:T(8,128)(2,1)S(1)}, u32[]{:S(2)}, u32[]{:S(2)}) collective-permute-start(bf16[128,256]{1,0:T(8,128)(2,1)S(1)} %add_convert_fusion.1), channel_id=1, source_target_pairs={{0,8},{8,16},{16,24},{24,32},{32,40},{40,48},{48,56},{56,64},{64,7... | collective-permute-start | bytes 196616 | tf_op jit(solution)/shard_map/ppermute | solution.py:299
  62.6 33.9 %collective-permute-start.5 = (bf16[128,256]{1,0:T(8,128)(2,1)S(1)}, bf16[128,256]{1,0:T(8,128)(2,1)S(1)}, u32[]{:S(2)}, u32[]{:S(2)}) collective-permute-start(bf16[128,256]{1,0:T(8,128)(2,1)S(1)} %select_select_fusion.3), channel_id=1, source_target_pairs={{312,296},{376,360},{440,424},{504,488},{313,297},{377,361},{441,4... | collective-permute-start | bytes 196616 | tf_op jit(solution)/shard_map/ppermute | solution.py:243
  63.3 33.2 %collective-permute-start.6 = (bf16[128,256]{1,0:T(8,128)(2,1)S(1)}, bf16[128,256]{1,0:T(8,128)(2,1)S(1)}, u32[]{:S(2)}, u32[]{:S(2)}) collective-permute-start(bf16[128,256]{1,0:T(8,128)(2,1)S(1)} %select_select_fusion.3), channel_id=1, source_target_pairs={{312,280},{376,344},{440,408},{504,472},{313,281},{377,345},{441,4... | collective-permute-start | bytes 196616 | tf_op jit(solution)/shard_map/ppermute | solution.py:243
  64.0 32.6 %collective-permute-start.7 = (bf16[128,256]{1,0:T(8,128)(2,1)S(1)}, bf16[128,256]{1,0:T(8,128)(2,1)S(1)}, u32[]{:S(2)}, u32[]{:S(2)}) collective-permute-start(bf16[128,256]{1,0:T(8,128)(2,1)S(1)} %select_select_fusion.3), channel_id=1, source_target_pairs={{312,264},{376,328},{440,392},{504,456},{313,265},{377,329},{441,3... | collective-permute-start | bytes 196616 | tf_op jit(solution)/shard_map/ppermute | solution.py:243
  92.9 17.5 %all-to-all-start.3 = ((bf16[4,128,256]{2,1,0:T(8,128)(2,1)}), bf16[4,128,256]{2,1,0:T(8,128)(2,1)S(1)}, u32[]{:S(2)}, u32[]{:S(2)}) async-start(bf16[4,128,256]{2,1,0:T(8,128)(2,1)} %reduce_sum.53), calls=%async_computation.3 | async-start | bytes 524288 | tf_op jit(solution)/shard_map/all_to_all | solution.py:272
  96.5 68.0 %all-gather.10.cloned.1.call-start = ((), (), s32[]{:S(2)}) async-start(), calls=%async_computation.8 | async-start | bytes 1179648 | tf_op jit(solution)/shard_map/all_gather | solution.py:267
  96.6 13.8 %collective-permute-start.8 = (bf16[128,256]{1,0:T(8,128)(2,1)S(1)}, bf16[128,256]{1,0:T(8,128)(2,1)S(1)}, u32[]{:S(2)}, u32[]{:S(2)}) collective-permute-start(bf16[128,256]{1,0:T(8,128)(2,1)S(1)} %select_select_fusion.2), channel_id=1, source_target_pairs={{264,256},{280,272},{296,288},{312,304},{328,320},{344,336},{360,3... | collective-permute-start | bytes 196616 | tf_op jit(solution)/shard_map/ppermute | solution.py:249
  111.2 2.7 %collective-permute-start.10 = (bf16[128,256]{1,0:T(8,128)(2,1)S(1)}, bf16[128,256]{1,0:T(8,128)(2,1)S(1)}, u32[]{:S(2)}, u32[]{:S(2)}) collective-permute-start(bf16[128,256]{1,0:T(8,128)(2,1)S(1)} %add_convert_fusion), channel_id=1, source_target_pairs={{248,504},{249,505},{250,506},{251,507},{252,508},{253,509},{254,5... | collective-permute-start | bytes 196616 | tf_op jit(solution)/shard_map/ppermute | solution.py:237
  111.9 2.0 %collective-permute-start.11 = (bf16[128,256]{1,0:T(8,128)(2,1)S(1)}, bf16[128,256]{1,0:T(8,128)(2,1)S(1)}, u32[]{:S(2)}, u32[]{:S(2)}) collective-permute-start(bf16[128,256]{1,0:T(8,128)(2,1)S(1)} %add_convert_fusion), channel_id=1, source_target_pairs={{248,440},{249,441},{250,442},{251,443},{252,444},{253,445},{254,4... | collective-permute-start | bytes 196616 | tf_op jit(solution)/shard_map/ppermute | solution.py:237
  112.6 1.4 collective-permute-start.12
  113.2 0.7 collective-permute-start.13
  114.0 14.8 %collective-permute-start.14 = (bf16[128,256]{1,0:T(8,128)(2,1)S(1)}, bf16[128,256]{1,0:T(8,128)(2,1)S(1)}, u32[]{:S(2)}, u32[]{:S(2)}) collective-permute-start(bf16[128,256]{1,0:T(8,128)(2,1)S(1)} %select_select_fusion.1), channel_id=1, source_target_pairs={{312,296},{376,360},{440,424},{504,488},{313,297},{377,361},{441,4... | collective-permute-start | bytes 196616 | tf_op jit(solution)/shard_map/ppermute | solution.py:243
  114.6 14.1 %collective-permute-start.15 = (bf16[128,256]{1,0:T(8,128)(2,1)S(1)}, bf16[128,256]{1,0:T(8,128)(2,1)S(1)}, u32[]{:S(2)}, u32[]{:S(2)}) collective-permute-start(bf16[128,256]{1,0:T(8,128)(2,1)S(1)} %select_select_fusion.1), channel_id=1, source_target_pairs={{312,280},{376,344},{440,408},{504,472},{313,281},{377,345},{441,4... | collective-permute-start | bytes 196616 | tf_op jit(solution)/shard_map/ppermute | solution.py:243
  115.3 13.4 %collective-permute-start.16 = (bf16[128,256]{1,0:T(8,128)(2,1)S(1)}, bf16[128,256]{1,0:T(8,128)(2,1)S(1)}, u32[]{:S(2)}, u32[]{:S(2)}) collective-permute-start(bf16[128,256]{1,0:T(8,128)(2,1)S(1)} %select_select_fusion.1), channel_id=1, source_target_pairs={{312,264},{376,328},{440,392},{504,456},{313,265},{377,329},{441,3... | collective-permute-start | bytes 196616 | tf_op jit(solution)/shard_map/ppermute | solution.py:243
  116.0 14.1 %collective-permute-start.9 = (bf16[128,256]{1,0:T(8,128)(2,1)S(1)}, bf16[128,256]{1,0:T(8,128)(2,1)S(1)}, u32[]{:S(2)}, u32[]{:S(2)}) collective-permute-start(bf16[128,256]{1,0:T(8,128)(2,1)S(1)} %add_convert_fusion), channel_id=1, source_target_pairs={{0,8},{8,16},{16,24},{24,32},{32,40},{40,48},{48,56},{56,64},{64,7... | collective-permute-start | bytes 196616 | tf_op jit(solution)/shard_map/ppermute | solution.py:318
  128.8 16.1 %collective-permute-start.17 = (bf16[128,256]{1,0:T(8,128)(2,1)S(1)}, bf16[128,256]{1,0:T(8,128)(2,1)S(1)}, u32[]{:S(2)}, u32[]{:S(2)}) collective-permute-start(bf16[128,256]{1,0:T(8,128)(2,1)S(1)} %select_select_fusion), channel_id=1, source_target_pairs={{264,256},{280,272},{296,288},{312,304},{328,320},{344,336},{360,3... | collective-permute-start | bytes 196616 | tf_op jit(solution)/shard_map/ppermute | solution.py:249
  130.9 33.0 %all-to-all-start.4 = ((f32[64,4,128]{2,1,0:T(4,128)}), f32[64,4,128]{2,1,0:T(4,128)S(1)}, u32[]{:S(2)}, u32[]{:S(2)}) async-start(f32[64,4,128]{2,1,0:T(4,128)} %bitcast.36), calls=%async_computation.5 | async-start | bytes 262144 | tf_op jit(solution)/shard_map/all_to_all | solution.py:316
Sparse Core Ops, SparseCore 0:
  11.0 37.6 all-gather.7
  111.2 36.1 all-gather.9
Sparse Core Ops, SparseCore 1:
  49.5 35.5 reduce-scatter.1

commit v10 on v9

--- a/solution.py
+++ b/solution.py
@@ -236,13 +236,13 @@
     for to in range(sy + 1, Y):
         sent = lax.ppermute(block, PIPE, [(source, place(to, sx, sz))])
         held = jnp.where(y == to, sent, held)
+    if beside is not None:
+        held, beside = lax.optimization_barrier((held, beside))
     column = held
     for to in range(X):
         if to != sx:
             pairs = [(place(k, sx, sz), place(k, to, sz)) for k in range(sy + 1, Y)]
             held = jnp.where(x == to, lax.ppermute(column, PIPE, pairs), held)
-    if beside is not None:
-        held, beside = lax.optimization_barrier((held, beside))
     pairs = [
         (place(k, to, sz), place(k, to, 1 - sz)) for k in range(sy + 1, Y) for to in range(X)
     ]
@@ -312,12 +312,13 @@
     current = jnp.where(place_here == half, fresh_rows[1], current)
     parts, first_memory = lax.optimization_barrier((exchanged(parts), first_memory))
     output = summed(parts, current)
+    output, share = lax.optimization_barrier((output, share))
+    share = lax.all_to_all(share, PIPE[1:] + HEAD, 0, 0, tiled=True)
     second_memory, share = spread(output, half - 1, share)
-    share = lax.all_to_all(share, PIPE[1:] + HEAD, 0, 0, tiled=True)
     first_memory = whole(jnp.stack([first_memory, entering]))
     passed = lax.ppermute(output, PIPE, shift)
     last = jnp.where(place_here == half, jnp.zeros_like(passed), passed)
-    share, second_memory = lax.optimization_barrier((share, whole(second_memory)))
+    second_memory = whole(second_memory)
     memory_grad = jnp.sum(share, axis=0)
 
     (new_kv,) = call(

time: 176 us -> 181 us (1.028)
  the two profiles are of different devices: /device:TPU:47 before, /device:TPU:25 now
where the time goes in v10:
time: 181 us; the launch traced here: 180 us
  blocking collectives  69.8 us (39%)
  starting transfers between devices  41.3 us (23%)
  waiting for transfers between devices  38.3 us (21%)
  between operations  15.9 us (9%)
  Pallas kernels  10.2 us (6%)
  other arithmetic  3.23 us (2%)
    all_gather x3, blocking collectives, whole(): return lax.all_gather(block, HEAD, axis=0)  59.7 us
    all_to_all x2, waiting for transfers between devices, exchanged(): return lax.all_to_all(parts, 'zh', 0, 0, tiled=True)  16.4 us
    all_to_all x1, starting transfers between devices, body(): share = lax.all_to_all(share, PIPE[1:] + HEAD, 0, 0, tiled=True)  15.8 us
    all_to_all x1, waiting for transfers between devices, body(): share = lax.all_to_all(share, PIPE[1:] + HEAD, 0, 0, tiled=True)  13.3 us
    pallas_call x4, Pallas kernels, call(): pl.pallas_call(kernel, out_shape=[jax.ShapeDtypeStruct(shape, kind) for s...  10.2 us
    all_to_all x2, blocking collectives, exchanged(): lax.all_to_all(parts.reshape((C, ZH) + parts.shape[1:]), 'c', 0, 0, tiled...  10.1 us
    all_to_all x2, starting transfers between devices, exchanged(): return lax.all_to_all(parts, 'zh', 0, 0, tiled=True)  8.2 us
    ppermute x2, waiting for transfers between devices, body(): passed = lax.ppermute(output, PIPE, shift)  7.75 us
  transfers between devices with their start and end apart: 24, of which 5 were waited for; matrix products, arithmetic and copies ran while one was open for 3% of the time, Pallas kernels for 5%

profile of v10, /device:TPU:25, one launch (start us, length us, event | category | flops | bytes accessed | tf_op | source)
XLA Modules:
  0.0 180.4 jit_solution(43213595777243124)
XLA Ops:
  8.0 0.0 all-gather.8.cloned.1.call-start
  8.0 0.7 all-gather.8.cloned.1.call-update
  8.7 0.9 copy.16
  9.7 22.2 %all-gather = bf16[1024,256]{1,0:T(8,128)(2,1)} all-gather(bf16[128,256]{1,0:T(8,128)(2,1)S(1)} %bitcast.32), channel_id=2, replica_groups=mesh['y'=8,'x'=4,'zl'=2,'zh'=4,'c'=2] {'zh','c'}, dimensions={0}, use_global_device_ids=true | all-gather | bytes 589824 | tf_op jit(solution)/shard_map/all_gather | solution.py:267
  31.9 4.2 %shard_map.112 = (bf16[8,128,256]{2,1,0:T(8,128)(2,1)}, bf16[2,128,256]{2,1,0:T(8,128)(2,1)}) custom-call(s32[1]{0:T(128)} %bitcast.section, bf16[8,128,256]{2,1,0:T(8,128)(2,1)} %bitcast.28, bf16[2,256,128]{2,1,0:T(8,128)(2,1)} %fresh.1, f32[1,2048]{1,0:T(1,128)} %gain.3, bf16[1,2048,256]{2,1,0:T(8,128)(2,1)} %wq.3, bf16[1,2,2048,256]{3,2,1,0:T(8,128)(2,1)} %wkv_hbm.3, ...), custom_call_target="tpu_custom_call" | custom-call | flops 536870912 | bytes 5000000 | tf_op jit(solution)/shard_map/pallas_call | solution.py:219
  36.1 5.1 %all_to_all.25 = bf16[2,4,128,256]{3,2,1,0:T(8,128)(2,1)S(1)} all-to-all(bf16[2,4,128,256]{3,2,1,0:T(8,128)(2,1)} %bitcast.34), channel_id=1, replica_groups=mesh['y'=8,'x'=4,'zl'=2,'zh'=4,'c'=2] {'c'}, dimensions={0} | all-to-all | bytes 1048576 | tf_op jit(solution)/shard_map/all_to_all | solution.py:270
  41.2 0.8 reduce_sum.51
  42.0 4.8 %all-to-all-start.1 = ((bf16[4,128,256]{2,1,0:T(8,128)(2,1)}), bf16[4,128,256]{2,1,0:T(8,128)(2,1)S(1)}, u32[]{:S(2)}, u32[]{:S(2)}) async-start(bf16[4,128,256]{2,1,0:T(8,128)(2,1)} %reduce_sum.51), calls=%async_computation.1 | async-start | bytes 524288 | tf_op jit(solution)/shard_map/all_to_all | solution.py:272
  46.8 0.0 reduce-scatter.2.cloned.1.call-start
  46.8 1.1 shard_map.114
  47.9 0.0 reduce-scatter.2.cloned.1.call-update
  47.9 7.5 %all-to-all-done.1 = bf16[4,128,256]{2,1,0:T(8,128)(2,1)S(1)} async-done(((bf16[4,128,256]{2,1,0:T(8,128)(2,1)}), bf16[4,128,256]{2,1,0:T(8,128)(2,1)S(1)}, u32[]{:S(2)}, u32[]{:S(2)}) %all-to-all-start.1) | async-done | bytes 262176 | tf_op jit(solution)/shard_map/all_to_all | solution.py:272
  55.5 0.7 collective-permute-start.1
  56.2 0.7 collective-permute-start.2
  56.9 0.7 collective-permute-start.3
  57.6 0.7 collective-permute-start.4
  58.3 4.6 %collective-permute-start = (bf16[128,256]{1,0:T(8,128)(2,1)S(1)}, bf16[128,256]{1,0:T(8,128)(2,1)S(1)}, u32[]{:S(2)}, u32[]{:S(2)}) collective-permute-start(bf16[128,256]{1,0:T(8,128)(2,1)S(1)} %add_convert_fusion.1), channel_id=1, source_target_pairs={{0,8},{8,16},{16,24},{24,32},{32,40},{40,48},{48,56},{56,64},{64,7... | collective-permute-start | bytes 196616 | tf_op jit(solution)/shard_map/ppermute | solution.py:299
  62.8 0.0 collective-permute-done.1
  62.9 0.0 collective-permute-done.2
  62.9 0.0 collective-permute-done.3
  62.9 0.0 collective-permute-done.4
  62.9 0.7 collective-permute-start.5
  63.6 0.7 collective-permute-start.6
  64.3 0.7 collective-permute-start.7
  64.9 1.6 collective-permute-done
  66.6 21.1 %all-gather.1 = bf16[1024,256]{1,0:T(8,128)(2,1)} all-gather(bf16[128,256]{1,0:T(8,128)(2,1)S(1)} %bitcast_select_fusion), channel_id=3, replica_groups=mesh['y'=8,'x'=4,'zl'=2,'zh'=4,'c'=2] {'zh','c'}, dimensions={0}, use_global_device_ids=true | all-gather | bytes 589824 | tf_op jit(solution)/shard_map/all_gather | solution.py:267
  87.7 4.2 %shard_map.113 = bf16[8,128,256]{2,1,0:T(8,128)(2,1)} custom-call(s32[1]{0:T(128)} %bitcast.section, bf16[8,128,256]{2,1,0:T(8,128)(2,1)} %bitcast.27, bf16[8,2,256,128]{3,2,1,0:T(8,128)(2,1)} %bitcast.30, f32[1,2048]{1,0:T(1,128)} %gain.3, f32[1,2048]{1,0:T(1,128)} %bitcast.37, bf16[1,2048,256]{2,1,0:T(8,128)(2,1)} %wq.3, ...), custom_call_target="tpu_custom_call" | custom-call | flops 536870912 | bytes 5000000 | tf_op jit(solution)/shard_map/pallas_call | solution.py:219
  91.9 5.0 %all_to_all.26 = bf16[2,4,128,256]{3,2,1,0:T(8,128)(2,1)S(1)} all-to-all(bf16[2,4,128,256]{3,2,1,0:T(8,128)(2,1)} %bitcast.29), channel_id=1, replica_groups=mesh['y'=8,'x'=4,'zl'=2,'zh'=4,'c'=2] {'c'}, dimensions={0} | all-to-all | bytes 1048576 | tf_op jit(solution)/shard_map/all_to_all | solution.py:270
  96.9 0.8 reduce_sum.53
  97.7 3.4 %all-to-all-start.3 = ((bf16[4,128,256]{2,1,0:T(8,128)(2,1)}), bf16[4,128,256]{2,1,0:T(8,128)(2,1)S(1)}, u32[]{:S(2)}, u32[]{:S(2)}) async-start(bf16[4,128,256]{2,1,0:T(8,128)(2,1)} %reduce_sum.53), calls=%async_computation.3 | async-start | bytes 524288 | tf_op jit(solution)/shard_map/all_to_all | solution.py:272
  101.1 0.0 all-gather.10.cloned.1.call-start
  101.2 0.0 collective-permute-done.5
  101.2 0.0 collective-permute-done.6
  101.2 0.0 collective-permute-done.7
  101.2 0.7 collective-permute-start.8
  101.9 0.0 collective-permute-done.8
  101.9 8.9 %all-to-all-done.3 = bf16[4,128,256]{2,1,0:T(8,128)(2,1)S(1)} async-done(((bf16[4,128,256]{2,1,0:T(8,128)(2,1)}), bf16[4,128,256]{2,1,0:T(8,128)(2,1)S(1)}, u32[]{:S(2)}, u32[]{:S(2)}) %all-to-all-start.3) | async-done | bytes 262176 | tf_op jit(solution)/shard_map/all_to_all | solution.py:272
  110.8 0.7 pad_maximum_fusion
  111.5 0.0 all-gather.10.cloned.1.call-update
  111.6 0.0 reduce-scatter.2.cloned.1.call-done
  111.6 0.7 collective-permute-start.10
  112.3 0.7 collective-permute-start.11
  113.0 0.7 collective-permute-start.12
  113.7 0.7 collective-permute-start.13
  114.3 15.8 %all-to-all-start.4 = ((f32[64,4,128]{2,1,0:T(4,128)}), f32[64,4,128]{2,1,0:T(4,128)S(1)}, u32[]{:S(2)}, u32[]{:S(2)}) async-start(f32[64,4,128]{2,1,0:T(4,128)} %bitcast.36), calls=%async_computation.5 | async-start | bytes 262144 | tf_op jit(solution)/shard_map/all_to_all | solution.py:316
  130.2 0.0 collective-permute-done.10
  130.2 0.0 collective-permute-done.11
  130.2 0.0 collective-permute-done.12
  130.2 0.0 collective-permute-done.13
  130.2 13.3 %all-to-all-done.4 = f32[64,4,128]{2,1,0:T(4,128)S(1)} async-done(((f32[64,4,128]{2,1,0:T(4,128)}), f32[64,4,128]{2,1,0:T(4,128)S(1)}, u32[]{:S(2)}, u32[]{:S(2)}) %all-to-all-start.4) | async-done | bytes 131104 | tf_op jit(solution)/shard_map/all_to_all | solution.py:316
  143.6 0.7 collective-permute-start.14
  144.2 0.7 collective-permute-start.15
  144.9 0.7 collective-permute-start.16
  145.6 1.9 %collective-permute-start.9 = (bf16[128,256]{1,0:T(8,128)(2,1)S(1)}, bf16[128,256]{1,0:T(8,128)(2,1)S(1)}, u32[]{:S(2)}, u32[]{:S(2)}) collective-permute-start(bf16[128,256]{1,0:T(8,128)(2,1)S(1)} %add_convert_fusion), channel_id=1, source_target_pairs={{0,8},{8,16},{16,24},{24,32},{32,40},{40,48},{48,56},{56,64},{64,7... | collective-permute-start | bytes 196616 | tf_op jit(solution)/shard_map/ppermute | solution.py:319
  147.5 0.0 collective-permute-done.14
  147.5 0.0 collective-permute-done.15
  147.5 0.0 collective-permute-done.16
  147.6 0.7 collective-permute-start.17
  148.2 6.1 %collective-permute-done.9 = bf16[128,256]{1,0:T(8,128)(2,1)S(1)} collective-permute-done((bf16[128,256]{1,0:T(8,128)(2,1)S(1)}, bf16[128,256]{1,0:T(8,128)(2,1)S(1)}, u32[]{:S(2)}, u32[]{:S(2)}) %collective-permute-start.9) | collective-permute-done | bytes 65568 | tf_op jit(solution)/shard_map/ppermute | solution.py:319
  154.4 0.7 copy.17
  155.1 0.7 reduce_sum.55
  155.8 0.0 collective-permute-done.17
  155.8 16.4 %all-gather.4 = bf16[1024,256]{1,0:T(8,128)(2,1)} all-gather(bf16[128,256]{1,0:T(8,128)(2,1)S(1)} %broadcast_select_fusion), channel_id=6, replica_groups=mesh['y'=8,'x'=4,'zl'=2,'zh'=4,'c'=2] {'zh','c'}, dimensions={0}, use_global_device_ids=true | all-gather | bytes 589824 | tf_op jit(solution)/shard_map/all_gather | solution.py:267
  172.2 0.8 shard_map.115
  (16 shorter events, 0.2 us)
Async XLA Ops:
  8.0 79.7 %all-gather.8.cloned.1.call-start = ((), (), s32[]{:S(2)}) async-start(), calls=%async_computation.7 | async-start | bytes 1179648 | tf_op jit(solution)/shard_map/all_gather | solution.py:267
  42.0 13.5 %all-to-all-start.1 = ((bf16[4,128,256]{2,1,0:T(8,128)(2,1)}), bf16[4,128,256]{2,1,0:T(8,128)(2,1)S(1)}, u32[]{:S(2)}, u32[]{:S(2)}) async-start(bf16[4,128,256]{2,1,0:T(8,128)(2,1)} %reduce_sum.51), calls=%async_computation.1 | async-start | bytes 524288 | tf_op jit(solution)/shard_map/all_to_all | solution.py:272
  46.8 19.8 %copy-start = (bf16[2,128,256]{2,1,0:T(8,128)(2,1)S(1)}, bf16[2,128,256]{2,1,0:T(8,128)(2,1)}, u32[]{:S(2)}) copy-start(bf16[2,128,256]{2,1,0:T(8,128)(2,1)} %get-tuple-element.11) | copy-start | bytes 393220
  46.8 64.8 %reduce-scatter.2.cloned.1.call-start = ((), (), s32[]{:S(2)}) async-start(), calls=%async_computation.6 | async-start | bytes 1179648 | tf_op jit(solution)/shard_map/reduce_scatter | solution.py:294
  55.5 7.3 %collective-permute-start.1 = (bf16[128,256]{1,0:T(8,128)(2,1)S(1)}, bf16[128,256]{1,0:T(8,128)(2,1)S(1)}, u32[]{:S(2)}, u32[]{:S(2)}) collective-permute-start(bf16[128,256]{1,0:T(8,128)(2,1)S(1)} %add_convert_fusion.1), channel_id=1, source_target_pairs={{248,504},{249,505},{250,506},{251,507},{252,508},{253,509},{254,5... | collective-permute-start | bytes 196616 | tf_op jit(solution)/shard_map/ppermute | solution.py:237
  56.2 6.6 %collective-permute-start.2 = (bf16[128,256]{1,0:T(8,128)(2,1)S(1)}, bf16[128,256]{1,0:T(8,128)(2,1)S(1)}, u32[]{:S(2)}, u32[]{:S(2)}) collective-permute-start(bf16[128,256]{1,0:T(8,128)(2,1)S(1)} %add_convert_fusion.1), channel_id=1, source_target_pairs={{248,440},{249,441},{250,442},{251,443},{252,444},{253,445},{254,4... | collective-permute-start | bytes 196616 | tf_op jit(solution)/shard_map/ppermute | solution.py:237
  56.9 6.0 %collective-permute-start.3 = (bf16[128,256]{1,0:T(8,128)(2,1)S(1)}, bf16[128,256]{1,0:T(8,128)(2,1)S(1)}, u32[]{:S(2)}, u32[]{:S(2)}) collective-permute-start(bf16[128,256]{1,0:T(8,128)(2,1)S(1)} %add_convert_fusion.1), channel_id=1, source_target_pairs={{248,376},{249,377},{250,378},{251,379},{252,380},{253,381},{254,3... | collective-permute-start | bytes 196616 | tf_op jit(solution)/shard_map/ppermute | solution.py:237
  57.6 5.3 %collective-permute-start.4 = (bf16[128,256]{1,0:T(8,128)(2,1)S(1)}, bf16[128,256]{1,0:T(8,128)(2,1)S(1)}, u32[]{:S(2)}, u32[]{:S(2)}) collective-permute-start(bf16[128,256]{1,0:T(8,128)(2,1)S(1)} %add_convert_fusion.1), channel_id=1, source_target_pairs={{248,312},{249,313},{250,314},{251,315},{252,316},{253,317},{254,3... | collective-permute-start | bytes 196616 | tf_op jit(solution)/shard_map/ppermute | solution.py:237
  58.3 8.3 %collective-permute-start = (bf16[128,256]{1,0:T(8,128)(2,1)S(1)}, bf16[128,256]{1,0:T(8,128)(2,1)S(1)}, u32[]{:S(2)}, u32[]{:S(2)}) collective-permute-start(bf16[128,256]{1,0:T(8,128)(2,1)S(1)} %add_convert_fusion.1), channel_id=1, source_target_pairs={{0,8},{8,16},{16,24},{24,32},{32,40},{40,48},{48,56},{56,64},{64,7... | collective-permute-start | bytes 196616 | tf_op jit(solution)/shard_map/ppermute | solution.py:299
  62.9 38.3 %collective-permute-start.5 = (bf16[128,256]{1,0:T(8,128)(2,1)S(1)}, bf16[128,256]{1,0:T(8,128)(2,1)S(1)}, u32[]{:S(2)}, u32[]{:S(2)}) collective-permute-start(bf16[128,256]{1,0:T(8,128)(2,1)S(1)} %select_select_fusion.3), channel_id=1, source_target_pairs={{312,296},{376,360},{440,424},{504,488},{313,297},{377,361},{441,4... | collective-permute-start | bytes 196616 | tf_op jit(solution)/shard_map/ppermute | solution.py:245
  63.6 37.6 %collective-permute-start.6 = (bf16[128,256]{1,0:T(8,128)(2,1)S(1)}, bf16[128,256]{1,0:T(8,128)(2,1)S(1)}, u32[]{:S(2)}, u32[]{:S(2)}) collective-permute-start(bf16[128,256]{1,0:T(8,128)(2,1)S(1)} %select_select_fusion.3), channel_id=1, source_target_pairs={{312,280},{376,344},{440,408},{504,472},{313,281},{377,345},{441,4... | collective-permute-start | bytes 196616 | tf_op jit(solution)/shard_map/ppermute | solution.py:245
  64.3 36.9 %collective-permute-start.7 = (bf16[128,256]{1,0:T(8,128)(2,1)S(1)}, bf16[128,256]{1,0:T(8,128)(2,1)S(1)}, u32[]{:S(2)}, u32[]{:S(2)}) collective-permute-start(bf16[128,256]{1,0:T(8,128)(2,1)S(1)} %select_select_fusion.3), channel_id=1, source_target_pairs={{312,264},{376,328},{440,392},{504,456},{313,265},{377,329},{441,3... | collective-permute-start | bytes 196616 | tf_op jit(solution)/shard_map/ppermute | solution.py:245
  97.7 13.1 %all-to-all-start.3 = ((bf16[4,128,256]{2,1,0:T(8,128)(2,1)}), bf16[4,128,256]{2,1,0:T(8,128)(2,1)S(1)}, u32[]{:S(2)}, u32[]{:S(2)}) async-start(bf16[4,128,256]{2,1,0:T(8,128)(2,1)} %reduce_sum.53), calls=%async_computation.3 | async-start | bytes 524288 | tf_op jit(solution)/shard_map/all_to_all | solution.py:272
  101.1 71.1 %all-gather.10.cloned.1.call-start = ((), (), s32[]{:S(2)}) async-start(), calls=%async_computation.8 | async-start | bytes 1179648 | tf_op jit(solution)/shard_map/all_gather | solution.py:267
  101.2 0.7 collective-permute-start.8
  111.6 18.5 %collective-permute-start.10 = (bf16[128,256]{1,0:T(8,128)(2,1)S(1)}, bf16[128,256]{1,0:T(8,128)(2,1)S(1)}, u32[]{:S(2)}, u32[]{:S(2)}) collective-permute-start(bf16[128,256]{1,0:T(8,128)(2,1)S(1)} %add_convert_fusion), channel_id=1, source_target_pairs={{248,504},{249,505},{250,506},{251,507},{252,508},{253,509},{254,5... | collective-permute-start | bytes 196616 | tf_op jit(solution)/shard_map/ppermute | solution.py:237
  112.3 17.9 %collective-permute-start.11 = (bf16[128,256]{1,0:T(8,128)(2,1)S(1)}, bf16[128,256]{1,0:T(8,128)(2,1)S(1)}, u32[]{:S(2)}, u32[]{:S(2)}) collective-permute-start(bf16[128,256]{1,0:T(8,128)(2,1)S(1)} %add_convert_fusion), channel_id=1, source_target_pairs={{248,440},{249,441},{250,442},{251,443},{252,444},{253,445},{254,4... | collective-permute-start | bytes 196616 | tf_op jit(solution)/shard_map/ppermute | solution.py:237
  113.0 17.2 %collective-permute-start.12 = (bf16[128,256]{1,0:T(8,128)(2,1)S(1)}, bf16[128,256]{1,0:T(8,128)(2,1)S(1)}, u32[]{:S(2)}, u32[]{:S(2)}) collective-permute-start(bf16[128,256]{1,0:T(8,128)(2,1)S(1)} %add_convert_fusion), channel_id=1, source_target_pairs={{248,376},{249,377},{250,378},{251,379},{252,380},{253,381},{254,3... | collective-permute-start | bytes 196616 | tf_op jit(solution)/shard_map/ppermute | solution.py:237
  113.7 16.5 %collective-permute-start.13 = (bf16[128,256]{1,0:T(8,128)(2,1)S(1)}, bf16[128,256]{1,0:T(8,128)(2,1)S(1)}, u32[]{:S(2)}, u32[]{:S(2)}) collective-permute-start(bf16[128,256]{1,0:T(8,128)(2,1)S(1)} %add_convert_fusion), channel_id=1, source_target_pairs={{248,312},{249,313},{250,314},{251,315},{252,316},{253,317},{254,3... | collective-permute-start | bytes 196616 | tf_op jit(solution)/shard_map/ppermute | solution.py:237
  114.3 29.2 %all-to-all-start.4 = ((f32[64,4,128]{2,1,0:T(4,128)}), f32[64,4,128]{2,1,0:T(4,128)S(1)}, u32[]{:S(2)}, u32[]{:S(2)}) async-start(f32[64,4,128]{2,1,0:T(4,128)} %bitcast.36), calls=%async_computation.5 | async-start | bytes 262144 | tf_op jit(solution)/shard_map/all_to_all | solution.py:316
  143.6 4.0 %collective-permute-start.14 = (bf16[128,256]{1,0:T(8,128)(2,1)S(1)}, bf16[128,256]{1,0:T(8,128)(2,1)S(1)}, u32[]{:S(2)}, u32[]{:S(2)}) collective-permute-start(bf16[128,256]{1,0:T(8,128)(2,1)S(1)} %select_select_fusion.1), channel_id=1, source_target_pairs={{312,296},{376,360},{440,424},{504,488},{313,297},{377,361},{441,4... | collective-permute-start | bytes 196616 | tf_op jit(solution)/shard_map/ppermute | solution.py:245
  144.2 3.3 %collective-permute-start.15 = (bf16[128,256]{1,0:T(8,128)(2,1)S(1)}, bf16[128,256]{1,0:T(8,128)(2,1)S(1)}, u32[]{:S(2)}, u32[]{:S(2)}) collective-permute-start(bf16[128,256]{1,0:T(8,128)(2,1)S(1)} %select_select_fusion.1), channel_id=1, source_target_pairs={{312,280},{376,344},{440,408},{504,472},{313,281},{377,345},{441,4... | collective-permute-start | bytes 196616 | tf_op jit(solution)/shard_map/ppermute | solution.py:245
  144.9 2.6 %collective-permute-start.16 = (bf16[128,256]{1,0:T(8,128)(2,1)S(1)}, bf16[128,256]{1,0:T(8,128)(2,1)S(1)}, u32[]{:S(2)}, u32[]{:S(2)}) collective-permute-start(bf16[128,256]{1,0:T(8,128)(2,1)S(1)} %select_select_fusion.1), channel_id=1, source_target_pairs={{312,264},{376,328},{440,392},{504,456},{313,265},{377,329},{441,3... | collective-permute-start | bytes 196616 | tf_op jit(solution)/shard_map/ppermute | solution.py:245
  145.6 8.8 %collective-permute-start.9 = (bf16[128,256]{1,0:T(8,128)(2,1)S(1)}, bf16[128,256]{1,0:T(8,128)(2,1)S(1)}, u32[]{:S(2)}, u32[]{:S(2)}) collective-permute-start(bf16[128,256]{1,0:T(8,128)(2,1)S(1)} %add_convert_fusion), channel_id=1, source_target_pairs={{0,8},{8,16},{16,24},{24,32},{32,40},{40,48},{48,56},{56,64},{64,7... | collective-permute-start | bytes 196616 | tf_op jit(solution)/shard_map/ppermute | solution.py:319
  147.6 8.2 %collective-permute-start.17 = (bf16[128,256]{1,0:T(8,128)(2,1)S(1)}, bf16[128,256]{1,0:T(8,128)(2,1)S(1)}, u32[]{:S(2)}, u32[]{:S(2)}) collective-permute-start(bf16[128,256]{1,0:T(8,128)(2,1)S(1)} %select_select_fusion), channel_id=1, source_target_pairs={{264,256},{280,272},{296,288},{312,304},{328,320},{344,336},{360,3... | collective-permute-start | bytes 196616 | tf_op jit(solution)/shard_map/ppermute | solution.py:249
Sparse Core Ops, SparseCore 0:
  11.0 37.9 all-gather.7
  111.6 37.9 all-gather.9
Sparse Core Ops, SparseCore 1:
  50.1 36.8 reduce-scatter.1

commit v11 on v9

--- a/solution.py
+++ b/solution.py
@@ -236,6 +236,8 @@
     for to in range(sy + 1, Y):
         sent = lax.ppermute(block, PIPE, [(source, place(to, sx, sz))])
         held = jnp.where(y == to, sent, held)
+    if beside is not None:
+        held, beside = lax.optimization_barrier((held, beside))
     column = held
     for to in range(X):
         if to != sx:
@@ -292,8 +294,7 @@
         3, flops, F32,
     )
     share = lax.psum_scatter(share, "y", scatter_dimension=0, tiled=True)
-    plane = X * ZL * heads
-    share = share.reshape(plane, depth // (pipe_count * heads), tokens)
+    share = share.reshape(X * ZL, -1, tokens)
 
     output = summed(exchanged(parts), current)
     passed = lax.ppermute(output, PIPE, shift)
@@ -312,8 +313,11 @@
     current = jnp.where(place_here == half, fresh_rows[1], current)
     parts, first_memory = lax.optimization_barrier((exchanged(parts), first_memory))
     output = summed(parts, current)
+    output, share = lax.optimization_barrier((output, share))
+    share = lax.all_to_all(share, ("x", "zl"), 0, 0, tiled=True)
+    share = jnp.sum(share, axis=0).reshape(heads, -1, tokens)
     second_memory, share = spread(output, half - 1, share)
-    share = lax.all_to_all(share, PIPE[1:] + HEAD, 0, 0, tiled=True)
+    share = lax.all_to_all(share, HEAD, 0, 0, tiled=True)
     first_memory = whole(jnp.stack([first_memory, entering]))
     passed = lax.ppermute(output, PIPE, shift)
     last = jnp.where(place_here == half, jnp.zeros_like(passed), passed)

time: 176 us -> 182 us (1.034)
  the two profiles are of different devices: /device:TPU:47 before, /device:TPU:25 now
where the time goes in v11:
time: 182 us; the launch traced here: 181 us
  blocking collectives  71.8 us (39%)
  starting transfers between devices  48.5 us (27%)
  waiting for transfers between devices  29.3 us (16%)
  between operations  15.9 us (9%)
  Pallas kernels  10.2 us (6%)
  other arithmetic  3.78 us (2%)
    all_gather x3, blocking collectives, whole(): return lax.all_gather(block, HEAD, axis=0)  61.7 us
    all_to_all x2, waiting for transfers between devices, exchanged(): return lax.all_to_all(parts, 'zh', 0, 0, tiled=True)  16.4 us
    all_to_all x1, starting transfers between devices, body(): share = lax.all_to_all(share, HEAD, 0, 0, tiled=True)  11.6 us
    all_to_all x1, starting transfers between devices, body(): share = lax.all_to_all(share, ('x', 'zl'), 0, 0, tiled=True)  11 us
    pallas_call x4, Pallas kernels, call(): pl.pallas_call(kernel, out_shape=[jax.ShapeDtypeStruct(shape, kind) for s...  10.2 us
    all_to_all x2, blocking collectives, exchanged(): lax.all_to_all(parts.reshape((C, ZH) + parts.shape[1:]), 'c', 0, 0, tiled...  10.1 us
    all_to_all x2, starting transfers between devices, exchanged(): return lax.all_to_all(parts, 'zh', 0, 0, tiled=True)  8.2 us
    ppermute x2, starting transfers between devices, body(): passed = lax.ppermute(output, PIPE, shift)  6.95 us
  transfers between devices with their start and end apart: 25, of which 5 were waited for; matrix products, arithmetic and copies ran while one was open for 3% of the time, Pallas kernels for 5%

profile of v11, /device:TPU:25, one launch (start us, length us, event | category | flops | bytes accessed | tf_op | source)
XLA Modules:
  0.0 181.1 jit_solution(9133769415918858989)
XLA Ops:
  8.0 0.0 all-gather.8.cloned.1.call-start
  8.0 0.7 all-gather.8.cloned.1.call-update
  8.7 0.9 copy.16
  9.7 22.2 %all-gather = bf16[1024,256]{1,0:T(8,128)(2,1)} all-gather(bf16[128,256]{1,0:T(8,128)(2,1)S(1)} %bitcast.33), channel_id=2, replica_groups=mesh['y'=8,'x'=4,'zl'=2,'zh'=4,'c'=2] {'zh','c'}, dimensions={0}, use_global_device_ids=true | all-gather | bytes 589824 | tf_op jit(solution)/shard_map/all_gather | solution.py:269
  31.9 4.2 %shard_map.112 = (bf16[8,128,256]{2,1,0:T(8,128)(2,1)}, bf16[2,128,256]{2,1,0:T(8,128)(2,1)}) custom-call(s32[1]{0:T(128)} %bitcast.section, bf16[8,128,256]{2,1,0:T(8,128)(2,1)} %bitcast.29, bf16[2,256,128]{2,1,0:T(8,128)(2,1)} %fresh.1, f32[1,2048]{1,0:T(1,128)} %gain.3, bf16[1,2048,256]{2,1,0:T(8,128)(2,1)} %wq.3, bf16[1,2,2048,256]{3,2,1,0:T(8,128)(2,1)} %wkv_hbm.3, ...), custom_call_target="tpu_custom_call" | custom-call | flops 536870912 | bytes 5000000 | tf_op jit(solution)/shard_map/pallas_call | solution.py:219
  36.1 5.1 %all_to_all.30 = bf16[2,4,128,256]{3,2,1,0:T(8,128)(2,1)S(1)} all-to-all(bf16[2,4,128,256]{3,2,1,0:T(8,128)(2,1)} %bitcast.35), channel_id=1, replica_groups=mesh['y'=8,'x'=4,'zl'=2,'zh'=4,'c'=2] {'c'}, dimensions={0} | all-to-all | bytes 1048576 | tf_op jit(solution)/shard_map/all_to_all | solution.py:272
  41.2 0.8 reduce_sum.60
  42.0 4.8 %all-to-all-start.1 = ((bf16[4,128,256]{2,1,0:T(8,128)(2,1)}), bf16[4,128,256]{2,1,0:T(8,128)(2,1)S(1)}, u32[]{:S(2)}, u32[]{:S(2)}) async-start(bf16[4,128,256]{2,1,0:T(8,128)(2,1)} %reduce_sum.60), calls=%async_computation.1 | async-start | bytes 524288 | tf_op jit(solution)/shard_map/all_to_all | solution.py:274
  46.8 1.1 shard_map.114
  47.9 0.0 reduce-scatter.2.cloned.1.call-update
  47.9 7.6 %all-to-all-done.1 = bf16[4,128,256]{2,1,0:T(8,128)(2,1)S(1)} async-done(((bf16[4,128,256]{2,1,0:T(8,128)(2,1)}), bf16[4,128,256]{2,1,0:T(8,128)(2,1)S(1)}, u32[]{:S(2)}, u32[]{:S(2)}) %all-to-all-start.1) | async-done | bytes 262176 | tf_op jit(solution)/shard_map/all_to_all | solution.py:274
  55.5 0.7 collective-permute-start.1
  56.2 0.7 collective-permute-start.2
  56.9 0.7 collective-permute-start.3
  57.6 0.7 collective-permute-start.4
  58.3 4.6 %collective-permute-start = (bf16[128,256]{1,0:T(8,128)(2,1)S(1)}, bf16[128,256]{1,0:T(8,128)(2,1)S(1)}, u32[]{:S(2)}, u32[]{:S(2)}) collective-permute-start(bf16[128,256]{1,0:T(8,128)(2,1)S(1)} %add_convert_fusion.1), channel_id=1, source_target_pairs={{0,8},{8,16},{16,24},{24,32},{32,40},{40,48},{48,56},{56,64},{64,7... | collective-permute-start | bytes 196616 | tf_op jit(solution)/shard_map/ppermute | solution.py:300
  62.8 0.0 collective-permute-done.1
  62.9 0.0 collective-permute-done.2
  62.9 0.0 collective-permute-done.3
  62.9 0.0 collective-permute-done.4
  62.9 0.7 collective-permute-start.5
  63.6 0.7 collective-permute-start.6
  64.3 0.7 collective-permute-start.7
  64.9 1.6 collective-permute-done
  66.6 21.1 %all-gather.1 = bf16[1024,256]{1,0:T(8,128)(2,1)} all-gather(bf16[128,256]{1,0:T(8,128)(2,1)S(1)} %bitcast_select_fusion), channel_id=3, replica_groups=mesh['y'=8,'x'=4,'zl'=2,'zh'=4,'c'=2] {'zh','c'}, dimensions={0}, use_global_device_ids=true | all-gather | bytes 589824 | tf_op jit(solution)/shard_map/all_gather | solution.py:269
  87.7 4.2 %shard_map.113 = bf16[8,128,256]{2,1,0:T(8,128)(2,1)} custom-call(s32[1]{0:T(128)} %bitcast.section, bf16[8,128,256]{2,1,0:T(8,128)(2,1)} %bitcast.28, bf16[8,2,256,128]{3,2,1,0:T(8,128)(2,1)} %bitcast.31, f32[1,2048]{1,0:T(1,128)} %gain.3, f32[1,2048]{1,0:T(1,128)} %bitcast.38, bf16[1,2048,256]{2,1,0:T(8,128)(2,1)} %wq.3, ...), custom_call_target="tpu_custom_call" | custom-call | flops 536870912 | bytes 5000000 | tf_op jit(solution)/shard_map/pallas_call | solution.py:219
  91.9 5.0 %all_to_all.31 = bf16[2,4,128,256]{3,2,1,0:T(8,128)(2,1)S(1)} all-to-all(bf16[2,4,128,256]{3,2,1,0:T(8,128)(2,1)} %bitcast.30), channel_id=1, replica_groups=mesh['y'=8,'x'=4,'zl'=2,'zh'=4,'c'=2] {'c'}, dimensions={0} | all-to-all | bytes 1048576 | tf_op jit(solution)/shard_map/all_to_all | solution.py:272
  96.9 0.8 reduce_sum.62
  97.7 3.4 %all-to-all-start.3 = ((bf16[4,128,256]{2,1,0:T(8,128)(2,1)}), bf16[4,128,256]{2,1,0:T(8,128)(2,1)S(1)}, u32[]{:S(2)}, u32[]{:S(2)}) async-start(bf16[4,128,256]{2,1,0:T(8,128)(2,1)} %reduce_sum.62), calls=%async_computation.3 | async-start | bytes 524288 | tf_op jit(solution)/shard_map/all_to_all | solution.py:274
  101.1 0.0 all-gather.10.cloned.1.call-start
  101.2 0.0 collective-permute-done.5
  101.2 0.0 collective-permute-done.6
  101.2 0.0 collective-permute-done.7
  101.2 0.7 collective-permute-start.8
  101.9 0.0 collective-permute-done.8
  101.9 8.9 %all-to-all-done.3 = bf16[4,128,256]{2,1,0:T(8,128)(2,1)S(1)} async-done(((bf16[4,128,256]{2,1,0:T(8,128)(2,1)}), bf16[4,128,256]{2,1,0:T(8,128)(2,1)S(1)}, u32[]{:S(2)}, u32[]{:S(2)}) %all-to-all-start.3) | async-done | bytes 262176 | tf_op jit(solution)/shard_map/all_to_all | solution.py:274
  110.8 0.7 pad_maximum_fusion
  111.5 0.0 all-gather.10.cloned.1.call-update
  111.6 0.0 reduce-scatter.2.cloned.1.call-done
  111.6 0.7 collective-permute-start.10
  112.3 0.7 collective-permute-start.11
  113.0 0.7 collective-permute-start.12
  113.6 0.7 collective-permute-start.13
  114.3 11.0 %all-to-all-start.4 = ((f32[8,32,128]{2,1,0:T(8,128)}), f32[8,32,128]{2,1,0:T(8,128)S(1)}, u32[]{:S(2)}, u32[]{:S(2)}) async-start(f32[8,32,128]{2,1,0:T(8,128)} %bitcast.37), calls=%async_computation.5 | async-start | bytes 262144 | tf_op jit(solution)/shard_map/all_to_all | solution.py:317
  125.3 0.0 collective-permute-done.10
  125.3 0.0 collective-permute-done.11
  125.3 0.0 collective-permute-done.12
  125.4 0.0 collective-permute-done.13
  125.4 5.5 %all-to-all-done.4 = f32[8,32,128]{2,1,0:T(8,128)S(1)} async-done(((f32[8,32,128]{2,1,0:T(8,128)}), f32[8,32,128]{2,1,0:T(8,128)S(1)}, u32[]{:S(2)}, u32[]{:S(2)}) %all-to-all-start.4) | async-done | bytes 131104 | tf_op jit(solution)/shard_map/all_to_all | solution.py:317
  130.9 0.6 reduce_sum.64
  131.5 0.7 collective-permute-start.14
  132.1 0.7 collective-permute-start.15
  132.8 0.7 collective-permute-start.16
  133.5 2.4 %collective-permute-start.9 = (bf16[128,256]{1,0:T(8,128)(2,1)S(1)}, bf16[128,256]{1,0:T(8,128)(2,1)S(1)}, u32[]{:S(2)}, u32[]{:S(2)}) collective-permute-start(bf16[128,256]{1,0:T(8,128)(2,1)S(1)} %add_convert_fusion), channel_id=1, source_target_pairs={{0,8},{8,16},{16,24},{24,32},{32,40},{40,48},{48,56},{56,64},{64,7... | collective-permute-start | bytes 196616 | tf_op jit(solution)/shard_map/ppermute | solution.py:322
  135.9 0.0 collective-permute-done.14
  135.9 0.0 collective-permute-done.15
  135.9 0.7 collective-permute-start.17
  136.6 4.9 %collective-permute-done.9 = bf16[128,256]{1,0:T(8,128)(2,1)S(1)} collective-permute-done((bf16[128,256]{1,0:T(8,128)(2,1)S(1)}, bf16[128,256]{1,0:T(8,128)(2,1)S(1)}, u32[]{:S(2)}, u32[]{:S(2)}) %collective-permute-start.9) | collective-permute-done | bytes 65568 | tf_op jit(solution)/shard_map/ppermute | solution.py:322
  141.6 0.7 copy.17
  142.3 11.6 %all-to-all-start.5 = ((f32[8,4,128]{2,1,0:T(4,128)}), f32[8,4,128]{2,1,0:T(4,128)S(1)}, u32[]{:S(2)}, u32[]{:S(2)}) async-start(f32[8,4,128]{2,1,0:T(4,128)} %bitcast.18), calls=%async_computation.6 | async-start | bytes 32768 | tf_op jit(solution)/shard_map/all_to_all | solution.py:320
  153.9 0.0 collective-permute-done.17
  153.9 18.4 %all-gather.4 = bf16[1024,256]{1,0:T(8,128)(2,1)} all-gather(bf16[128,256]{1,0:T(8,128)(2,1)S(1)} %broadcast_select_fusion), channel_id=6, replica_groups=mesh['y'=8,'x'=4,'zl'=2,'zh'=4,'c'=2] {'zh','c'}, dimensions={0}, use_global_device_ids=true | all-gather | bytes 589824 | tf_op jit(solution)/shard_map/all_gather | solution.py:269
  172.3 0.6 reduce_sum.65
  172.9 0.8 shard_map.115
  (19 shorter events, 0.3 us)
Async XLA Ops:
  8.0 79.7 %all-gather.8.cloned.1.call-start = ((), (), s32[]{:S(2)}) async-start(), calls=%async_computation.8 | async-start | bytes 1179648 | tf_op jit(solution)/shard_map/all_gather | solution.py:269
  42.0 13.5 %all-to-all-start.1 = ((bf16[4,128,256]{2,1,0:T(8,128)(2,1)}), bf16[4,128,256]{2,1,0:T(8,128)(2,1)S(1)}, u32[]{:S(2)}, u32[]{:S(2)}) async-start(bf16[4,128,256]{2,1,0:T(8,128)(2,1)} %reduce_sum.60), calls=%async_computation.1 | async-start | bytes 524288 | tf_op jit(solution)/shard_map/all_to_all | solution.py:274
  46.8 19.8 %copy-start = (bf16[2,128,256]{2,1,0:T(8,128)(2,1)S(1)}, bf16[2,128,256]{2,1,0:T(8,128)(2,1)}, u32[]{:S(2)}) copy-start(bf16[2,128,256]{2,1,0:T(8,128)(2,1)} %get-tuple-element.15) | copy-start | bytes 393220
  46.8 64.8 %reduce-scatter.2.cloned.1.call-start = ((), (), s32[]{:S(2)}) async-start(), calls=%async_computation.7 | async-start | bytes 1179648 | tf_op jit(solution)/shard_map/reduce_scatter | solution.py:296
  55.5 7.3 %collective-permute-start.1 = (bf16[128,256]{1,0:T(8,128)(2,1)S(1)}, bf16[128,256]{1,0:T(8,128)(2,1)S(1)}, u32[]{:S(2)}, u32[]{:S(2)}) collective-permute-start(bf16[128,256]{1,0:T(8,128)(2,1)S(1)} %add_convert_fusion.1), channel_id=1, source_target_pairs={{248,504},{249,505},{250,506},{251,507},{252,508},{253,509},{254,5... | collective-permute-start | bytes 196616 | tf_op jit(solution)/shard_map/ppermute | solution.py:237
  56.2 6.6 %collective-permute-start.2 = (bf16[128,256]{1,0:T(8,128)(2,1)S(1)}, bf16[128,256]{1,0:T(8,128)(2,1)S(1)}, u32[]{:S(2)}, u32[]{:S(2)}) collective-permute-start(bf16[128,256]{1,0:T(8,128)(2,1)S(1)} %add_convert_fusion.1), channel_id=1, source_target_pairs={{248,440},{249,441},{250,442},{251,443},{252,444},{253,445},{254,4... | collective-permute-start | bytes 196616 | tf_op jit(solution)/shard_map/ppermute | solution.py:237
  56.9 6.0 %collective-permute-start.3 = (bf16[128,256]{1,0:T(8,128)(2,1)S(1)}, bf16[128,256]{1,0:T(8,128)(2,1)S(1)}, u32[]{:S(2)}, u32[]{:S(2)}) collective-permute-start(bf16[128,256]{1,0:T(8,128)(2,1)S(1)} %add_convert_fusion.1), channel_id=1, source_target_pairs={{248,376},{249,377},{250,378},{251,379},{252,380},{253,381},{254,3... | collective-permute-start | bytes 196616 | tf_op jit(solution)/shard_map/ppermute | solution.py:237
  57.6 5.3 %collective-permute-start.4 = (bf16[128,256]{1,0:T(8,128)(2,1)S(1)}, bf16[128,256]{1,0:T(8,128)(2,1)S(1)}, u32[]{:S(2)}, u32[]{:S(2)}) collective-permute-start(bf16[128,256]{1,0:T(8,128)(2,1)S(1)} %add_convert_fusion.1), channel_id=1, source_target_pairs={{248,312},{249,313},{250,314},{251,315},{252,316},{253,317},{254,3... | collective-permute-start | bytes 196616 | tf_op jit(solution)/shard_map/ppermute | solution.py:237
  58.3 8.3 %collective-permute-start = (bf16[128,256]{1,0:T(8,128)(2,1)S(1)}, bf16[128,256]{1,0:T(8,128)(2,1)S(1)}, u32[]{:S(2)}, u32[]{:S(2)}) collective-permute-start(bf16[128,256]{1,0:T(8,128)(2,1)S(1)} %add_convert_fusion.1), channel_id=1, source_target_pairs={{0,8},{8,16},{16,24},{24,32},{32,40},{40,48},{48,56},{56,64},{64,7... | collective-permute-start | bytes 196616 | tf_op jit(solution)/shard_map/ppermute | solution.py:300
  62.9 38.3 %collective-permute-start.5 = (bf16[128,256]{1,0:T(8,128)(2,1)S(1)}, bf16[128,256]{1,0:T(8,128)(2,1)S(1)}, u32[]{:S(2)}, u32[]{:S(2)}) collective-permute-start(bf16[128,256]{1,0:T(8,128)(2,1)S(1)} %select_select_fusion.3), channel_id=1, source_target_pairs={{312,296},{376,360},{440,424},{504,488},{313,297},{377,361},{441,4... | collective-permute-start | bytes 196616 | tf_op jit(solution)/shard_map/ppermute | solution.py:245
  63.6 37.6 %collective-permute-start.6 = (bf16[128,256]{1,0:T(8,128)(2,1)S(1)}, bf16[128,256]{1,0:T(8,128)(2,1)S(1)}, u32[]{:S(2)}, u32[]{:S(2)}) collective-permute-start(bf16[128,256]{1,0:T(8,128)(2,1)S(1)} %select_select_fusion.3), channel_id=1, source_target_pairs={{312,280},{376,344},{440,408},{504,472},{313,281},{377,345},{441,4... | collective-permute-start | bytes 196616 | tf_op jit(solution)/shard_map/ppermute | solution.py:245
  64.3 36.9 %collective-permute-start.7 = (bf16[128,256]{1,0:T(8,128)(2,1)S(1)}, bf16[128,256]{1,0:T(8,128)(2,1)S(1)}, u32[]{:S(2)}, u32[]{:S(2)}) collective-permute-start(bf16[128,256]{1,0:T(8,128)(2,1)S(1)} %select_select_fusion.3), channel_id=1, source_target_pairs={{312,264},{376,328},{440,392},{504,456},{313,265},{377,329},{441,3... | collective-permute-start | bytes 196616 | tf_op jit(solution)/shard_map/ppermute | solution.py:245
  97.7 13.1 %all-to-all-start.3 = ((bf16[4,128,256]{2,1,0:T(8,128)(2,1)}), bf16[4,128,256]{2,1,0:T(8,128)(2,1)S(1)}, u32[]{:S(2)}, u32[]{:S(2)}) async-start(bf16[4,128,256]{2,1,0:T(8,128)(2,1)} %reduce_sum.62), calls=%async_computation.3 | async-start | bytes 524288 | tf_op jit(solution)/shard_map/all_to_all | solution.py:274
  101.1 71.8 %all-gather.10.cloned.1.call-start = ((), (), s32[]{:S(2)}) async-start(), calls=%async_computation.9 | async-start | bytes 1179648 | tf_op jit(solution)/shard_map/all_gather | solution.py:269
  101.2 0.7 collective-permute-start.8
  111.6 13.7 %collective-permute-start.10 = (bf16[128,256]{1,0:T(8,128)(2,1)S(1)}, bf16[128,256]{1,0:T(8,128)(2,1)S(1)}, u32[]{:S(2)}, u32[]{:S(2)}) collective-permute-start(bf16[128,256]{1,0:T(8,128)(2,1)S(1)} %add_convert_fusion), channel_id=1, source_target_pairs={{248,504},{249,505},{250,506},{251,507},{252,508},{253,509},{254,5... | collective-permute-start | bytes 196616 | tf_op jit(solution)/shard_map/ppermute | solution.py:237
  112.3 13.0 %collective-permute-start.11 = (bf16[128,256]{1,0:T(8,128)(2,1)S(1)}, bf16[128,256]{1,0:T(8,128)(2,1)S(1)}, u32[]{:S(2)}, u32[]{:S(2)}) collective-permute-start(bf16[128,256]{1,0:T(8,128)(2,1)S(1)} %add_convert_fusion), channel_id=1, source_target_pairs={{248,440},{249,441},{250,442},{251,443},{252,444},{253,445},{254,4... | collective-permute-start | bytes 196616 | tf_op jit(solution)/shard_map/ppermute | solution.py:237
  113.0 12.4 %collective-permute-start.12 = (bf16[128,256]{1,0:T(8,128)(2,1)S(1)}, bf16[128,256]{1,0:T(8,128)(2,1)S(1)}, u32[]{:S(2)}, u32[]{:S(2)}) collective-permute-start(bf16[128,256]{1,0:T(8,128)(2,1)S(1)} %add_convert_fusion), channel_id=1, source_target_pairs={{248,376},{249,377},{250,378},{251,379},{252,380},{253,381},{254,3... | collective-permute-start | bytes 196616 | tf_op jit(solution)/shard_map/ppermute | solution.py:237
  113.6 11.7 %collective-permute-start.13 = (bf16[128,256]{1,0:T(8,128)(2,1)S(1)}, bf16[128,256]{1,0:T(8,128)(2,1)S(1)}, u32[]{:S(2)}, u32[]{:S(2)}) collective-permute-start(bf16[128,256]{1,0:T(8,128)(2,1)S(1)} %add_convert_fusion), channel_id=1, source_target_pairs={{248,312},{249,313},{250,314},{251,315},{252,316},{253,317},{254,3... | collective-permute-start | bytes 196616 | tf_op jit(solution)/shard_map/ppermute | solution.py:237
  114.3 16.6 %all-to-all-start.4 = ((f32[8,32,128]{2,1,0:T(8,128)}), f32[8,32,128]{2,1,0:T(8,128)S(1)}, u32[]{:S(2)}, u32[]{:S(2)}) async-start(f32[8,32,128]{2,1,0:T(8,128)} %bitcast.37), calls=%async_computation.5 | async-start | bytes 262144 | tf_op jit(solution)/shard_map/all_to_all | solution.py:317
  131.5 4.4 %collective-permute-start.14 = (bf16[128,256]{1,0:T(8,128)(2,1)S(1)}, bf16[128,256]{1,0:T(8,128)(2,1)S(1)}, u32[]{:S(2)}, u32[]{:S(2)}) collective-permute-start(bf16[128,256]{1,0:T(8,128)(2,1)S(1)} %select_select_fusion.1), channel_id=1, source_target_pairs={{312,296},{376,360},{440,424},{504,488},{313,297},{377,361},{441,4... | collective-permute-start | bytes 196616 | tf_op jit(solution)/shard_map/ppermute | solution.py:245
  132.1 3.7 %collective-permute-start.15 = (bf16[128,256]{1,0:T(8,128)(2,1)S(1)}, bf16[128,256]{1,0:T(8,128)(2,1)S(1)}, u32[]{:S(2)}, u32[]{:S(2)}) collective-permute-start(bf16[128,256]{1,0:T(8,128)(2,1)S(1)} %select_select_fusion.1), channel_id=1, source_target_pairs={{312,280},{376,344},{440,408},{504,472},{313,281},{377,345},{441,4... | collective-permute-start | bytes 196616 | tf_op jit(solution)/shard_map/ppermute | solution.py:245
  132.8 3.1 %collective-permute-start.16 = (bf16[128,256]{1,0:T(8,128)(2,1)S(1)}, bf16[128,256]{1,0:T(8,128)(2,1)S(1)}, u32[]{:S(2)}, u32[]{:S(2)}) collective-permute-start(bf16[128,256]{1,0:T(8,128)(2,1)S(1)} %select_select_fusion.1), channel_id=1, source_target_pairs={{312,264},{376,328},{440,392},{504,456},{313,265},{377,329},{441,3... | collective-permute-start | bytes 196616 | tf_op jit(solution)/shard_map/ppermute | solution.py:245
  133.5 8.1 %collective-permute-start.9 = (bf16[128,256]{1,0:T(8,128)(2,1)S(1)}, bf16[128,256]{1,0:T(8,128)(2,1)S(1)}, u32[]{:S(2)}, u32[]{:S(2)}) collective-permute-start(bf16[128,256]{1,0:T(8,128)(2,1)S(1)} %add_convert_fusion), channel_id=1, source_target_pairs={{0,8},{8,16},{16,24},{24,32},{32,40},{40,48},{48,56},{56,64},{64,7... | collective-permute-start | bytes 196616 | tf_op jit(solution)/shard_map/ppermute | solution.py:322
  135.9 18.0 %collective-permute-start.17 = (bf16[128,256]{1,0:T(8,128)(2,1)S(1)}, bf16[128,256]{1,0:T(8,128)(2,1)S(1)}, u32[]{:S(2)}, u32[]{:S(2)}) collective-permute-start(bf16[128,256]{1,0:T(8,128)(2,1)S(1)} %select_select_fusion), channel_id=1, source_target_pairs={{264,256},{280,272},{296,288},{312,304},{328,320},{344,336},{360,3... | collective-permute-start | bytes 196616 | tf_op jit(solution)/shard_map/ppermute | solution.py:251
  142.3 30.0 %all-to-all-start.5 = ((f32[8,4,128]{2,1,0:T(4,128)}), f32[8,4,128]{2,1,0:T(4,128)S(1)}, u32[]{:S(2)}, u32[]{:S(2)}) async-start(f32[8,4,128]{2,1,0:T(4,128)} %bitcast.18), calls=%async_computation.6 | async-start | bytes 32768 | tf_op jit(solution)/shard_map/all_to_all | solution.py:320
Sparse Core Ops, SparseCore 0:
  11.0 37.9 all-gather.7
  111.6 36.5 all-gather.9
Sparse Core Ops, SparseCore 1:
  50.1 36.8 reduce-scatter.1

commit v12 on v9

--- a/solution.py
+++ b/solution.py
@@ -131,7 +131,7 @@
         out[h] = jnp.dot(
             attn, wo[:, h * width : (h + 1) * width], preferred_element_type=F32
         ).astype(BF)
-        puts.append(copy(8 + h, out.at[h], out_hbm.at[h % C * ZH + h // C]))
+        puts.append(copy(8 + h, out.at[h], out_hbm.at[h]))
         puts[-1].start()
     if tick == 0:
         get_fresh.wait()
@@ -177,8 +177,9 @@
     put.wait()
 
 
-def memory_kernel(half, section, first_hbm, second_hbm, final_hbm, wkv_hbm, out_hbm, sources, rows,
-                  final_gain, wkv, out, sems):
+def last_kernel(half, section, first_hbm, second_hbm, final_hbm, wkv_hbm, passed_hbm, shares_hbm,
+                out_hbm, stream_hbm, grad_hbm, sources, rows, final_gain, wkv, passed, shares, out,
+                stream, grad, sems):
     width = wkv.shape[2]
     tokens = sources.shape[2]
 
@@ -191,11 +192,28 @@
         copy(2, first_hbm.at[:, 0], sources.at[0]),
         copy(3, wkv_hbm.at[0], wkv),
     ]
+    get_passed = copy(4, passed_hbm, passed)
+    get_shares = copy(5, shares_hbm, shares)
 
     @pl.when(section[0] >= half)
     def _():
         for get in gets:
             get.start()
+
+    get_passed.start()
+    get_shares.start()
+    get_passed.wait()
+    turned = passed[...].T
+    stream[...] = jnp.where(section[0] == half, jnp.zeros_like(turned), turned)
+    put_stream = copy(6, stream, stream_hbm.at[0])
+    put_stream.start()
+    get_shares.wait()
+    grad[...] = jnp.sum(shares[...], axis=0)
+    put_grad = copy(7, grad, grad_hbm)
+    put_grad.start()
+
+    @pl.when(section[0] >= half)
+    def _():
         for get in gets[:3]:
             get.wait()
         for t in range(TICKS):
@@ -210,15 +228,20 @@
     def _():
         out[...] = jnp.zeros_like(out)
 
-    put = copy(4, out, out_hbm.at[0])
+    put = copy(8, out, out_hbm.at[0])
     put.start()
+    put_stream.wait()
+    put_grad.wait()
     put.wait()
 
 
-def call(kernel, section, operands, out_shapes, scratch, copies, flops, kind=BF):
+def call(kernel, section, operands, out_shapes, scratch, copies, flops, kinds=None):
     return pl.pallas_call(
         kernel,
-        out_shape=[jax.ShapeDtypeStruct(shape, kind) for shape in out_shapes],
+        out_shape=[
+            jax.ShapeDtypeStruct(shape, kind)
+            for shape, kind in zip(out_shapes, kinds or [BF] * len(out_shapes))
+        ],
         in_specs=[pl.BlockSpec(memory_space=pltpu.SMEM)]
         + [pl.BlockSpec(memory_space=pl.ANY)] * len(operands),
         out_specs=[pl.BlockSpec(memory_space=pl.ANY)] * len(out_shapes),
@@ -267,9 +290,7 @@
         return lax.all_gather(block, HEAD, axis=0)
 
     def exchanged(parts):
-        parts = lax.all_to_all(parts.reshape((C, ZH) + parts.shape[1:]), "c", 0, 0, tiled=True)
-        parts = jnp.sum(parts.astype(F32), axis=0).astype(BF)
-        return lax.all_to_all(parts, "zh", 0, 0, tiled=True)
+        return lax.all_to_all(parts, HEAD, 0, 0, tiled=True)
 
     def summed(parts, current):
         return (current.astype(F32) + jnp.sum(parts.astype(F32), axis=0)).astype(BF)
@@ -289,7 +310,7 @@
     (share,) = call(
         functools.partial(share_kernel, half), section, (cache_grad, w_kv), ((depth, tokens),),
         ((pair_shape, BF), ((2, depth, width), BF), ((depth, tokens), F32)),
-        3, flops, F32,
+        3, flops, (F32,),
     )
     share = lax.psum_scatter(share, "y", scatter_dimension=0, tiled=True)
     plane = X * ZL * heads
@@ -316,19 +337,18 @@
     share = lax.all_to_all(share, PIPE[1:] + HEAD, 0, 0, tiled=True)
     first_memory = whole(jnp.stack([first_memory, entering]))
     passed = lax.ppermute(output, PIPE, shift)
-    last = jnp.where(place_here == half, jnp.zeros_like(passed), passed)
     share, second_memory = lax.optimization_barrier((share, whole(second_memory)))
-    memory_grad = jnp.sum(share, axis=0)
-
-    (new_kv,) = call(
-        functools.partial(memory_kernel, half), section,
-        (first_memory, second_memory, final_scale, w_kv),
-        ((1, TICKS, tokens, 2 * width),),
+    each = share.shape[1]
+    new_kv, last, memory_grad = call(
+        functools.partial(last_kernel, half), section,
+        (first_memory, second_memory, final_scale, w_kv, passed, share),
+        ((1, TICKS, tokens, 2 * width), (1, width, tokens), (each, tokens)),
         (((TICKS,) + rows8, BF), ((heads, TICKS * tokens, width), BF), ((1, depth), F32),
-         ((2, depth, width), BF), ((TICKS,) + pair_shape, BF)),
-        5, flops,
-    )
-    return (last.T[None], new_kv, memory_grad)
+         ((2, depth, width), BF), ((tokens, width), BF), (share.shape, F32),
+         ((TICKS,) + pair_shape, BF), ((width, tokens), BF), ((each, tokens), F32)),
+        9, flops, (BF, BF, F32),
+    )
+    return (last, new_kv, memory_grad)
 
 
 def solution(mesh):

time: 176 us -> 173 us (0.983)
  the two profiles are of different devices: /device:TPU:47 before, /device:TPU:39 now
where the time goes in v12:
time: 173 us
  blocking collectives  59 us (34%)
  starting transfers between devices  50.4 us (29%)
  waiting for transfers between devices  30.7 us (18%)
  between operations  15.9 us (9%)
  Pallas kernels  14 us (8%)
    all_gather x3, blocking collectives, whole(): return lax.all_gather(block, HEAD, axis=0)  59 us
    ppermute x2, starting transfers between devices, body(): passed = lax.ppermute(output, PIPE, shift)  14.7 us
    all_to_all x1, starting transfers between devices, body(): share = lax.all_to_all(share, PIPE[1:] + HEAD, 0, 0, tiled=True)  14.4 us
    all_to_all x2, waiting for transfers between devices, exchanged(): return lax.all_to_all(parts, HEAD, 0, 0, tiled=True)  14.1 us
    pallas_call x4, Pallas kernels, call(): pl.pallas_call(kernel, out_shape=[jax.ShapeDtypeStruct(shape, kind) for s...  14 us
    ppermute x2, waiting for transfers between devices, spread(): return (jnp.where(zl == sz, held, lax.ppermute(held, PIPE, pairs)), beside)  13.4 us
    all_to_all x2, starting transfers between devices, exchanged(): return lax.all_to_all(parts, HEAD, 0, 0, tiled=True)  9.35 us
    ppermute x8, starting transfers between devices, spread(): sent = lax.ppermute(block, PIPE, [(source, place(to, sx, sz))])  5.31 us
  transfers between devices with their start and end apart: 24, of which 3 were waited for; matrix products, arithmetic and copies ran while one was open for 1% of the time, Pallas kernels for 6%

profile of v12, /device:TPU:39, one launch (start us, length us, event | category | flops | bytes accessed | tf_op | source)
XLA Modules:
  0.0 172.6 jit_solution(11818135415180732590)
XLA Ops:
  8.0 0.0 all-gather.8.cloned.1.call-start
  8.0 0.7 all-gather.8.cloned.1.call-update
  8.7 0.9 copy.13
  9.7 22.2 %all-gather = bf16[1024,256]{1,0:T(8,128)(2,1)} all-gather(bf16[128,256]{1,0:T(8,128)(2,1)S(1)} %bitcast.25), channel_id=2, replica_groups=mesh['y'=8,'x'=4,'zl'=2,'zh'=4,'c'=2] {'zh','c'}, dimensions={0}, use_global_device_ids=true | all-gather | bytes 589824 | tf_op jit(solution)/shard_map/all_gather | solution.py:290
  31.9 3.4 %shard_map.112 = (bf16[8,128,256]{2,1,0:T(8,128)(2,1)}, bf16[2,128,256]{2,1,0:T(8,128)(2,1)}) custom-call(s32[1]{0:T(128)} %bitcast.section, bf16[8,128,256]{2,1,0:T(8,128)(2,1)} %bitcast.22, bf16[2,256,128]{2,1,0:T(8,128)(2,1)} %fresh.1, f32[1,2048]{1,0:T(1,128)} %gain.3, bf16[1,2048,256]{2,1,0:T(8,128)(2,1)} %wq.3, bf16[1,2,2048,256]{3,2,1,0:T(8,128)(2,1)} %wkv_hbm.3, ...), custom_call_target="tpu_custom_call" | custom-call | flops 536870912 | bytes 5000000 | tf_op jit(solution)/shard_map/pallas_call | solution.py:239
  35.3 5.3 %all-to-all-start = ((bf16[8,128,256]{2,1,0:T(8,128)(2,1)}), bf16[8,128,256]{2,1,0:T(8,128)(2,1)S(1)}, u32[]{:S(2)}, u32[]{:S(2)}) async-start(bf16[8,128,256]{2,1,0:T(8,128)(2,1)} %get-tuple-element.15), calls=%async_computation | async-start | bytes 1048576 | tf_op jit(solution)/shard_map/all_to_all | solution.py:293
  40.5 0.0 reduce-scatter.2.cloned.1.call-start
  40.5 3.4 %shard_map.114 = f32[2048,128]{1,0:T(8,128)} custom-call(s32[1]{0:T(128)} %bitcast.section, bf16[1,128,512]{2,1,0:T(8,128)(2,1)} %grads_hbm.1, bf16[1,2,2048,256]{3,2,1,0:T(8,128)(2,1)} %wkv_hbm.3), custom_call_target="tpu_custom_call" | custom-call | flops 536870912 | bytes 5000000 | tf_op jit(solution)/shard_map/pallas_call | solution.py:239
  43.9 0.0 reduce-scatter.2.cloned.1.call-update
  44.0 14.1 %all-to-all-done = bf16[8,128,256]{2,1,0:T(8,128)(2,1)S(1)} async-done(((bf16[8,128,256]{2,1,0:T(8,128)(2,1)}), bf16[8,128,256]{2,1,0:T(8,128)(2,1)S(1)}, u32[]{:S(2)}, u32[]{:S(2)}) %all-to-all-start) | async-done | bytes 524320 | tf_op jit(solution)/shard_map/all_to_all | solution.py:293
  58.1 0.1 convert_reduce_fusion.1
  58.2 3.5 %collective-permute-start = (bf16[128,256]{1,0:T(8,128)(2,1)S(1)}, bf16[128,256]{1,0:T(8,128)(2,1)S(1)}, u32[]{:S(2)}, u32[]{:S(2)}) collective-permute-start(bf16[128,256]{1,0:T(8,128)(2,1)S(1)} %add_convert_fusion.1), channel_id=1, source_target_pairs={{0,8},{8,16},{16,24},{24,32},{32,40},{40,48},{48,56},{56,64},{64,7... | collective-permute-start | bytes 196616 | tf_op jit(solution)/shard_map/ppermute | solution.py:320
  61.7 2.4 %collective-permute-done = bf16[128,256]{1,0:T(8,128)(2,1)S(1)} collective-permute-done((bf16[128,256]{1,0:T(8,128)(2,1)S(1)}, bf16[128,256]{1,0:T(8,128)(2,1)S(1)}, u32[]{:S(2)}, u32[]{:S(2)}) %collective-permute-start) | collective-permute-done | bytes 65568 | tf_op jit(solution)/shard_map/ppermute | solution.py:320
  64.1 0.0 copy-done.1
  64.1 18.0 %all-gather.1 = bf16[1024,256]{1,0:T(8,128)(2,1)} all-gather(bf16[128,256]{1,0:T(8,128)(2,1)S(1)} %bitcast_select_fusion.1), channel_id=3, replica_groups=mesh['y'=8,'x'=4,'zl'=2,'zh'=4,'c'=2] {'zh','c'}, dimensions={0}, use_global_device_ids=true | all-gather | bytes 589824 | tf_op jit(solution)/shard_map/all_gather | solution.py:290
  82.1 3.3 %shard_map.113 = bf16[8,128,256]{2,1,0:T(8,128)(2,1)} custom-call(s32[1]{0:T(128)} %bitcast.section, bf16[8,128,256]{2,1,0:T(8,128)(2,1)} %bitcast.21, bf16[8,2,256,128]{3,2,1,0:T(8,128)(2,1)} %bitcast.24, f32[1,2048]{1,0:T(1,128)} %gain.3, f32[1,2048]{1,0:T(1,128)} %bitcast.29, bf16[1,2048,256]{2,1,0:T(8,128)(2,1)} %wq.3, ...), custom_call_target="tpu_custom_call" | custom-call | flops 536870912 | bytes 5000000 | tf_op jit(solution)/shard_map/pallas_call | solution.py:239
  85.4 4.1 %all-to-all-start.1 = ((bf16[8,128,256]{2,1,0:T(8,128)(2,1)}), bf16[8,128,256]{2,1,0:T(8,128)(2,1)S(1)}, u32[]{:S(2)}, u32[]{:S(2)}) async-start(bf16[8,128,256]{2,1,0:T(8,128)(2,1)} %shard_map.113), calls=%async_computation.1 | async-start | bytes 1048576 | tf_op jit(solution)/shard_map/all_to_all | solution.py:293
  89.5 0.0 all-gather.10.cloned.1.call-start
  89.5 0.7 collective-permute-start.1
  90.2 0.7 collective-permute-start.2
  90.9 0.7 collective-permute-start.3
  91.5 0.7 collective-permute-start.4
  92.2 0.0 collective-permute-done.1
  92.2 0.0 collective-permute-done.2
  92.3 0.0 collective-permute-done.3
  92.3 0.0 collective-permute-done.4
  92.3 0.7 collective-permute-start.5
  93.0 0.7 collective-permute-start.6
  93.6 0.7 collective-permute-start.7
  94.3 0.0 collective-permute-done.5
  94.3 0.0 collective-permute-done.6
  94.4 0.0 collective-permute-done.7
  94.4 1.3 collective-permute-start.8
  95.7 13.4 %collective-permute-done.8 = bf16[128,256]{1,0:T(8,128)(2,1)S(1)} collective-permute-done((bf16[128,256]{1,0:T(8,128)(2,1)S(1)}, bf16[128,256]{1,0:T(8,128)(2,1)S(1)}, u32[]{:S(2)}, u32[]{:S(2)}) %collective-permute-start.8) | collective-permute-done | bytes 65568 | tf_op jit(solution)/shard_map/ppermute | solution.py:272
  109.1 0.0 all-to-all-done.1
  109.1 0.7 pad_maximum_fusion
  109.8 0.0 all-gather.10.cloned.1.call-update
  109.8 0.1 convert_reduce_fusion
  109.9 0.7 collective-permute-start.9
  110.6 0.7 collective-permute-start.10
  111.3 0.7 collective-permute-start.11
  111.9 0.7 collective-permute-start.12
  112.6 0.0 collective-permute-done.9
  112.6 0.0 collective-permute-done.10
  112.6 0.0 collective-permute-done.11
  112.6 0.0 collective-permute-done.12
  112.7 0.7 collective-permute-start.13
  113.4 0.7 collective-permute-start.14
  114.0 0.7 collective-permute-start.15
  114.7 0.0 collective-permute-done.13
  114.7 0.0 collective-permute-done.14
  114.7 0.0 collective-permute-done.15
  114.8 0.0 reduce-scatter.2.cloned.1.call-done
  114.8 1.3 collective-permute-start.16
  116.1 11.2 %collective-permute-start.17 = (bf16[128,256]{1,0:T(8,128)(2,1)S(1)}, bf16[128,256]{1,0:T(8,128)(2,1)S(1)}, u32[]{:S(2)}, u32[]{:S(2)}) collective-permute-start(bf16[128,256]{1,0:T(8,128)(2,1)S(1)} %add_convert_fusion), channel_id=1, source_target_pairs={{0,8},{8,16},{16,24},{24,32},{32,40},{40,48},{48,56},{56,64},{64,7... | collective-permute-start | bytes 196616 | tf_op jit(solution)/shard_map/ppermute | solution.py:339
  127.3 14.4 %all-to-all-start.2 = ((f32[64,4,128]{2,1,0:T(4,128)}), f32[64,4,128]{2,1,0:T(4,128)S(1)}, u32[]{:S(2)}, u32[]{:S(2)}) async-start(f32[64,4,128]{2,1,0:T(4,128)} %bitcast.28), calls=%async_computation.3 | async-start | bytes 262144 | tf_op jit(solution)/shard_map/all_to_all | solution.py:337
  141.7 0.0 collective-permute-done.16
  141.8 18.8 %all-gather.4 = bf16[1024,256]{1,0:T(8,128)(2,1)} all-gather(bf16[128,256]{1,0:T(8,128)(2,1)S(1)} %broadcast_select_fusion), channel_id=6, replica_groups=mesh['y'=8,'x'=4,'zl'=2,'zh'=4,'c'=2] {'zh','c'}, dimensions={0}, use_global_device_ids=true | all-gather | bytes 589824 | tf_op jit(solution)/shard_map/all_gather | solution.py:290
  160.5 0.0 all-to-all-done.2.shares_hbm
  160.5 0.0 collective-permute-done.17.passed_hbm
  160.6 0.0 all-gather.10.cloned.1.call-done
  160.6 0.6 copy-done
  161.2 0.0 copy-done.2
  161.2 3.9 %shard_map.115 = (bf16[1,2,128,512]{3,2,1,0:T(8,128)(2,1)}, bf16[1,256,128]{2,1,0:T(8,128)(2,1)}, f32[4,128]{1,0:T(4,128)}) custom-call(s32[1]{0:T(128)} %bitcast.section, bf16[8,2,128,256]{3,2,1,0:T(8,128)(2,1)} %bitcast.23, bf16[8,128,256]{2,1,0:T(8,128)(2,1)} %bitcast.20, f32[1,2048]{1,0:T(1,128)} %bitcast.30, bf16[1,2,2048,256]{3,2,1,0:T(8,128)(2,1)} %wkv_hbm.3, ...), custom_call_target="tpu_custom_call" | custom-call | flops 536870912 | bytes 5000000 | tf_op jit(solution)/shard_map/pallas_call | solution.py:239
  (13 shorter events, 0.2 us)
Async XLA Ops:
  8.0 74.1 %all-gather.8.cloned.1.call-start = ((), (), s32[]{:S(2)}) async-start(), calls=%async_computation.5 | async-start | bytes 1179648 | tf_op jit(solution)/shard_map/all_gather | solution.py:290
  35.3 22.8 %all-to-all-start = ((bf16[8,128,256]{2,1,0:T(8,128)(2,1)}), bf16[8,128,256]{2,1,0:T(8,128)(2,1)S(1)}, u32[]{:S(2)}, u32[]{:S(2)}) async-start(bf16[8,128,256]{2,1,0:T(8,128)(2,1)} %get-tuple-element.15), calls=%async_computation | async-start | bytes 1048576 | tf_op jit(solution)/shard_map/all_to_all | solution.py:293
  40.5 23.5 %copy-start.1 = (bf16[2,128,256]{2,1,0:T(8,128)(2,1)S(1)}, bf16[2,128,256]{2,1,0:T(8,128)(2,1)}, u32[]{:S(2)}) copy-start(bf16[2,128,256]{2,1,0:T(8,128)(2,1)} %get-tuple-element.14) | copy-start | bytes 393220
  40.5 74.2 %reduce-scatter.2.cloned.1.call-start = ((), (), s32[]{:S(2)}) async-start(), calls=%async_computation.4 | async-start | bytes 1179648 | tf_op jit(solution)/shard_map/reduce_scatter | solution.py:315
  58.2 5.9 %collective-permute-start = (bf16[128,256]{1,0:T(8,128)(2,1)S(1)}, bf16[128,256]{1,0:T(8,128)(2,1)S(1)}, u32[]{:S(2)}, u32[]{:S(2)}) collective-permute-start(bf16[128,256]{1,0:T(8,128)(2,1)S(1)} %add_convert_fusion.1), channel_id=1, source_target_pairs={{0,8},{8,16},{16,24},{24,32},{32,40},{40,48},{48,56},{56,64},{64,7... | collective-permute-start | bytes 196616 | tf_op jit(solution)/shard_map/ppermute | solution.py:320
  85.4 23.7 %all-to-all-start.1 = ((bf16[8,128,256]{2,1,0:T(8,128)(2,1)}), bf16[8,128,256]{2,1,0:T(8,128)(2,1)S(1)}, u32[]{:S(2)}, u32[]{:S(2)}) async-start(bf16[8,128,256]{2,1,0:T(8,128)(2,1)} %shard_map.113), calls=%async_computation.1 | async-start | bytes 1048576 | tf_op jit(solution)/shard_map/all_to_all | solution.py:293
  89.5 71.0 %all-gather.10.cloned.1.call-start = ((), (), s32[]{:S(2)}) async-start(), calls=%async_computation.6 | async-start | bytes 1179648 | tf_op jit(solution)/shard_map/all_gather | solution.py:290
  89.5 2.7 %collective-permute-start.1 = (bf16[128,256]{1,0:T(8,128)(2,1)S(1)}, bf16[128,256]{1,0:T(8,128)(2,1)S(1)}, u32[]{:S(2)}, u32[]{:S(2)}) collective-permute-start(bf16[128,256]{1,0:T(8,128)(2,1)S(1)} %add_convert_fusion.1), channel_id=1, source_target_pairs={{248,504},{249,505},{250,506},{251,507},{252,508},{253,509},{254,5... | collective-permute-start | bytes 196616 | tf_op jit(solution)/shard_map/ppermute | solution.py:260
  90.2 2.0 %collective-permute-start.2 = (bf16[128,256]{1,0:T(8,128)(2,1)S(1)}, bf16[128,256]{1,0:T(8,128)(2,1)S(1)}, u32[]{:S(2)}, u32[]{:S(2)}) collective-permute-start(bf16[128,256]{1,0:T(8,128)(2,1)S(1)} %add_convert_fusion.1), channel_id=1, source_target_pairs={{248,440},{249,441},{250,442},{251,443},{252,444},{253,445},{254,4... | collective-permute-start | bytes 196616 | tf_op jit(solution)/shard_map/ppermute | solution.py:260
  90.9 1.4 collective-permute-start.3
  91.5 0.7 collective-permute-start.4
  92.3 2.0 %collective-permute-start.5 = (bf16[128,256]{1,0:T(8,128)(2,1)S(1)}, bf16[128,256]{1,0:T(8,128)(2,1)S(1)}, u32[]{:S(2)}, u32[]{:S(2)}) collective-permute-start(bf16[128,256]{1,0:T(8,128)(2,1)S(1)} %select_select_fusion.3), channel_id=1, source_target_pairs={{312,296},{376,360},{440,424},{504,488},{313,297},{377,361},{441,4... | collective-permute-start | bytes 196616 | tf_op jit(solution)/shard_map/ppermute | solution.py:266
  93.0 1.4 collective-permute-start.6
  93.6 0.7 collective-permute-start.7
  94.4 14.7 %collective-permute-start.8 = (bf16[128,256]{1,0:T(8,128)(2,1)S(1)}, bf16[128,256]{1,0:T(8,128)(2,1)S(1)}, u32[]{:S(2)}, u32[]{:S(2)}) collective-permute-start(bf16[128,256]{1,0:T(8,128)(2,1)S(1)} %select_select_fusion.2), channel_id=1, source_target_pairs={{264,256},{280,272},{296,288},{312,304},{328,320},{344,336},{360,3... | collective-permute-start | bytes 196616 | tf_op jit(solution)/shard_map/ppermute | solution.py:272
  109.9 2.7 %collective-permute-start.9 = (bf16[128,256]{1,0:T(8,128)(2,1)S(1)}, bf16[128,256]{1,0:T(8,128)(2,1)S(1)}, u32[]{:S(2)}, u32[]{:S(2)}) collective-permute-start(bf16[128,256]{1,0:T(8,128)(2,1)S(1)} %add_convert_fusion), channel_id=1, source_target_pairs={{248,504},{249,505},{250,506},{251,507},{252,508},{253,509},{254,5... | collective-permute-start | bytes 196616 | tf_op jit(solution)/shard_map/ppermute | solution.py:260
  110.6 2.0 %collective-permute-start.10 = (bf16[128,256]{1,0:T(8,128)(2,1)S(1)}, bf16[128,256]{1,0:T(8,128)(2,1)S(1)}, u32[]{:S(2)}, u32[]{:S(2)}) collective-permute-start(bf16[128,256]{1,0:T(8,128)(2,1)S(1)} %add_convert_fusion), channel_id=1, source_target_pairs={{248,440},{249,441},{250,442},{251,443},{252,444},{253,445},{254,4... | collective-permute-start | bytes 196616 | tf_op jit(solution)/shard_map/ppermute | solution.py:260
  111.3 1.4 collective-permute-start.11
  111.9 0.7 collective-permute-start.12
  112.7 2.0 %collective-permute-start.13 = (bf16[128,256]{1,0:T(8,128)(2,1)S(1)}, bf16[128,256]{1,0:T(8,128)(2,1)S(1)}, u32[]{:S(2)}, u32[]{:S(2)}) collective-permute-start(bf16[128,256]{1,0:T(8,128)(2,1)S(1)} %select_select_fusion.1), channel_id=1, source_target_pairs={{312,296},{376,360},{440,424},{504,488},{313,297},{377,361},{441,4... | collective-permute-start | bytes 196616 | tf_op jit(solution)/shard_map/ppermute | solution.py:266
  113.4 1.4 collective-permute-start.14
  114.0 0.7 collective-permute-start.15
  114.8 26.9 %collective-permute-start.16 = (bf16[128,256]{1,0:T(8,128)(2,1)S(1)}, bf16[128,256]{1,0:T(8,128)(2,1)S(1)}, u32[]{:S(2)}, u32[]{:S(2)}) collective-permute-start(bf16[128,256]{1,0:T(8,128)(2,1)S(1)} %select_select_fusion), channel_id=1, source_target_pairs={{264,256},{280,272},{296,288},{312,304},{328,320},{344,336},{360,3... | collective-permute-start | bytes 196616 | tf_op jit(solution)/shard_map/ppermute | solution.py:272
  116.1 44.5 %collective-permute-start.17 = (bf16[128,256]{1,0:T(8,128)(2,1)S(1)}, bf16[128,256]{1,0:T(8,128)(2,1)S(1)}, u32[]{:S(2)}, u32[]{:S(2)}) collective-permute-start(bf16[128,256]{1,0:T(8,128)(2,1)S(1)} %add_convert_fusion), channel_id=1, source_target_pairs={{0,8},{8,16},{16,24},{24,32},{32,40},{40,48},{48,56},{56,64},{64,7... | collective-permute-start | bytes 196616 | tf_op jit(solution)/shard_map/ppermute | solution.py:339
  127.3 33.2 %all-to-all-start.2 = ((f32[64,4,128]{2,1,0:T(4,128)}), f32[64,4,128]{2,1,0:T(4,128)S(1)}, u32[]{:S(2)}, u32[]{:S(2)}) async-start(f32[64,4,128]{2,1,0:T(4,128)} %bitcast.28), calls=%async_computation.3 | async-start | bytes 262144 | tf_op jit(solution)/shard_map/all_to_all | solution.py:337
  160.5 0.7 copy-start
  160.6 0.7 copy-start.2
Sparse Core Ops, SparseCore 0:
  11.0 40.4 all-gather.7
  109.9 36.4 all-gather.9
Sparse Core Ops, SparseCore 1:
  44.1 34.7 reduce-scatter.1

commit v13 on v12

--- a/solution.py
+++ b/solution.py
@@ -331,11 +331,12 @@
         8 + heads, flops,
     )
     current = jnp.where(place_here == half, fresh_rows[1], current)
-    parts, first_memory = lax.optimization_barrier((exchanged(parts), first_memory))
+    first_memory = jnp.stack([first_memory, entering])
+    parts, _ = lax.optimization_barrier((exchanged(parts), first_memory))
     output = summed(parts, current)
     second_memory, share = spread(output, half - 1, share)
     share = lax.all_to_all(share, PIPE[1:] + HEAD, 0, 0, tiled=True)
-    first_memory = whole(jnp.stack([first_memory, entering]))
+    first_memory = whole(first_memory)
     passed = lax.ppermute(output, PIPE, shift)
     share, second_memory = lax.optimization_barrier((share, whole(second_memory)))
     each = share.shape[1]

time: 173 us -> 180 us (1.040)
  the two profiles are of different devices: /device:TPU:39 before, /device:TPU:63 now
where the time goes in v13:
time: 180 us; the launch traced here: 179 us
  blocking collectives  59.4 us (33%)
  starting transfers between devices  57 us (32%)
  waiting for transfers between devices  30.3 us (17%)
  between operations  16 us (9%)
  Pallas kernels  14 us (8%)
    all_gather x3, blocking collectives, whole(): return lax.all_gather(block, HEAD, axis=0)  59.4 us
    ppermute x2, starting transfers between devices, body(): passed = lax.ppermute(output, PIPE, shift)  25.1 us
    ppermute x2, waiting for transfers between devices, spread(): return (jnp.where(zl == sz, held, lax.ppermute(held, PIPE, pairs)), beside)  15.8 us
    pallas_call x4, Pallas kernels, call(): pl.pallas_call(kernel, out_shape=[jax.ShapeDtypeStruct(shape, kind) for s...  14 us
    all_to_all x2, waiting for transfers between devices, exchanged(): return lax.all_to_all(parts, HEAD, 0, 0, tiled=True)  13.7 us
    all_to_all x1, starting transfers between devices, body(): share = lax.all_to_all(share, PIPE[1:] + HEAD, 0, 0, tiled=True)  10.8 us
    all_to_all x2, starting transfers between devices, exchanged(): return lax.all_to_all(parts, HEAD, 0, 0, tiled=True)  9.18 us
    ppermute x8, starting transfers between devices, spread(): sent = lax.ppermute(block, PIPE, [(source, place(to, sx, sz))])  5.32 us
  transfers between devices with their start and end apart: 24, of which 2 were waited for; matrix products, arithmetic and copies ran while one was open for 1% of the time, Pallas kernels for 6%

profile of v13, /device:TPU:63, one launch (start us, length us, event | category | flops | bytes accessed | tf_op | source)
XLA Modules:
  0.0 179.3 jit_solution(4143877132369196429)
XLA Ops:
  8.0 0.0 all-gather.10.cloned.1.call-start
  8.0 0.7 all-gather.10.cloned.1.call-update
  8.7 0.9 copy.13
  9.7 22.2 %all-gather = bf16[1024,256]{1,0:T(8,128)(2,1)} all-gather(bf16[128,256]{1,0:T(8,128)(2,1)S(1)} %bitcast.26), channel_id=2, replica_groups=mesh['y'=8,'x'=4,'zl'=2,'zh'=4,'c'=2] {'zh','c'}, dimensions={0}, use_global_device_ids=true | all-gather | bytes 589824 | tf_op jit(solution)/shard_map/all_gather | solution.py:290
  31.9 3.4 %shard_map.112 = (bf16[8,128,256]{2,1,0:T(8,128)(2,1)}, bf16[2,128,256]{2,1,0:T(8,128)(2,1)}) custom-call(s32[1]{0:T(128)} %bitcast.section, bf16[8,128,256]{2,1,0:T(8,128)(2,1)} %bitcast.23, bf16[2,256,128]{2,1,0:T(8,128)(2,1)} %fresh.1, f32[1,2048]{1,0:T(1,128)} %gain.3, bf16[1,2048,256]{2,1,0:T(8,128)(2,1)} %wq.3, bf16[1,2,2048,256]{3,2,1,0:T(8,128)(2,1)} %wkv_hbm.3, ...), custom_call_target="tpu_custom_call" | custom-call | flops 536870912 | bytes 5000000 | tf_op jit(solution)/shard_map/pallas_call | solution.py:239
  35.3 5.3 %all-to-all-start = ((bf16[8,128,256]{2,1,0:T(8,128)(2,1)}), bf16[8,128,256]{2,1,0:T(8,128)(2,1)S(1)}, u32[]{:S(2)}, u32[]{:S(2)}) async-start(bf16[8,128,256]{2,1,0:T(8,128)(2,1)} %get-tuple-element.13), calls=%async_computation | async-start | bytes 1048576 | tf_op jit(solution)/shard_map/all_to_all | solution.py:293
  40.5 0.0 reduce-scatter.2.cloned.1.call-start
  40.6 3.4 %shard_map.114 = f32[2048,128]{1,0:T(8,128)} custom-call(s32[1]{0:T(128)} %bitcast.section, bf16[1,128,512]{2,1,0:T(8,128)(2,1)} %grads_hbm.1, bf16[1,2,2048,256]{3,2,1,0:T(8,128)(2,1)} %wkv_hbm.3), custom_call_target="tpu_custom_call" | custom-call | flops 536870912 | bytes 5000000 | tf_op jit(solution)/shard_map/pallas_call | solution.py:239
  44.0 0.0 reduce-scatter.2.cloned.1.call-update
  44.0 13.7 %all-to-all-done = bf16[8,128,256]{2,1,0:T(8,128)(2,1)S(1)} async-done(((bf16[8,128,256]{2,1,0:T(8,128)(2,1)}), bf16[8,128,256]{2,1,0:T(8,128)(2,1)S(1)}, u32[]{:S(2)}, u32[]{:S(2)}) %all-to-all-start) | async-done | bytes 524320 | tf_op jit(solution)/shard_map/all_to_all | solution.py:293
  57.7 0.1 convert_reduce_fusion.1
  57.8 0.7 collective-permute-start
  58.4 0.7 collective-permute-start.1
  59.1 0.7 collective-permute-start.2
  59.8 0.7 collective-permute-start.3
  60.5 4.1 %collective-permute-start.8 = (bf16[128,256]{1,0:T(8,128)(2,1)S(1)}, bf16[128,256]{1,0:T(8,128)(2,1)S(1)}, u32[]{:S(2)}, u32[]{:S(2)}) collective-permute-start(bf16[128,256]{1,0:T(8,128)(2,1)S(1)} %add_convert_fusion.1), channel_id=1, source_target_pairs={{0,8},{8,16},{16,24},{24,32},{32,40},{40,48},{48,56},{56,64},{64,7... | collective-permute-start | bytes 196616 | tf_op jit(solution)/shard_map/ppermute | solution.py:320
  64.5 0.0 collective-permute-done
  64.5 0.0 collective-permute-done.1
  64.6 0.0 collective-permute-done.2
  64.6 0.0 collective-permute-done.3
  64.6 0.7 collective-permute-start.4
  65.3 0.7 collective-permute-start.5
  66.0 0.7 collective-permute-start.6
  66.6 0.0 collective-permute-done.8
  66.6 0.0 copy-done.1
  66.7 18.3 %all-gather.2 = bf16[1024,256]{1,0:T(8,128)(2,1)} all-gather(bf16[128,256]{1,0:T(8,128)(2,1)S(1)} %bitcast_select_fusion), channel_id=4, replica_groups=mesh['y'=8,'x'=4,'zl'=2,'zh'=4,'c'=2] {'zh','c'}, dimensions={0}, use_global_device_ids=true | all-gather | bytes 589824 | tf_op jit(solution)/shard_map/all_gather | solution.py:290
  85.0 3.3 %shard_map.113 = bf16[8,128,256]{2,1,0:T(8,128)(2,1)} custom-call(s32[1]{0:T(128)} %bitcast.section, bf16[8,128,256]{2,1,0:T(8,128)(2,1)} %bitcast.22, bf16[8,2,256,128]{3,2,1,0:T(8,128)(2,1)} %bitcast.24, f32[1,2048]{1,0:T(1,128)} %gain.3, f32[1,2048]{1,0:T(1,128)} %bitcast.29, bf16[1,2048,256]{2,1,0:T(8,128)(2,1)} %wq.3, ...), custom_call_target="tpu_custom_call" | custom-call | flops 536870912 | bytes 5000000 | tf_op jit(solution)/shard_map/pallas_call | solution.py:239
  88.3 3.9 %all-to-all-start.1 = ((bf16[8,128,256]{2,1,0:T(8,128)(2,1)}), bf16[8,128,256]{2,1,0:T(8,128)(2,1)S(1)}, u32[]{:S(2)}, u32[]{:S(2)}) async-start(bf16[8,128,256]{2,1,0:T(8,128)(2,1)} %shard_map.113), calls=%async_computation.1 | async-start | bytes 1048576 | tf_op jit(solution)/shard_map/all_to_all | solution.py:293
  92.2 0.0 all-gather.8.cloned.1.call-start
  92.2 0.0 collective-permute-done.4
  92.3 0.0 collective-permute-done.5
  92.3 0.0 collective-permute-done.6
  92.3 1.3 collective-permute-start.7
  93.6 15.8 %collective-permute-done.7 = bf16[128,256]{1,0:T(8,128)(2,1)S(1)} collective-permute-done((bf16[128,256]{1,0:T(8,128)(2,1)S(1)}, bf16[128,256]{1,0:T(8,128)(2,1)S(1)}, u32[]{:S(2)}, u32[]{:S(2)}) %collective-permute-start.7) | collective-permute-done | bytes 65568 | tf_op jit(solution)/shard_map/ppermute | solution.py:272
  109.4 0.7 pad_maximum_fusion
  110.1 0.0 all-gather.8.cloned.1.call-update
  110.1 0.0 all-to-all-done.1
  110.2 0.1 convert_reduce_fusion
  110.3 0.7 collective-permute-start.10
  110.9 0.7 collective-permute-start.11
  111.6 0.7 collective-permute-start.12
  112.3 0.7 collective-permute-start.9
  113.0 0.0 collective-permute-done.10
  113.0 0.0 collective-permute-done.11
  113.0 0.0 collective-permute-done.12
  113.0 0.0 collective-permute-done.9
  113.0 0.7 collective-permute-start.13
  113.7 0.7 collective-permute-start.14
  114.4 0.7 collective-permute-start.15
  115.0 0.0 collective-permute-done.13
  115.1 0.0 collective-permute-done.14
  115.1 0.0 collective-permute-done.15
  115.1 0.0 reduce-scatter.2.cloned.1.call-done
  115.1 1.3 collective-permute-start.16
  116.4 21.0 %collective-permute-start.17 = (bf16[128,256]{1,0:T(8,128)(2,1)S(1)}, bf16[128,256]{1,0:T(8,128)(2,1)S(1)}, u32[]{:S(2)}, u32[]{:S(2)}) collective-permute-start(bf16[128,256]{1,0:T(8,128)(2,1)S(1)} %add_convert_fusion), channel_id=1, source_target_pairs={{0,8},{8,16},{16,24},{24,32},{32,40},{40,48},{48,56},{56,64},{64,7... | collective-permute-start | bytes 196616 | tf_op jit(solution)/shard_map/ppermute | solution.py:340
  137.5 10.8 %all-to-all-start.2 = ((f32[64,4,128]{2,1,0:T(4,128)}), f32[64,4,128]{2,1,0:T(4,128)S(1)}, u32[]{:S(2)}, u32[]{:S(2)}) async-start(f32[64,4,128]{2,1,0:T(4,128)} %bitcast.28), calls=%async_computation.3 | async-start | bytes 262144 | tf_op jit(solution)/shard_map/all_to_all | solution.py:338
  148.3 0.0 collective-permute-done.16
  148.3 18.9 %all-gather.4 = bf16[1024,256]{1,0:T(8,128)(2,1)} all-gather(bf16[128,256]{1,0:T(8,128)(2,1)S(1)} %broadcast_select_fusion), channel_id=6, replica_groups=mesh['y'=8,'x'=4,'zl'=2,'zh'=4,'c'=2] {'zh','c'}, dimensions={0}, use_global_device_ids=true | all-gather | bytes 589824 | tf_op jit(solution)/shard_map/all_gather | solution.py:290
  167.3 0.0 all-to-all-done.2.shares_hbm
  167.3 0.0 collective-permute-done.17.passed_hbm
  167.3 0.0 all-gather.8.cloned.1.call-done
  167.3 0.6 copy-done
  167.9 0.0 copy-done.2
  168.0 3.9 %shard_map.115 = (bf16[1,2,128,512]{3,2,1,0:T(8,128)(2,1)}, bf16[1,256,128]{2,1,0:T(8,128)(2,1)}, f32[4,128]{1,0:T(4,128)}) custom-call(s32[1]{0:T(128)} %bitcast.section, bf16[8,2,128,256]{3,2,1,0:T(8,128)(2,1)} %bitcast.25, bf16[8,128,256]{2,1,0:T(8,128)(2,1)} %bitcast.21, f32[1,2048]{1,0:T(1,128)} %bitcast.30, bf16[1,2,2048,256]{3,2,1,0:T(8,128)(2,1)} %wkv_hbm.3, ...), custom_call_target="tpu_custom_call" | custom-call | flops 536870912 | bytes 5000000 | tf_op jit(solution)/shard_map/pallas_call | solution.py:239
  (13 shorter events, 0.2 us)
Async XLA Ops:
  8.0 77.0 %all-gather.10.cloned.1.call-start = ((), (), s32[]{:S(2)}) async-start(), calls=%async_computation.6 | async-start | bytes 1179648 | tf_op jit(solution)/shard_map/all_gather | solution.py:290
  35.3 22.4 %all-to-all-start = ((bf16[8,128,256]{2,1,0:T(8,128)(2,1)}), bf16[8,128,256]{2,1,0:T(8,128)(2,1)S(1)}, u32[]{:S(2)}, u32[]{:S(2)}) async-start(bf16[8,128,256]{2,1,0:T(8,128)(2,1)} %get-tuple-element.13), calls=%async_computation | async-start | bytes 1048576 | tf_op jit(solution)/shard_map/all_to_all | solution.py:293
  40.5 26.1 %copy-start.1 = (bf16[2,128,256]{2,1,0:T(8,128)(2,1)S(1)}, bf16[2,128,256]{2,1,0:T(8,128)(2,1)}, u32[]{:S(2)}) copy-start(bf16[2,128,256]{2,1,0:T(8,128)(2,1)} %get-tuple-element.14) | copy-start | bytes 393220
  40.5 74.6 %reduce-scatter.2.cloned.1.call-start = ((), (), s32[]{:S(2)}) async-start(), calls=%async_computation.4 | async-start | bytes 1179648 | tf_op jit(solution)/shard_map/reduce_scatter | solution.py:315
  57.8 6.8 %collective-permute-start = (bf16[128,256]{1,0:T(8,128)(2,1)S(1)}, bf16[128,256]{1,0:T(8,128)(2,1)S(1)}, u32[]{:S(2)}, u32[]{:S(2)}) collective-permute-start(bf16[128,256]{1,0:T(8,128)(2,1)S(1)} %add_convert_fusion.1), channel_id=1, source_target_pairs={{248,504},{249,505},{250,506},{251,507},{252,508},{253,509},{254,5... | collective-permute-start | bytes 196616 | tf_op jit(solution)/shard_map/ppermute | solution.py:260
  58.4 6.1 %collective-permute-start.1 = (bf16[128,256]{1,0:T(8,128)(2,1)S(1)}, bf16[128,256]{1,0:T(8,128)(2,1)S(1)}, u32[]{:S(2)}, u32[]{:S(2)}) collective-permute-start(bf16[128,256]{1,0:T(8,128)(2,1)S(1)} %add_convert_fusion.1), channel_id=1, source_target_pairs={{248,440},{249,441},{250,442},{251,443},{252,444},{253,445},{254,4... | collective-permute-start | bytes 196616 | tf_op jit(solution)/shard_map/ppermute | solution.py:260
  59.1 5.5 %collective-permute-start.2 = (bf16[128,256]{1,0:T(8,128)(2,1)S(1)}, bf16[128,256]{1,0:T(8,128)(2,1)S(1)}, u32[]{:S(2)}, u32[]{:S(2)}) collective-permute-start(bf16[128,256]{1,0:T(8,128)(2,1)S(1)} %add_convert_fusion.1), channel_id=1, source_target_pairs={{248,376},{249,377},{250,378},{251,379},{252,380},{253,381},{254,3... | collective-permute-start | bytes 196616 | tf_op jit(solution)/shard_map/ppermute | solution.py:260
  59.8 4.8 %collective-permute-start.3 = (bf16[128,256]{1,0:T(8,128)(2,1)S(1)}, bf16[128,256]{1,0:T(8,128)(2,1)S(1)}, u32[]{:S(2)}, u32[]{:S(2)}) collective-permute-start(bf16[128,256]{1,0:T(8,128)(2,1)S(1)} %add_convert_fusion.1), channel_id=1, source_target_pairs={{248,312},{249,313},{250,314},{251,315},{252,316},{253,317},{254,3... | collective-permute-start | bytes 196616 | tf_op jit(solution)/shard_map/ppermute | solution.py:260
  60.5 6.2 %collective-permute-start.8 = (bf16[128,256]{1,0:T(8,128)(2,1)S(1)}, bf16[128,256]{1,0:T(8,128)(2,1)S(1)}, u32[]{:S(2)}, u32[]{:S(2)}) collective-permute-start(bf16[128,256]{1,0:T(8,128)(2,1)S(1)} %add_convert_fusion.1), channel_id=1, source_target_pairs={{0,8},{8,16},{16,24},{24,32},{32,40},{40,48},{48,56},{56,64},{64,7... | collective-permute-start | bytes 196616 | tf_op jit(solution)/shard_map/ppermute | solution.py:320
  64.6 27.6 %collective-permute-start.4 = (bf16[128,256]{1,0:T(8,128)(2,1)S(1)}, bf16[128,256]{1,0:T(8,128)(2,1)S(1)}, u32[]{:S(2)}, u32[]{:S(2)}) collective-permute-start(bf16[128,256]{1,0:T(8,128)(2,1)S(1)} %select_select_fusion.3), channel_id=1, source_target_pairs={{312,296},{376,360},{440,424},{504,488},{313,297},{377,361},{441,4... | collective-permute-start | bytes 196616 | tf_op jit(solution)/shard_map/ppermute | solution.py:266
  65.3 27.0 %collective-permute-start.5 = (bf16[128,256]{1,0:T(8,128)(2,1)S(1)}, bf16[128,256]{1,0:T(8,128)(2,1)S(1)}, u32[]{:S(2)}, u32[]{:S(2)}) collective-permute-start(bf16[128,256]{1,0:T(8,128)(2,1)S(1)} %select_select_fusion.3), channel_id=1, source_target_pairs={{312,280},{376,344},{440,408},{504,472},{313,281},{377,345},{441,4... | collective-permute-start | bytes 196616 | tf_op jit(solution)/shard_map/ppermute | solution.py:266
  66.0 26.3 %collective-permute-start.6 = (bf16[128,256]{1,0:T(8,128)(2,1)S(1)}, bf16[128,256]{1,0:T(8,128)(2,1)S(1)}, u32[]{:S(2)}, u32[]{:S(2)}) collective-permute-start(bf16[128,256]{1,0:T(8,128)(2,1)S(1)} %select_select_fusion.3), channel_id=1, source_target_pairs={{312,264},{376,328},{440,392},{504,456},{313,265},{377,329},{441,3... | collective-permute-start | bytes 196616 | tf_op jit(solution)/shard_map/ppermute | solution.py:266
  88.3 21.8 %all-to-all-start.1 = ((bf16[8,128,256]{2,1,0:T(8,128)(2,1)}), bf16[8,128,256]{2,1,0:T(8,128)(2,1)S(1)}, u32[]{:S(2)}, u32[]{:S(2)}) async-start(bf16[8,128,256]{2,1,0:T(8,128)(2,1)} %shard_map.113), calls=%async_computation.1 | async-start | bytes 1048576 | tf_op jit(solution)/shard_map/all_to_all | solution.py:293
  92.2 75.1 %all-gather.8.cloned.1.call-start = ((), (), s32[]{:S(2)}) async-start(), calls=%async_computation.5 | async-start | bytes 1179648 | tf_op jit(solution)/shard_map/all_gather | solution.py:290
  92.3 17.1 %collective-permute-start.7 = (bf16[128,256]{1,0:T(8,128)(2,1)S(1)}, bf16[128,256]{1,0:T(8,128)(2,1)S(1)}, u32[]{:S(2)}, u32[]{:S(2)}) collective-permute-start(bf16[128,256]{1,0:T(8,128)(2,1)S(1)} %select_select_fusion.2), channel_id=1, source_target_pairs={{264,256},{280,272},{296,288},{312,304},{328,320},{344,336},{360,3... | collective-permute-start | bytes 196616 | tf_op jit(solution)/shard_map/ppermute | solution.py:272
  110.3 2.7 %collective-permute-start.10 = (bf16[128,256]{1,0:T(8,128)(2,1)S(1)}, bf16[128,256]{1,0:T(8,128)(2,1)S(1)}, u32[]{:S(2)}, u32[]{:S(2)}) collective-permute-start(bf16[128,256]{1,0:T(8,128)(2,1)S(1)} %add_convert_fusion), channel_id=1, source_target_pairs={{248,440},{249,441},{250,442},{251,443},{252,444},{253,445},{254,4... | collective-permute-start | bytes 196616 | tf_op jit(solution)/shard_map/ppermute | solution.py:260
  110.9 2.0 %collective-permute-start.11 = (bf16[128,256]{1,0:T(8,128)(2,1)S(1)}, bf16[128,256]{1,0:T(8,128)(2,1)S(1)}, u32[]{:S(2)}, u32[]{:S(2)}) collective-permute-start(bf16[128,256]{1,0:T(8,128)(2,1)S(1)} %add_convert_fusion), channel_id=1, source_target_pairs={{248,376},{249,377},{250,378},{251,379},{252,380},{253,381},{254,3... | collective-permute-start | bytes 196616 | tf_op jit(solution)/shard_map/ppermute | solution.py:260
  111.6 1.4 collective-permute-start.12
  112.3 0.7 collective-permute-start.9
  113.0 2.0 %collective-permute-start.13 = (bf16[128,256]{1,0:T(8,128)(2,1)S(1)}, bf16[128,256]{1,0:T(8,128)(2,1)S(1)}, u32[]{:S(2)}, u32[]{:S(2)}) collective-permute-start(bf16[128,256]{1,0:T(8,128)(2,1)S(1)} %select_select_fusion.1), channel_id=1, source_target_pairs={{312,296},{376,360},{440,424},{504,488},{313,297},{377,361},{441,4... | collective-permute-start | bytes 196616 | tf_op jit(solution)/shard_map/ppermute | solution.py:266
  113.7 1.4 collective-permute-start.14
  114.4 0.7 collective-permute-start.15
  115.1 33.2 %collective-permute-start.16 = (bf16[128,256]{1,0:T(8,128)(2,1)S(1)}, bf16[128,256]{1,0:T(8,128)(2,1)S(1)}, u32[]{:S(2)}, u32[]{:S(2)}) collective-permute-start(bf16[128,256]{1,0:T(8,128)(2,1)S(1)} %select_select_fusion), channel_id=1, source_target_pairs={{264,256},{280,272},{296,288},{312,304},{328,320},{344,336},{360,3... | collective-permute-start | bytes 196616 | tf_op jit(solution)/shard_map/ppermute | solution.py:272
  116.4 50.8 %collective-permute-start.17 = (bf16[128,256]{1,0:T(8,128)(2,1)S(1)}, bf16[128,256]{1,0:T(8,128)(2,1)S(1)}, u32[]{:S(2)}, u32[]{:S(2)}) collective-permute-start(bf16[128,256]{1,0:T(8,128)(2,1)S(1)} %add_convert_fusion), channel_id=1, source_target_pairs={{0,8},{8,16},{16,24},{24,32},{32,40},{40,48},{48,56},{56,64},{64,7... | collective-permute-start | bytes 196616 | tf_op jit(solution)/shard_map/ppermute | solution.py:340
  137.5 29.8 %all-to-all-start.2 = ((f32[64,4,128]{2,1,0:T(4,128)}), f32[64,4,128]{2,1,0:T(4,128)S(1)}, u32[]{:S(2)}, u32[]{:S(2)}) async-start(f32[64,4,128]{2,1,0:T(4,128)} %bitcast.28), calls=%async_computation.3 | async-start | bytes 262144 | tf_op jit(solution)/shard_map/all_to_all | solution.py:338
  167.3 0.7 copy-start
  167.3 0.7 copy-start.2
Sparse Core Ops, SparseCore 0:
  11.0 42.3 all-gather.9
  110.3 37.8 all-gather.7
Sparse Core Ops, SparseCore 1:
  44.1 35.3 reduce-scatter.1
